TPU v7x, 32 devices: a whole 2x2x4 slice. The times are simulated.
32 devices in a mesh: dp: 2 (over core), expert: 16 (over z, y, x).
Axes of the slice: x: 2, y: 2, z: 4, core: 2. Of those that a mesh axis runs over, the one named last changes fastest.
Arguments:
- hidden_in: bfloat16 [6144, 2048], P(('dp', 'expert')), may hold values from -6 to 6
- cotangent: bfloat16 [6144, 2048], P(('dp', 'expert')), may hold values from -6 to 6
- doc_ids: int32 [32, 192], P(('dp', 'expert')), may hold values from 0 to 3, never falling along the last dimension, each value on 1 to 96 neighbouring positions
- routes: int32 [6144, 8], P(('dp', 'expert')), may hold values from 0 to 15, all different within a row; in each aligned block of 192 rows (0 to 191, 192 to 383, ...) at most 128 rows name the same one
- attn_gain: float32 [2048], replicated, may hold values from 0.5 to 1.5
- w_query: bfloat16 [2048, 2048], P(('dp', 'expert')), may hold values from -0.125 to 0.125
- w_key: bfloat16 [2048, 2048], P(('dp', 'expert')), may hold values from -0.125 to 0.125
- w_value: bfloat16 [2048, 2048], P(('dp', 'expert')), may hold values from -0.125 to 0.125
- query_gain: float32 [2048], replicated, may hold values from 0.5 to 1.5
- key_gain: float32 [2048], replicated, may hold values from 0.5 to 1.5
- w_output: bfloat16 [2048, 2048], P(('dp', 'expert')), may hold values from -0.375 to 0.375
- moe_gain: float32 [2048], replicated, may hold values from 0.5 to 1.5
- w_router: bfloat16 [2048, 16], P(('dp', 'expert')), may hold values from -0.0625 to 0.0625
- w_gate: bfloat16 [16, 2048, 1024], P('expert'), may hold values from -0.125 to 0.125
- w_up: bfloat16 [16, 2048, 1024], P('expert'), may hold values from -0.125 to 0.125
- w_down: bfloat16 [16, 1024, 2048], P('expert'), may hold values from -4 to 4
Outputs:
- block_out: bfloat16 [6144, 2048], P(('dp', 'expert'))
- input_grad: bfloat16 [6144, 2048], P(('dp', 'expert'))
- grad_attn_gain: float32 [2048], P(('dp', 'expert'))
- grad_query: float32 [2048, 2048], P(('dp', 'expert'))
- grad_key: float32 [2048, 2048], P(('dp', 'expert'))
- grad_value: float32 [2048, 2048], P(('dp', 'expert'))
- grad_query_gain: float32 [2048], P(('dp', 'expert'))
- grad_key_gain: float32 [2048], P(('dp', 'expert'))
- grad_output: float32 [2048, 2048], P(('dp', 'expert'))
- grad_moe_gain: float32 [2048], P(('dp', 'expert'))
- grad_router: float32 [2048, 16], P(('dp', 'expert'))
- grad_gate: float32 [16, 2048, 1024], P('expert', None, 'dp')
- grad_up: float32 [16, 2048, 1024], P('expert', None, 'dp')
- grad_down: float32 [16, 1024, 2048], P('expert', 'dp')
Inputs may be any that keep to these rules, and one draw needn't show every extreme that they name: `routes`: each row names 8 different experts. Among the rows of one device no expert is named more than 128 times, and in some device's rows one expert is named exactly 128 times. `doc_ids`: along each row of 192 positions the numbers never fall; a document has at most 96 positions, and one has exactly that many.
All inputs are finite; a program needn't handle non-finite values.
Results may differ from a plain program's by a relative error of at most 0.019.
Values may be sent and summed in bfloat16 or wider, within the bound.
No kernel may reach another device: no remote copies, remote signals or barrier semaphores. Data moves between devices by JAX's collectives and lax.ppermute only.
A program may use at most 256 MiB of HBM per device.

v0:
```python
import jax
import jax.numpy as jnp
from jax import lax
from jax.sharding import PartitionSpec as P

HD = 128


EPSILON = 1e-05


def norm_forward(values, gain_vector):
    inverse = lax.rsqrt(jnp.mean(values * values, axis=-1, keepdims=True) + EPSILON)
    return (values * inverse * gain_vector, inverse)


def norm_backward(values, inverse, gain_vector, upstream):
    gain_grad = jnp.sum(upstream * values * inverse, axis=0)
    scaled = upstream * gain_vector
    inner_mean = jnp.mean(scaled * values, axis=-1, keepdims=True)
    return (inverse * (scaled - values * inner_mean * inverse * inverse), gain_grad)


def rotary_tables(length, head_dim):
    half_dim = head_dim // 2
    frequency = 10000.0 ** (-jnp.arange(half_dim, dtype=jnp.float32) * 2.0 / head_dim)
    angles = jnp.arange(length, dtype=jnp.float32)[:, None] * frequency[None, :]
    angles = jnp.concatenate([angles, angles], axis=1)
    return (jnp.cos(angles)[:, None, :], jnp.sin(angles)[:, None, :])


def rotate(values, cosine, sine_table):
    half_dim = values.shape[-1] // 2
    turned = jnp.concatenate([-values[..., half_dim:], values[..., :half_dim]], axis=-1)
    return values * cosine + turned * sine_table


def rotate_back(upstream, cosine, sine_table):
    half_dim = upstream.shape[-1] // 2
    with_sine = upstream * sine_table
    turned = jnp.concatenate([with_sine[..., half_dim:], -with_sine[..., :half_dim]], axis=-1)
    return upstream * cosine + turned


def times_transposed(left, right):
    return jnp.einsum("ta,ba->tb", left, right, preferred_element_type=jnp.float32)


def inner_product(left, right):
    return jnp.einsum("ta,tb->ab", left, right, preferred_element_type=jnp.float32)


def body(
    hidden_in,
    cotangent,
    doc_ids,
    routes,
    attn_gain,
    w_query,
    w_key,
    w_value,
    query_gain,
    key_gain,
    w_output,
    moe_gain,
    w_router,
    w_gate,
    w_up,
    w_down,
):
    f32 = jnp.float32
    bf16 = jnp.bfloat16
    tokens_here = hidden_in.shape[0]
    model_width = hidden_in.shape[1]
    head_dim = HD
    head_count = model_width // head_dim
    top_count = routes.shape[1]
    experts_all = w_router.shape[1]
    capacity = tokens_here * top_count * 4 // (3 * experts_all)
    local_experts = w_gate.shape[0]
    owners = lax.axis_size("expert")
    full_query, full_key, full_value, full_output, full_router = (
        lax.all_gather(w_query, ("dp", "expert"), axis=0, tiled=True),
        lax.all_gather(w_key, ("dp", "expert"), axis=0, tiled=True),
        lax.all_gather(w_value, ("dp", "expert"), axis=0, tiled=True),
        lax.all_gather(w_output, ("dp", "expert"), axis=0, tiled=True),
        lax.all_gather(w_router, ("dp", "expert"), axis=0, tiled=True),
    )
    inputs_f32 = hidden_in.astype(f32)
    normed_attn, inverse_attn = norm_forward(inputs_f32, attn_gain)
    act_attn = normed_attn.astype(bf16)
    query_pre = jnp.dot(act_attn, full_query, preferred_element_type=f32)
    key_pre = jnp.dot(act_attn, full_key, preferred_element_type=f32)
    value_low = jnp.dot(act_attn, full_value, preferred_element_type=f32).astype(bf16)
    query_normed, query_inverse = norm_forward(query_pre, query_gain)
    key_normed, key_inverse = norm_forward(key_pre, key_gain)
    cosine, sine_table = rotary_tables(tokens_here, head_dim)
    head_shape = (tokens_here, head_count, head_dim)
    query_rot = rotate(query_normed.reshape(head_shape), cosine, sine_table).astype(bf16)
    key_rot = rotate(key_normed.reshape(head_shape), cosine, sine_table).astype(bf16)
    value_heads = value_low.reshape(head_shape)
    score_scale = head_dim ** (-0.5)
    position = jnp.arange(tokens_here, dtype=jnp.int32)
    allowed = (position[:, None] >= position[None, :]) & (
        doc_ids[0][:, None] == doc_ids[0][None, :]
    )

    def masked_scores():
        scores = (
            jnp.einsum("qhd,khd->hqk", query_rot, key_rot, preferred_element_type=f32) * score_scale
        )
        return jnp.where(allowed[None], scores, -1e30)

    scores = masked_scores()
    row_max = jnp.max(scores, axis=-1, keepdims=True)
    row_sum = jnp.sum(jnp.exp(scores - row_max), axis=-1, keepdims=True)
    log_total = row_max + jnp.log(row_sum)
    probs_low = jnp.exp(scores - log_total).astype(bf16)
    attended = jnp.einsum("hqk,khd->qhd", probs_low, value_heads, preferred_element_type=f32)
    attended_low = attended.reshape(tokens_here, model_width).astype(bf16)
    middle = inputs_f32 + jnp.dot(attended_low, full_output, preferred_element_type=f32)
    normed_moe, inverse_moe = norm_forward(middle, moe_gain)
    act_moe = normed_moe.astype(bf16)
    logits = jnp.dot(act_moe, full_router, preferred_element_type=f32)
    router_probs = jax.nn.softmax(logits, axis=-1)
    expert_ids = jnp.arange(experts_all, dtype=jnp.int32)
    chosen = routes[:, :, None] == expert_ids[None, None, :]
    gate_values = jnp.sum(jnp.where(chosen, router_probs[:, None, :], 0.0), axis=-1)
    flat_routes = routes.reshape(-1)
    onehot = (flat_routes[:, None] == expert_ids[None, :]).astype(jnp.int32)
    slot_of = jnp.sum((jnp.cumsum(onehot, axis=0) - 1) * onehot, axis=1)
    target_slot = flat_routes * capacity + slot_of
    pair_token = jnp.arange(tokens_here * top_count, dtype=jnp.int32) // top_count

    def to_experts(pair_rows):
        buffer = (
            jnp.zeros((experts_all * capacity, model_width), bf16).at[target_slot].set(pair_rows)
        )
        return buffer.reshape(experts_all, capacity, model_width)

    def from_experts(buffer):
        return buffer.reshape(experts_all * capacity, model_width)[target_slot]

    received = lax.all_to_all(
        to_experts(act_moe[pair_token]), "expert", split_axis=0, concat_axis=0, tiled=True
    )
    owner_rows = received.reshape(owners, local_experts, capacity, model_width)
    gate_pre = jnp.einsum("secd,edf->secf", owner_rows, w_gate, preferred_element_type=f32)
    up_pre = jnp.einsum("secd,edf->secf", owner_rows, w_up, preferred_element_type=f32)
    sigmoid = jax.nn.sigmoid(gate_pre)
    swish = gate_pre * sigmoid
    hidden_low = (swish * up_pre).astype(bf16)
    expert_out = jnp.einsum(
        "secf,efd->secd", hidden_low, w_down, preferred_element_type=f32
    ).astype(bf16)
    returned = lax.all_to_all(
        expert_out.reshape(owners * local_experts, capacity, model_width),
        "expert",
        split_axis=0,
        concat_axis=0,
        tiled=True,
    )
    pair_out = from_experts(returned).reshape(tokens_here, top_count, model_width).astype(f32)
    moe_term = jnp.sum(gate_values[:, :, None] * pair_out, axis=1)
    block_out = (middle + moe_term).astype(bf16)
    upstream = cotangent.astype(f32)
    pair_grad = (gate_values[:, :, None] * upstream[:, None, :]).astype(bf16)
    gate_grad = jnp.sum(upstream[:, None, :] * pair_out, axis=-1)
    out_grad = lax.all_to_all(
        to_experts(pair_grad.reshape(-1, model_width)),
        "expert",
        split_axis=0,
        concat_axis=0,
        tiled=True,
    )
    out_grad = out_grad.reshape(owners, local_experts, capacity, model_width)
    hidden_grad = jnp.einsum("secd,efd->secf", out_grad, w_down, preferred_element_type=f32)
    down_grad = jnp.einsum("secf,secd->efd", hidden_low, out_grad, preferred_element_type=f32)
    slope = sigmoid * (1.0 + gate_pre * (1.0 - sigmoid))
    gate_pre_grad = (hidden_grad * up_pre * slope).astype(bf16)
    up_pre_grad = (hidden_grad * swish).astype(bf16)
    row_grad = jnp.einsum("secf,edf->secd", gate_pre_grad, w_gate, preferred_element_type=f32)
    row_grad = (
        row_grad + jnp.einsum("secf,edf->secd", up_pre_grad, w_up, preferred_element_type=f32)
    ).astype(bf16)
    gate_weight_grad = jnp.einsum(
        "secd,secf->edf", owner_rows, gate_pre_grad, preferred_element_type=f32
    )
    up_weight_grad = jnp.einsum(
        "secd,secf->edf", owner_rows, up_pre_grad, preferred_element_type=f32
    )
    gate_weight_grad, up_weight_grad, down_grad = (
        lax.psum_scatter(
            gate_weight_grad.astype(jnp.bfloat16), "dp", scatter_dimension=2, tiled=True
        ).astype(jnp.float32),
        lax.psum_scatter(
            up_weight_grad.astype(jnp.bfloat16), "dp", scatter_dimension=2, tiled=True
        ).astype(jnp.float32),
        lax.psum_scatter(
            down_grad.astype(jnp.bfloat16), "dp", scatter_dimension=1, tiled=True
        ).astype(jnp.float32),
    )
    back_rows = lax.all_to_all(
        row_grad.reshape(owners * local_experts, capacity, model_width),
        "expert",
        split_axis=0,
        concat_axis=0,
        tiled=True,
    )
    moe_in_grad = jnp.sum(
        from_experts(back_rows).reshape(tokens_here, top_count, model_width).astype(f32), axis=1
    )
    choice_grad = jnp.sum(jnp.where(chosen, gate_grad[:, :, None], 0.0), axis=1)
    logit_grad = router_probs * (
        choice_grad - jnp.sum(router_probs * choice_grad, axis=-1, keepdims=True)
    )
    logit_low = logit_grad.astype(bf16)
    moe_in_grad = moe_in_grad + times_transposed(logit_low, full_router)
    router_grad = inner_product(act_moe, logit_low)
    mid_norm_grad, moe_gain_grad = norm_backward(middle, inverse_moe, moe_gain, moe_in_grad)
    mid_grad = upstream + mid_norm_grad
    mid_low = mid_grad.astype(bf16)
    output_grad = inner_product(attended_low, mid_low)
    attended_grad = times_transposed(mid_low, full_output).astype(bf16).reshape(head_shape)
    probs = jnp.exp(masked_scores() - log_total)
    probs_grad = jnp.einsum("qhd,khd->hqk", attended_grad, value_heads, preferred_element_type=f32)
    row_inner = jnp.sum(probs * probs_grad, axis=-1, keepdims=True)
    scores_grad = (probs * (probs_grad - row_inner)).astype(bf16)
    query_rot_grad = (
        jnp.einsum("hqk,khd->qhd", scores_grad, key_rot, preferred_element_type=f32) * score_scale
    )
    key_rot_grad = (
        jnp.einsum("hqk,qhd->khd", scores_grad, query_rot, preferred_element_type=f32) * score_scale
    )
    value_grad = jnp.einsum("hqk,qhd->khd", probs_low, attended_grad, preferred_element_type=f32)
    value_grad = value_grad.reshape(tokens_here, model_width).astype(bf16)
    query_back = rotate_back(query_rot_grad, cosine, sine_table).reshape(tokens_here, model_width)
    key_back = rotate_back(key_rot_grad, cosine, sine_table).reshape(tokens_here, model_width)
    query_pre_grad, query_gain_grad = norm_backward(
        query_pre, query_inverse, query_gain, query_back
    )
    key_pre_grad, key_gain_grad = norm_backward(key_pre, key_inverse, key_gain, key_back)
    query_low = query_pre_grad.astype(bf16)
    key_low = key_pre_grad.astype(bf16)
    act_grad = (
        times_transposed(query_low, full_query)
        + times_transposed(key_low, full_key)
        + times_transposed(value_grad, full_value)
    )
    query_weight_grad = inner_product(act_attn, query_low)
    key_weight_grad = inner_product(act_attn, key_low)
    value_weight_grad = inner_product(act_attn, value_grad)
    input_norm_grad, attn_gain_grad = norm_backward(inputs_f32, inverse_attn, attn_gain, act_grad)
    input_grad = (mid_grad + input_norm_grad).astype(bf16)
    sharded_grads = (
        lax.psum_scatter(attn_gain_grad, ("dp", "expert"), scatter_dimension=0, tiled=True),
        lax.psum_scatter(query_weight_grad, ("dp", "expert"), scatter_dimension=0, tiled=True),
        lax.psum_scatter(key_weight_grad, ("dp", "expert"), scatter_dimension=0, tiled=True),
        lax.psum_scatter(value_weight_grad, ("dp", "expert"), scatter_dimension=0, tiled=True),
        lax.psum_scatter(query_gain_grad, ("dp", "expert"), scatter_dimension=0, tiled=True),
        lax.psum_scatter(key_gain_grad, ("dp", "expert"), scatter_dimension=0, tiled=True),
        lax.psum_scatter(output_grad, ("dp", "expert"), scatter_dimension=0, tiled=True),
        lax.psum_scatter(moe_gain_grad, ("dp", "expert"), scatter_dimension=0, tiled=True),
        lax.psum_scatter(router_grad, ("dp", "expert"), scatter_dimension=0, tiled=True),
    )
    return (
        block_out,
        input_grad,
        sharded_grads[0],
        sharded_grads[1],
        sharded_grads[2],
        sharded_grads[3],
        sharded_grads[4],
        sharded_grads[5],
        sharded_grads[6],
        sharded_grads[7],
        sharded_grads[8],
        gate_weight_grad,
        up_weight_grad,
        down_grad,
    )


def solution(mesh):
    return jax.shard_map(
        body,
        mesh=mesh,
        in_specs=(
            P(("dp", "expert"), None),
            P(("dp", "expert"), None),
            P(("dp", "expert"), None),
            P(("dp", "expert"), None),
            P(),
            P(("dp", "expert"), None),
            P(("dp", "expert"), None),
            P(("dp", "expert"), None),
            P(),
            P(),
            P(("dp", "expert"), None),
            P(),
            P(("dp", "expert"), None),
            P("expert", None, None),
            P("expert", None, None),
            P("expert", None, None),
        ),
        out_specs=(
            P(("dp", "expert"), None),
            P(("dp", "expert"), None),
            P(("dp", "expert")),
            P(("dp", "expert"), None),
            P(("dp", "expert"), None),
            P(("dp", "expert"), None),
            P(("dp", "expert")),
            P(("dp", "expert")),
            P(("dp", "expert"), None),
            P(("dp", "expert")),
            P(("dp", "expert"), None),
            P("expert", None, "dp"),
            P("expert", None, "dp"),
            P("expert", "dp", None),
        ),
        check_vma=False,
    )
```

profile of v0, /device:TPU:0, one launch (start us, length us, event | category | flops | bytes accessed | tf_op | source)
XLA Modules:
  0.0 2884.2 jit_solution(9028882916465504682)
XLA Ops:
  19.0 72.2 %all-gather.8.cloned.1.call-done = bf16[2048,2048]{1,0:T(8,128)(2,1)} async-done(((bf16[64,2048]{1,0:T(8,128)(2,1)}), bf16[2048,2048]{1,0:T(8,128)(2,1)}) %all-gather.8.cloned.1.call-update) | async-done | bytes 8388624 | tf_op jit(solution)/shard_map/all_gather | solution.py:83
  96.6 73.7 %all-gather.10.cloned.1.call-done = bf16[2048,2048]{1,0:T(8,128)(2,1)} async-done(((bf16[64,2048]{1,0:T(8,128)(2,1)}), bf16[2048,2048]{1,0:T(8,128)(2,1)}) %all-gather.10.cloned.1.call-update) | async-done | bytes 8388624 | tf_op jit(solution)/shard_map/all_gather | solution.py:84
  181.1 68.2 %all-gather.6.cloned.1.call-done = bf16[2048,2048]{1,0:T(8,128)(2,1)} async-done(((bf16[64,2048]{1,0:T(8,128)(2,1)}), bf16[2048,2048]{1,0:T(8,128)(2,1)}) %all-gather.6.cloned.1.call-update) | async-done | bytes 8388624 | tf_op jit(solution)/shard_map/all_gather | solution.py:85
  257.7 70.5 %all-gather.12.cloned.1.call-done = bf16[2048,2048]{1,0:T(8,128)(2,1)} async-done(((bf16[64,2048]{1,0:T(8,128)(2,1)}), bf16[2048,2048]{1,0:T(8,128)(2,1)}) %all-gather.12.cloned.1.call-update) | async-done | bytes 8388624 | tf_op jit(solution)/shard_map/all_gather | solution.py:86
  328.2 16.1 multiply_reduce_fusion.5
  345.7 34.5 %scatter_custom_fusion = bf16[2048,2048]{1,0:T(8,128)(2,1)} fusion(s32[1536]{0:T(1024)S(1)} %fusion.98, bf16[192,2048]{1,0:T(8,128)(2,1)S(1)} %multiply_convert_fusion.3, s32[2048]{0:T(1024)S(1)} %pad_clamp_fusion.1, bf16[]{:T(256)} %constant.55.clone.1), kind=kCustom, calls=%fused_computation.32 | custom fusion | bytes 8388610 | tf_op jit(solution)/shard_map/scatter | solution.py:137
  385.2 238.4 %all-gather = bf16[32,64,16]{1,2,0:T(8,128)(2,1)S(1)} all-gather(bf16[1,64,16]{1,2,0:T(8,128)(2,1)S(1)} %bitcast.270), channel_id=1, replica_groups=mesh['dp'=2,'expert'=16] {'dp','expert'}, dimensions={0}, use_global_device_ids=true | all-gather | bytes 67584 | tf_op jit(solution)/shard_map/all_gather | solution.py:87
  624.8 14.6 scatter_custom_fusion.1
  645.4 14.5 fusion.27
  659.9 139.7 %all-to-all-done.2 = bf16[16,128,2048]{2,1,0:T(8,128)(2,1)} async-done(((bf16[16,128,2048]{2,1,0:T(8,128)(2,1)}), bf16[16,128,2048]{2,1,0:T(8,128)(2,1)}, u32[]{:S(2)}, u32[]{:S(2)}) %all-to-all-start.2) | async-done | bytes 8388640 | tf_op jit(solution)/shard_map/all_to_all | solution.py:169
  799.5 14.5 fusion.23
  814.0 21.3 fusion.19
  835.3 13.5 convolution_convert_fusion
  848.8 39.6 %all-to-all-start.1 = ((bf16[16,128,2048]{2,1,0:T(8,128)(2,1)}), bf16[16,128,2048]{2,1,0:T(8,128)(2,1)}, u32[]{:S(2)}, u32[]{:S(2)}) async-start(bf16[16,128,2048]{2,1,0:T(8,128)(2,1)} %convolution_convert_fusion), calls=%async_computation.1 | async-start | bytes 16777216 | tf_op jit(solution)/shard_map/all_to_all | solution.py:156
  888.5 14.1 fusion.38
  902.6 15.3 fusion.21
  918.0 15.0 add_convert_fusion
  933.0 106.6 %all-to-all-done.1 = bf16[16,128,2048]{2,1,0:T(8,128)(2,1)} async-done(((bf16[16,128,2048]{2,1,0:T(8,128)(2,1)}), bf16[16,128,2048]{2,1,0:T(8,128)(2,1)}, u32[]{:S(2)}, u32[]{:S(2)}) %all-to-all-start.1) | async-done | bytes 8388640 | tf_op jit(solution)/shard_map/all_to_all | solution.py:156
  1039.6 37.1 %all-to-all-start.3 = ((bf16[16,128,2048]{2,1,0:T(8,128)(2,1)}), bf16[16,128,2048]{2,1,0:T(8,128)(2,1)}, u32[]{:S(2)}, u32[]{:S(2)}) async-start(bf16[16,128,2048]{2,1,0:T(8,128)(2,1)} %add_convert_fusion), calls=%async_computation.3 | async-start | bytes 16777216 | tf_op jit(solution)/shard_map/all_to_all | solution.py:203
  1076.7 14.0 fusion.37
  1090.8 14.2 fusion.34
  1105.7 17.7 gather_fusion
  1130.0 100.2 %all-to-all-done.3 = bf16[16,128,2048]{2,1,0:T(8,128)(2,1)} async-done(((bf16[16,128,2048]{2,1,0:T(8,128)(2,1)}), bf16[16,128,2048]{2,1,0:T(8,128)(2,1)}, u32[]{:S(2)}, u32[]{:S(2)}) %all-to-all-start.3) | async-done | bytes 8388640 | tf_op jit(solution)/shard_map/all_to_all | solution.py:203
  1230.3 17.3 gather_fusion.1
  1280.5 8.2 fusion.67
  1299.2 8.2 fusion.105
  1311.5 8.2 fusion.107
  1346.2 72.3 %all-reduce.4 = (f32[2048]{0:T(1024)S(1)}, f32[2048]{0:T(1024)S(1)}, f32[2048]{0:T(1024)S(1)}, f32[2048]{0:T(1024)S(1)}) all-reduce(f32[2048]{0:T(1024)S(1)} %get-tuple-element.22, f32[2048]{0:T(1024)S(1)} %get-tuple-element.20, f32[2048]{0:T(1024)S(1)} %get-tuple-element.18, ...), channel_id=2, replica_groups=mesh['dp'=2,'expert'=16] {'dp','expert'}, use_global_device_ids=true, to_apply=%region_25.26.clone | all-reduce | flops 8192 | bytes 65536
  1433.3 355.4 %reduce-scatter.17.cloned.1.call-done = f32[64,2048]{1,0:T(8,128)} async-done(((f32[2048,2048]{1,0:T(8,128)}), f32[64,2048]{1,0:T(8,128)}) %reduce-scatter.17.cloned.1.call-update) | async-done | bytes 524304 | tf_op jit(solution)/shard_map/reduce_scatter | solution.py:262
  1788.7 362.8 %reduce-scatter.15.cloned.1.call-done = f32[64,2048]{1,0:T(8,128)} async-done(((f32[2048,2048]{1,0:T(8,128)}), f32[64,2048]{1,0:T(8,128)}) %reduce-scatter.15.cloned.1.call-update) | async-done | bytes 524304 | tf_op jit(solution)/shard_map/reduce_scatter | solution.py:259
  2151.5 362.9 %reduce-scatter.13.cloned.1.call-done = f32[64,2048]{1,0:T(8,128)} async-done(((f32[2048,2048]{1,0:T(8,128)}), f32[64,2048]{1,0:T(8,128)}) %reduce-scatter.13.cloned.1.call-update) | async-done | bytes 524304 | tf_op jit(solution)/shard_map/reduce_scatter | solution.py:258
  2514.4 362.8 %reduce-scatter.11.cloned.1.call-done = f32[64,2048]{1,0:T(8,128)} async-done(((f32[2048,2048]{1,0:T(8,128)}), f32[64,2048]{1,0:T(8,128)}) %reduce-scatter.11.cloned.1.call-update) | async-done | bytes 524304 | tf_op jit(solution)/shard_map/reduce_scatter | solution.py:257
  (268 shorter events, 145.0 us)
Async XLA Ops:
  7.2 84.0 %all-gather.8.cloned.1.call-start = ((), (), s32[]{:S(2)}) async-start(), calls=%async_computation.13 | async-start | bytes 8650752 | tf_op jit(solution)/shard_map/all_gather | solution.py:83
  7.9 162.3 %all-gather.10.cloned.1.call-start = ((), (), s32[]{:S(2)}) async-start(), calls=%async_computation.14 | async-start | bytes 8650752 | tf_op jit(solution)/shard_map/all_gather | solution.py:84
  8.7 240.6 %all-gather.6.cloned.1.call-start = ((), (), s32[]{:S(2)}) async-start(), calls=%async_computation.12 | async-start | bytes 8650752 | tf_op jit(solution)/shard_map/all_gather | solution.py:85
  9.4 81.8 %copy-start.39 = (f32[2048]{0:T(1024)S(1)}, f32[2048]{0:T(1024)}, u32[]{:S(2)}) copy-start(f32[2048]{0:T(1024)} %param.20) | copy-start | bytes 24580
  9.4 318.8 %all-gather.12.cloned.1.call-start = ((), (), s32[]{:S(2)}) async-start(), calls=%async_computation.15 | async-start | bytes 8650752 | tf_op jit(solution)/shard_map/all_gather | solution.py:86
  17.4 607.4 %copy-start.53 = (s32[1536]{0:T(1024)}, s32[1536]{0:T(1024)S(1)}, u32[]{:S(2)}) copy-start(s32[1536]{0:T(1024)S(1)} %fusion.98) | copy-start | bytes 18436
  18.8 230.5 %copy-start.51 = (f32[192]{0:T(256)}, f32[192]{0:T(256)S(1)}, u32[]{:S(2)}) copy-start(f32[192]{0:T(256)S(1)} %add_rsqrt_fusion.3) | copy-start | bytes 2308
  18.9 235.9 %copy-start.24 = (pred[192,192]{0,1:T(8,128)(4,1)}, pred[192,192]{0,1:T(8,128)(4,1)S(1)}, u32[]{:S(2)}) copy-start(pred[192,192]{0,1:T(8,128)(4,1)S(1)} %fusion.88) | copy-start | bytes 110596
  96.5 79.1 %copy-start.5 = (f32[192,2048]{1,0:T(8,128)}, f32[192,2048]{1,0:T(8,128)S(1)}, u32[]{:S(2)}) copy-start(f32[192,2048]{1,0:T(8,128)S(1)} %get-tuple-element.54) | copy-start | bytes 4718596
  96.5 79.1 %copy-start.57 = (f32[192]{0:T(256)}, f32[192]{0:T(256)S(1)}, u32[]{:S(2)}) copy-start(f32[192]{0:T(256)S(1)} %add_rsqrt_fusion.2) | copy-start | bytes 2308
  96.6 79.1 %copy-start.47 = (f32[2048]{0:T(1024)S(1)}, f32[2048]{0:T(1024)}, u32[]{:S(2)}) copy-start(f32[2048]{0:T(1024)} %param.25) | copy-start | bytes 24580
  96.6 79.1 %copy-start.49 = (f32[2048]{0:T(1024)S(1)}, f32[2048]{0:T(1024)}, u32[]{:S(2)}) copy-start(f32[2048]{0:T(1024)} %param.24) | copy-start | bytes 24580
  180.3 74.5 %copy-start = (f32[16,192,192]{1,2,0:T(8,128)}, f32[16,192,192]{1,2,0:T(8,128)S(1)}, u32[]{:S(2)}) copy-start(f32[16,192,192]{1,2,0:T(8,128)S(1)} %get-tuple-element.56) | copy-start | bytes 7077892
  181.1 73.7 %copy-start.41 = (f32[16,192]{1,0:T(8,128)}, f32[16,192]{1,0:T(8,128)S(1)}, u32[]{:S(2)}) copy-start(f32[16,192]{1,0:T(8,128)S(1)} %log_add_fusion) | copy-start | bytes 36868
  257.7 87.8 %copy-start.45 = (f32[2048]{0:T(1024)S(1)}, f32[2048]{0:T(1024)}, u32[]{:S(2)}) copy-start(f32[2048]{0:T(1024)} %param.27) | copy-start | bytes 24580
  344.3 35.9 %copy-start.61 = (f32[192]{0:T(256)}, f32[192]{0:T(256)S(1)}, u32[]{:S(2)}) copy-start(f32[192]{0:T(256)S(1)} %add_rsqrt_fusion) | copy-start | bytes 2308
  345.6 278.4 %copy-start.15 = (bf16[192,2048]{1,0:T(8,128)(2,1)}, bf16[192,2048]{1,0:T(8,128)(2,1)S(1)}, u32[]{:S(2)}) copy-start(bf16[192,2048]{1,0:T(8,128)(2,1)S(1)} %multiply_convert_fusion.3) | copy-start | bytes 2359300
  380.2 243.6 %copy-start.23 = (bf16[192,2048]{1,0:T(8,128)(2,1)S(1)}, bf16[192,2048]{1,0:T(8,128)(2,1)}, u32[]{:S(2)}) copy-start(bf16[192,2048]{1,0:T(8,128)(2,1)} %param.17) | copy-start | bytes 2359300
  380.2 259.3 %all-to-all-start = ((bf16[16,128,2048]{2,1,0:T(8,128)(2,1)}), bf16[16,128,2048]{2,1,0:T(8,128)(2,1)}, u32[]{:S(2)}, u32[]{:S(2)}) async-start(bf16[16,128,2048]{2,1,0:T(8,128)(2,1)} %bitcast.262), calls=%async_computation | async-start | bytes 16777216 | tf_op jit(solution)/shard_map/all_to_all | solution.py:144
  639.5 160.0 %all-to-all-start.2 = ((bf16[16,128,2048]{2,1,0:T(8,128)(2,1)}), bf16[16,128,2048]{2,1,0:T(8,128)(2,1)}, u32[]{:S(2)}, u32[]{:S(2)}) async-start(bf16[16,128,2048]{2,1,0:T(8,128)(2,1)} %bitcast.263), calls=%async_computation.2 | async-start | bytes 16777216 | tf_op jit(solution)/shard_map/all_to_all | solution.py:169
  814.0 21.3 copy-start.67
  848.8 190.8 %all-to-all-start.1 = ((bf16[16,128,2048]{2,1,0:T(8,128)(2,1)}), bf16[16,128,2048]{2,1,0:T(8,128)(2,1)}, u32[]{:S(2)}, u32[]{:S(2)}) async-start(bf16[16,128,2048]{2,1,0:T(8,128)(2,1)} %convolution_convert_fusion), calls=%async_computation.1 | async-start | bytes 16777216 | tf_op jit(solution)/shard_map/all_to_all | solution.py:156
  888.4 431.3 %reduce-scatter.23.cloned.1.call-start = ((), (), s32[]{:S(2)}) async-start(), calls=%async_computation.22 | async-start | bytes 6291456 | tf_op jit(solution)/shard_map/reduce_scatter | solution.py:199
  1039.6 190.7 %all-to-all-start.3 = ((bf16[16,128,2048]{2,1,0:T(8,128)(2,1)}), bf16[16,128,2048]{2,1,0:T(8,128)(2,1)}, u32[]{:S(2)}, u32[]{:S(2)}) async-start(bf16[16,128,2048]{2,1,0:T(8,128)(2,1)} %add_convert_fusion), calls=%async_computation.3 | async-start | bytes 16777216 | tf_op jit(solution)/shard_map/all_to_all | solution.py:203
  1076.6 247.2 %reduce-scatter.21.cloned.1.call-start = ((), (), s32[]{:S(2)}) async-start(), calls=%async_computation.21 | async-start | bytes 6291456 | tf_op jit(solution)/shard_map/reduce_scatter | solution.py:196
  1090.7 237.4 %reduce-scatter.19.cloned.1.call-start = ((), (), s32[]{:S(2)}) async-start(), calls=%async_computation.20 | async-start | bytes 6291456 | tf_op jit(solution)/shard_map/reduce_scatter | solution.py:193
  1105.0 326.8 %reduce-scatter.25.cloned.1.call-start = ((), (), s32[]{:S(2)}) async-start(), calls=%async_computation.23 | async-start | bytes 1081344
  1259.1 529.6 %reduce-scatter.17.cloned.1.call-start = ((), (), s32[]{:S(2)}) async-start(), calls=%async_computation.19 | async-start | bytes 17301504 | tf_op jit(solution)/shard_map/reduce_scatter | solution.py:262
  1271.5 880.0 %reduce-scatter.15.cloned.1.call-start = ((), (), s32[]{:S(2)}) async-start(), calls=%async_computation.18 | async-start | bytes 17301504 | tf_op jit(solution)/shard_map/reduce_scatter | solution.py:259
  1288.7 1225.7 %reduce-scatter.13.cloned.1.call-start = ((), (), s32[]{:S(2)}) async-start(), calls=%async_computation.17 | async-start | bytes 17301504 | tf_op jit(solution)/shard_map/reduce_scatter | solution.py:258
  1307.4 1569.7 %reduce-scatter.11.cloned.1.call-start = ((), (), s32[]{:S(2)}) async-start(), calls=%async_computation.16 | async-start | bytes 17301504 | tf_op jit(solution)/shard_map/reduce_scatter | solution.py:257
  1341.9 79.0 %copy-start.14 = (f32[192,2048]{1,0:T(8,128)S(1)}, f32[192,2048]{1,0:T(8,128)}, u32[]{:S(2)}) copy-start(f32[192,2048]{1,0:T(8,128)} %copy-done.13) | copy-start | bytes 4718596
  (58 other events, 363.8 us)
Sparse Core Ops, SparseCore 0:
  10.9 80.2 all-gather.7
  94.1 76.1 all-gather.9
  173.1 76.1 all-gather.5
  252.0 76.1 all-gather.11
  902.7 13.2 reduce-scatter.22
  1090.8 13.2 reduce-scatter.20
  1107.0 13.3 reduce-scatter.18
  1259.2 172.6 reduce-scatter.24
  1434.7 353.9 reduce-scatter.16
  1791.4 360.0 reduce-scatter.14
  2154.3 360.0 reduce-scatter.12
  2517.1 360.0 reduce-scatter.10
where the time goes:
time: 2890 us; the launch traced here: 2880 us
  waiting for transfers between devices  2090 us (72%)
  blocking collectives  311 us (11%)
  matrix products  233 us (8%)
  starting transfers between devices  88.8 us (3%)
  local copies, waits for them, and re-layouts  85.4 us (3%)
  other arithmetic  65 us (2%)
    reduce_scatter x1, waiting for transfers between devices, body(): lax.psum_scatter(key_weight_grad, ('dp', 'expert'), scatter_dimension=0,...  363 us
    reduce_scatter x1, waiting for transfers between devices, body(): lax.psum_scatter(query_weight_grad, ('dp', 'expert'), scatter_dimension=0...  363 us
    reduce_scatter x1, waiting for transfers between devices, body(): lax.psum_scatter(value_weight_grad, ('dp', 'expert'), scatter_dimension=0...  363 us
    reduce_scatter x1, waiting for transfers between devices, body(): lax.psum_scatter(output_grad, ('dp', 'expert'), scatter_dimension=0, tile...  355 us
    all_gather x1, blocking collectives, body(): lax.all_gather(w_router, ('dp', 'expert'), axis=0, tiled=True)  238 us
    all_to_all x1, waiting for transfers between devices, body(): lax.all_to_all(to_experts(pair_grad.reshape(-1, model_width)), 'expert',...  140 us
    all_to_all x1, waiting for transfers between devices, body(): lax.all_to_all(expert_out.reshape(owners * local_experts, capacity, model...  107 us
    all_to_all x1, waiting for transfers between devices, body(): lax.all_to_all(row_grad.reshape(owners * local_experts, capacity, model_w...  100 us
  transfers between devices with their start and end apart: 16, of which 12 were waited for; matrix products, arithmetic and copies ran while one was open for 9% of the time, Pallas kernels for 0%

commit v1 on v0

--- a/solution.py
+++ b/solution.py
@@ -1,6 +1,10 @@
+import functools
+
 import jax
 import jax.numpy as jnp
 from jax import lax
+from jax.experimental import pallas as pl
+from jax.experimental.pallas import tpu as pltpu
 from jax.sharding import PartitionSpec as P
 
 HD = 128
@@ -50,7 +54,7 @@
     return jnp.einsum("ta,tb->ab", left, right, preferred_element_type=jnp.float32)
 
 
-def body(
+def body_routed(
     hidden_in,
     cotangent,
     doc_ids,
@@ -281,7 +285,502 @@
     )
 
 
+NZ, NY, NX = 4, 2, 2
+VMEM_LIMIT = 48 * 1024 * 1024
+
+
+def chip(z, y, x):
+    return (z * NY + y) * NX + x
+
+
+GRID = [(z, y, x) for z in range(NZ) for y in range(NY) for x in range(NX)]
+X_PAIRS = [(chip(z, y, x), chip(z, y, 1 - x)) for z, y, x in GRID]
+Y_PAIRS = [(chip(z, y, x), chip(z, 1 - y, x)) for z, y, x in GRID]
+Z_PAIRS = [(chip(z, y, x), chip((z + 1) % NZ, y, x)) for z, y, x in GRID]
+CORE_PAIRS = [(0, 1), (1, 0)]
+
+
+def move_x(values):
+    return lax.ppermute(values, "expert", X_PAIRS)
+
+
+def move_y(values):
+    return lax.ppermute(values, "expert", Y_PAIRS)
+
+
+def move_z(values):
+    return lax.ppermute(values, "expert", Z_PAIRS)
+
+
+def move_core(values):
+    return lax.ppermute(values, "dp", CORE_PAIRS)
+
+
+def split_row(rows):
+    return (rows // 2 + 15) // 16 * 16
+
+
+def gather_z(block):
+    ring = [block]
+    for _ in range(1, NZ):
+        ring.append(move_z(ring[-1]))
+    return ring
+
+
+def gather_plane(block):
+    cut = split_row(block.shape[0])
+    from_x = move_x(block)
+    from_y = move_y(block)
+    across = jnp.concatenate([move_x(from_y[:cut]), move_y(from_x[cut:])], axis=0)
+    return [block, from_x, from_y, across]
+
+
+def gather_chips(block):
+    return [gather_plane(part) for part in gather_z(block)]
+
+
+def add_f32(left, right):
+    return left.astype(jnp.float32) + right.astype(jnp.float32)
+
+
+def reduce_plane(parts):
+    own, for_x, for_y, for_across = parts
+    low = own.dtype
+    cut = split_row(own.shape[0])
+    by_x = move_x(for_across[:cut])
+    by_y = move_y(for_across[cut:])
+    for_y = jnp.concatenate([add_f32(for_y[:cut], by_x).astype(low), for_y[cut:]], axis=0)
+    for_x = jnp.concatenate([for_x[:cut], add_f32(for_x[cut:], by_y).astype(low)], axis=0)
+    return add_f32(own, move_x(for_x)) + move_y(for_y).astype(jnp.float32)
+
+
+def reduce_z(ring):
+    total = ring[1].astype(jnp.bfloat16)
+    for step in range(2, NZ):
+        total = add_f32(move_z(total), ring[step]).astype(jnp.bfloat16)
+    return add_f32(move_z(total), ring[0])
+
+
+def reduce_chips(parts):
+    return reduce_z([reduce_plane(part) for part in parts])
+
+
+def place_of(position, k):
+    return (position[2] ^ (k >> 1)) * NX + (position[3] ^ (k & 1))
+
+
+def chunk_copies(position, pieces, rows, slot, held, sems, chunk):
+    out = []
+    for k in range(NY * NX):
+        place = pl.multiple_of(place_of(position, k) * rows, rows)
+        out.append(
+            pltpu.make_async_copy(
+                pieces[chunk].at[k, pl.ds(slot * rows, rows)],
+                held.at[chunk, pl.ds(place, rows)],
+                sems.at[chunk, k],
+            )
+        )
+    return out
+
+
+def chunk_base(position, rows, chunk):
+    other, step = chunk // NZ, chunk % NZ
+    half = position[0] ^ other
+    z_of = (position[1] + NZ - step) % NZ
+    span = NY * NX * rows
+    return pl.multiple_of((half * NZ + z_of) * span, span)
+
+
+def apply_kernel(position, acts, *refs, rows, slot, tile):
+    pieces, (out, held, sems) = refs[: 2 * NZ], refs[2 * NZ :]
+    for chunk in range(2 * NZ):
+        for copy in chunk_copies(position, pieces, rows, slot, held, sems, chunk):
+            copy.start()
+    span = NY * NX * rows
+    for chunk in range(2 * NZ):
+        for copy in chunk_copies(position, pieces, rows, slot, held, sems, chunk):
+            copy.wait()
+        left = acts[:, pl.ds(chunk_base(position, rows, chunk), span)]
+
+        @pl.loop(0, out.shape[1] // tile)
+        def _(i):
+            columns = pl.ds(pl.multiple_of(i * tile, tile), tile)
+            part = jnp.dot(left, held[chunk, :, columns], preferred_element_type=jnp.float32)
+            if chunk == 0:
+                out[:, columns] = part
+            else:
+                out[:, columns] += part
+
+
+def apply_back_kernel(position, grads, *refs, rows, slot):
+    pieces, (out, held, sems) = refs[: 2 * NZ], refs[2 * NZ :]
+    for chunk in range(2 * NZ):
+        for copy in chunk_copies(position, pieces, rows, slot, held, sems, chunk):
+            copy.start()
+    span = NY * NX * rows
+    for chunk in range(2 * NZ):
+        for copy in chunk_copies(position, pieces, rows, slot, held, sems, chunk):
+            copy.wait()
+        out[:, pl.ds(chunk_base(position, rows, chunk), span)] = lax.dot_general(
+            grads[...], held[chunk], (((1,), (1,)), ((), ())), preferred_element_type=jnp.float32
+        )
+
+
+def apply_weight(position, values, pieces, rows, slot, back=False):
+    tokens, width = values.shape
+    kernel = (
+        functools.partial(apply_back_kernel, rows=rows, slot=slot)
+        if back
+        else functools.partial(apply_kernel, rows=rows, slot=slot, tile=512)
+    )
+    return pl.pallas_call(
+        kernel,
+        out_shape=jax.ShapeDtypeStruct((tokens, width), jnp.float32),
+        in_specs=[pl.BlockSpec(memory_space=pltpu.SMEM), pl.BlockSpec(memory_space=pltpu.VMEM)]
+        + [pl.BlockSpec(memory_space=pl.ANY)] * len(pieces),
+        out_specs=pl.BlockSpec(memory_space=pltpu.VMEM),
+        scratch_shapes=[
+            pltpu.VMEM((2 * NZ, NY * NX * rows, width), jnp.bfloat16),
+            pltpu.SemaphoreType.DMA((2 * NZ, NY * NX)),
+        ],
+        compiler_params=pltpu.CompilerParams(vmem_limit_bytes=VMEM_LIMIT),
+        cost_estimate=pl.CostEstimate(
+            flops=2 * tokens * width * width,
+            bytes_accessed=2 * width * width + 6 * tokens * width,
+            transcendentals=0,
+        ),
+    )(position, values, *pieces)
+
+
+def weight_grad_kernel(position, own_left, other_left, *refs, rows, count, tile):
+    grads, outs, stage = refs[: 2 * count], refs[2 * count : -1], refs[-1]
+    span = NY * NX * rows
+    for step in range(NZ):
+        z_of = (position[1] + NZ - step) % NZ
+        columns = pl.ds(pl.multiple_of(z_of * span, span), span)
+        own, other = own_left[:, columns], other_left[:, columns]
+        for i in range(count):
+
+            @pl.loop(0, grads[0].shape[1] // tile)
+            def _(j):
+                part = pl.ds(pl.multiple_of(j * tile, tile), tile)
+                product = lax.dot_general(
+                    own,
+                    grads[2 * i][:, part],
+                    (((0,), (0,)), ((), ())),
+                    preferred_element_type=jnp.float32,
+                ) + lax.dot_general(
+                    other,
+                    grads[2 * i + 1][:, part],
+                    (((0,), (0,)), ((), ())),
+                    preferred_element_type=jnp.float32,
+                )
+                stage[...] = product.astype(stage.dtype)
+                for k in range(NY * NX):
+                    place = pl.multiple_of(place_of(position, k) * rows, rows)
+                    outs[step * NY * NX + k][pl.ds(i * rows, rows), part] = stage[pl.ds(place, rows), :]
+
+
+def weight_grad_parts(position, own_left, other_left, grads, rows):
+    count, width = len(grads) // 2, grads[0].shape[1]
+    tokens, tile = own_left.shape[0], 512
+    block = jax.ShapeDtypeStruct((count * rows, width), jnp.bfloat16)
+    outs = pl.pallas_call(
+        functools.partial(weight_grad_kernel, rows=rows, count=count, tile=tile),
+        out_shape=[block] * (NZ * NY * NX),
+        in_specs=[pl.BlockSpec(memory_space=pltpu.SMEM)]
+        + [pl.BlockSpec(memory_space=pltpu.VMEM)] * (2 + len(grads)),
+        out_specs=[pl.BlockSpec(memory_space=pltpu.VMEM)] * (NZ * NY * NX),
+        scratch_shapes=[pltpu.VMEM((NY * NX * rows, tile), jnp.bfloat16)],
+        compiler_params=pltpu.CompilerParams(vmem_limit_bytes=VMEM_LIMIT),
+        cost_estimate=pl.CostEstimate(
+            flops=4 * count * tokens * NZ * NY * NX * rows * width,
+            bytes_accessed=2 * count * NZ * NY * NX * rows * width + 4 * tokens * width * (count + 1),
+            transcendentals=0,
+        ),
+    )(position, own_left, other_left, *grads)
+    return [outs[s * NY * NX : (s + 1) * NY * NX] for s in range(NZ)]
+
+
+def gather_weights(blocks):
+    ring = [jnp.stack(part) for part in gather_chips(jnp.concatenate(blocks, axis=0))]
+    return ring + [move_core(part) for part in ring]
+
+
+def after(values, earlier):
+    return values + (earlier[(0,) * earlier.ndim] * 0).astype(values.dtype)
+
+
+def body_dense(
+    hidden_in,
+    cotangent,
+    doc_ids,
+    routes,
+    attn_gain,
+    w_query,
+    w_key,
+    w_value,
+    query_gain,
+    key_gain,
+    w_output,
+    moe_gain,
+    w_router,
+    w_gate,
+    w_up,
+    w_down,
+):
+    f32 = jnp.float32
+    bf16 = jnp.bfloat16
+    tokens_here, model_width = hidden_in.shape
+    head_dim = HD
+    head_count = model_width // head_dim
+    rows = w_query.shape[0]
+    experts_all = w_router.shape[1]
+    owners = lax.axis_size("expert")
+    core = lax.axis_index("dp")
+    here = lax.axis_index("expert")
+    z_at, y_at, x_at = here // (NY * NX), here // NX % NY, here % NX
+    position = jnp.stack([core, z_at, y_at, x_at]).astype(jnp.int32)
+    half_width = model_width // 2
+    order = jnp.stack(
+        [
+            chip((z_at + NZ - s) % NZ, y_at ^ (k >> 1), x_at ^ (k & 1))
+            for s in range(NZ)
+            for k in range(NY * NX)
+        ]
+    )
+
+    expert_ids = jnp.arange(experts_all, dtype=jnp.int32)
+    chosen = routes[:, :, None] == expert_ids[None, None, :]
+    uses = jnp.any(chosen, axis=1).astype(f32)
+    router_block = jnp.broadcast_to(w_router.astype(f32).reshape(1, -1), (owners, w_router.size))
+    small = lax.all_to_all(
+        jnp.concatenate([uses.T, router_block], axis=1), "expert", split_axis=0, concat_axis=0, tiled=True
+    )
+    used_here = small[:, :tokens_here][order].reshape(NZ, NY * NX * tokens_here, 1)
+    own_router = small[:, tokens_here:].reshape(-1, experts_all)
+    other_router = move_core(own_router)
+    full_router = jnp.where(
+        core == 0,
+        jnp.concatenate([own_router, other_router], axis=0),
+        jnp.concatenate([other_router, own_router], axis=0),
+    ).astype(bf16)
+
+    pieces_qk = gather_weights([w_query, w_key])
+    pieces_vo = gather_weights([w_value, w_output])
+
+    inputs_f32 = hidden_in.astype(f32)
+    normed_attn, inverse_attn = norm_forward(inputs_f32, attn_gain)
+    act_attn = normed_attn.astype(bf16)
+    own_act = lax.dynamic_slice_in_dim(act_attn, core * half_width, half_width, axis=1)
+    other_act = move_core(
+        lax.dynamic_slice_in_dim(act_attn, (1 - core) * half_width, half_width, axis=1)
+    )
+    query_pre = apply_weight(position, act_attn, pieces_qk, rows, 0)
+    key_pre = apply_weight(position, act_attn, pieces_qk, rows, 1)
+    value_low = apply_weight(position, act_attn, pieces_vo, rows, 0).astype(bf16)
+    query_normed, query_inverse = norm_forward(query_pre, query_gain)
+    key_normed, key_inverse = norm_forward(key_pre, key_gain)
+    cosine, sine_table = rotary_tables(tokens_here, head_dim)
+    head_shape = (tokens_here, head_count, head_dim)
+    query_rot = rotate(query_normed.reshape(head_shape), cosine, sine_table).astype(bf16)
+    key_rot = rotate(key_normed.reshape(head_shape), cosine, sine_table).astype(bf16)
+    value_heads = value_low.reshape(head_shape)
+    score_scale = head_dim ** (-0.5)
+    token_at = jnp.arange(tokens_here, dtype=jnp.int32)
+    allowed = (token_at[:, None] >= token_at[None, :]) & (
+        doc_ids[0][:, None] == doc_ids[0][None, :]
+    )
+    scores = (
+        jnp.einsum("qhd,khd->hqk", query_rot, key_rot, preferred_element_type=f32) * score_scale
+    )
+    scores = jnp.where(allowed[None], scores, -1e30)
+    row_max = jnp.max(scores, axis=-1, keepdims=True)
+    row_sum = jnp.sum(jnp.exp(scores - row_max), axis=-1, keepdims=True)
+    log_total = row_max + jnp.log(row_sum)
+    probs = jnp.exp(scores - log_total)
+    probs_low = probs.astype(bf16)
+    attended = jnp.einsum("hqk,khd->qhd", probs_low, value_heads, preferred_element_type=f32)
+    attended_low = attended.reshape(tokens_here, model_width).astype(bf16)
+    middle = inputs_f32 + apply_weight(position, attended_low, pieces_vo, rows, 1)
+    normed_moe, inverse_moe = norm_forward(middle, moe_gain)
+    act_moe = normed_moe.astype(bf16)
+
+    acts = gather_chips(act_moe)
+    grads_out = gather_chips(after(cotangent, pieces_vo[NZ - 1]))
+
+    logits = jnp.dot(act_moe, full_router, preferred_element_type=f32)
+    router_probs = jax.nn.softmax(logits, axis=-1)
+
+    gate_w, up_w, down_w = w_gate[0], w_up[0], w_down[0]
+    mine = (expert_ids == here).astype(f32)
+    out_parts, row_parts, dots = [], [], []
+    all_acts, all_hidden, all_out_grads, all_gate_grads, all_up_grads = [], [], [], [], []
+    for s in range(NZ):
+        act_rows = jnp.concatenate(acts[s], axis=0)
+        probs_rows = jax.nn.softmax(
+            jnp.dot(act_rows, full_router, preferred_element_type=f32), axis=-1
+        )
+        gate_rows = jnp.sum(probs_rows * mine[None, :], axis=-1, keepdims=True) * used_here[s]
+        gate_pre = jnp.dot(act_rows, gate_w, preferred_element_type=f32)
+        up_pre = jnp.dot(act_rows, up_w, preferred_element_type=f32)
+        sigmoid = jax.nn.sigmoid(gate_pre)
+        swish = gate_pre * sigmoid
+        hidden_low = (swish * up_pre).astype(bf16)
+        expert_out = jnp.dot(hidden_low, down_w, preferred_element_type=f32).astype(bf16)
+        out_low = (gate_rows * expert_out.astype(f32)).astype(bf16)
+        out_parts.append(jnp.split(out_low, NY * NX, axis=0))
+        upstream_rows = jnp.concatenate(grads_out[s], axis=0)
+        upstream_f32 = upstream_rows.astype(f32)
+        dots.append(jnp.sum(upstream_f32 * expert_out.astype(f32), axis=-1, keepdims=True) * used_here[s])
+        out_grad = (gate_rows * upstream_f32).astype(bf16)
+        hidden_grad = times_transposed(out_grad, down_w)
+        slope = sigmoid * (1.0 + gate_pre * (1.0 - sigmoid))
+        gate_pre_grad = (hidden_grad * up_pre * slope).astype(bf16)
+        up_pre_grad = (hidden_grad * swish).astype(bf16)
+        row_grad = (
+            times_transposed(gate_pre_grad, gate_w) + times_transposed(up_pre_grad, up_w)
+        ).astype(bf16)
+        row_parts.append(jnp.split(row_grad, NY * NX, axis=0))
+        all_acts.append(act_rows)
+        all_hidden.append(hidden_low)
+        all_out_grads.append(out_grad)
+        all_gate_grads.append(gate_pre_grad)
+        all_up_grads.append(up_pre_grad)
+    choice_rows = jnp.zeros((owners, tokens_here), f32).at[order].set(
+        jnp.concatenate(dots, axis=0).reshape(owners, tokens_here)
+    )
+    choice_grad = lax.all_to_all(
+        choice_rows, "expert", split_axis=0, concat_axis=0, tiled=True
+    ).T
+    moe_in_grad = reduce_chips(row_parts)
+
+    logit_grad = router_probs * (
+        choice_grad - jnp.sum(router_probs * choice_grad, axis=-1, keepdims=True)
+    )
+    logit_low = logit_grad.astype(bf16)
+    moe_in_grad = moe_in_grad + times_transposed(logit_low, full_router)
+    router_grad = inner_product(act_moe, logit_low)
+    upstream = cotangent.astype(f32)
+    mid_norm_grad, moe_gain_grad = norm_backward(middle, inverse_moe, moe_gain, moe_in_grad)
+    mid_grad = upstream + mid_norm_grad
+    mid_low = mid_grad.astype(bf16)
+
+    own_attended = lax.dynamic_slice_in_dim(attended_low, core * half_width, half_width, axis=1)
+    other_attended = move_core(
+        lax.dynamic_slice_in_dim(attended_low, (1 - core) * half_width, half_width, axis=1)
+    )
+    output_grad = reduce_chips(
+        weight_grad_parts(
+            position, own_attended, other_attended, [mid_low, move_core(mid_low)], rows
+        )
+    )
+    attended_grad = (
+        apply_weight(position, mid_low, pieces_vo, rows, 1, back=True)
+        .astype(bf16)
+        .reshape(head_shape)
+    )
+    probs_grad = jnp.einsum("qhd,khd->hqk", attended_grad, value_heads, preferred_element_type=f32)
+    row_inner = jnp.sum(probs * probs_grad, axis=-1, keepdims=True)
+    scores_grad = (probs * (probs_grad - row_inner)).astype(bf16)
+    query_rot_grad = (
+        jnp.einsum("hqk,khd->qhd", scores_grad, key_rot, preferred_element_type=f32) * score_scale
+    )
+    key_rot_grad = (
+        jnp.einsum("hqk,qhd->khd", scores_grad, query_rot, preferred_element_type=f32) * score_scale
+    )
+    value_grad = jnp.einsum("hqk,qhd->khd", probs_low, attended_grad, preferred_element_type=f32)
+    value_grad = value_grad.reshape(tokens_here, model_width).astype(bf16)
+    query_back = rotate_back(query_rot_grad, cosine, sine_table).reshape(tokens_here, model_width)
+    key_back = rotate_back(key_rot_grad, cosine, sine_table).reshape(tokens_here, model_width)
+    query_pre_grad, query_gain_grad = norm_backward(
+        query_pre, query_inverse, query_gain, query_back
+    )
+    key_pre_grad, key_gain_grad = norm_backward(key_pre, key_inverse, key_gain, key_back)
+    query_low = query_pre_grad.astype(bf16)
+    key_low = key_pre_grad.astype(bf16)
+    attn_weight_grads = reduce_chips(
+        weight_grad_parts(
+            position,
+            own_act,
+            other_act,
+            [
+                query_low,
+                move_core(query_low),
+                key_low,
+                move_core(key_low),
+                value_grad,
+                move_core(value_grad),
+            ],
+            rows,
+        )
+    )
+    query_weight_grad, key_weight_grad, value_weight_grad = jnp.split(attn_weight_grads, 3, axis=0)
+    act_grad = (
+        apply_weight(position, query_low, pieces_qk, rows, 0, back=True)
+        + apply_weight(position, key_low, pieces_qk, rows, 1, back=True)
+        + apply_weight(position, value_grad, pieces_vo, rows, 0, back=True)
+    )
+    input_norm_grad, attn_gain_grad = norm_backward(inputs_f32, inverse_attn, attn_gain, act_grad)
+    input_grad = (mid_grad + input_norm_grad).astype(bf16)
+
+    devices = 2 * owners
+    small_grads = jnp.concatenate(
+        [
+            part.reshape(devices, -1)
+            for part in (attn_gain_grad, query_gain_grad, key_gain_grad, moe_gain_grad, router_grad)
+        ],
+        axis=1,
+    )
+    small_grads = jnp.sum(
+        lax.all_to_all(
+            small_grads, ("dp", "expert"), split_axis=0, concat_axis=0, tiled=True
+        ),
+        axis=0,
+    )
+    attn_gain_grad, query_gain_grad, key_gain_grad, moe_gain_grad, router_grad = jnp.split(
+        small_grads, [rows, 2 * rows, 3 * rows, 4 * rows]
+    )
+
+    moe_term = reduce_chips(out_parts)
+    block_out = (middle + moe_term).astype(bf16)
+    expert_acts = jnp.concatenate(all_acts, axis=0)
+    gate_weight_grad = inner_product(expert_acts, jnp.concatenate(all_gate_grads, axis=0))
+    up_weight_grad = inner_product(expert_acts, jnp.concatenate(all_up_grads, axis=0))
+    down_grad = inner_product(
+        jnp.concatenate(all_hidden, axis=0), jnp.concatenate(all_out_grads, axis=0)
+    )
+    gate_weight_grad, up_weight_grad, down_grad = (
+        lax.psum_scatter(
+            gate_weight_grad.astype(bf16)[None], "dp", scatter_dimension=2, tiled=True
+        ).astype(f32),
+        lax.psum_scatter(
+            up_weight_grad.astype(bf16)[None], "dp", scatter_dimension=2, tiled=True
+        ).astype(f32),
+        lax.psum_scatter(
+            down_grad.astype(bf16)[None], "dp", scatter_dimension=1, tiled=True
+        ).astype(f32),
+    )
+    return (
+        block_out,
+        input_grad,
+        attn_gain_grad,
+        query_weight_grad,
+        key_weight_grad,
+        value_weight_grad,
+        query_gain_grad,
+        key_gain_grad,
+        output_grad,
+        moe_gain_grad,
+        router_grad.reshape(w_router.shape),
+        gate_weight_grad,
+        up_weight_grad,
+        down_grad,
+    )
+
+
 def solution(mesh):
+    body = body_dense if mesh.shape["expert"] == NZ * NY * NX else body_routed
     return jax.shard_map(
         body,
         mesh=mesh,

time: 2890 us -> 1140 us (0.39)
  waiting for transfers between devices: 2090 us -> 447 us
  blocking collectives: 311 us -> 0 us
  starting transfers between devices: 88.8 us -> 200 us
  Pallas kernels: 0 us -> 92.1 us
    reduce_scatter x7 -> x3, waiting for transfers between devices: 1440 us -> 0.01 us  [the longest x1 0.01 us: body_dense(): lax.psum_scatter(down_grad.astype(bf16)[None], 'dp', scatter_dimension=1,...]
    ppermute x0 -> x167, waiting for transfers between devices: none -> 440 us  [the longest x64 254 us: move_x(): return lax.ppermute(values, 'expert', X_PAIRS)]
    all_to_all x4 -> x3, waiting for transfers between devices: 347 us -> 6.03 us  [the longest x1 6.03 us: body_dense(): lax.all_to_all(jnp.concatenate([uses.T, router_block], axis=1), 'expert',...]
    all_gather x4 -> x0, waiting for transfers between devices: 285 us -> none  [the longest x1 73.7 us: body(): lax.all_gather(w_key, ('dp', 'expert'), axis=0, tiled=True)]
    all_gather x1 -> x0, blocking collectives: 238 us -> none  [body(): lax.all_gather(w_router, ('dp', 'expert'), axis=0, tiled=True)]
    ppermute x0 -> x167, starting transfers between devices: none -> 187 us  [the longest x64 72.5 us: move_x(): return lax.ppermute(values, 'expert', X_PAIRS)]
    pallas_call x0 -> x10, Pallas kernels: none -> 92.1 us  [the longest x8 62.7 us: apply_weight(): pl.pallas_call(kernel, out_shape=jax.ShapeDtypeStruct((tokens, width), jn...]
    dot_general x20 -> x23, matrix products: 176 us -> 91.2 us  [the longest x4 33.1 us: body_dense(): gate_pre = jnp.dot(act_rows, gate_w, preferred_element_type=f32)]
  transfers between devices with their start and end apart: 16 -> 173, of which waited for: 12 -> 69; matrix products, arithmetic and copies ran while one was open for 9% -> 21% of each run, Pallas kernels for 0% -> 8%
where the time goes in v1:
time: 1140 us
  waiting for transfers between devices  447 us (39%)
  matrix products  208 us (18%)
  starting transfers between devices  200 us (18%)
  local copies, waits for them, and re-layouts  93.1 us (8%)
  Pallas kernels  92.1 us (8%)
  other arithmetic  79 us (7%)
  between operations  18.5 us (2%)
    ppermute x64, waiting for transfers between devices, move_x(): return lax.ppermute(values, 'expert', X_PAIRS)  254 us
    ppermute x64, waiting for transfers between devices, move_y(): return lax.ppermute(values, 'expert', Y_PAIRS)  112 us
    ppermute x24, waiting for transfers between devices, move_z(): return lax.ppermute(values, 'expert', Z_PAIRS)  73.7 us
    ppermute x64, starting transfers between devices, move_x(): return lax.ppermute(values, 'expert', X_PAIRS)  72.5 us
    ppermute x64, starting transfers between devices, move_y(): return lax.ppermute(values, 'expert', Y_PAIRS)  67.5 us
    pallas_call x8, Pallas kernels, apply_weight(): pl.pallas_call(kernel, out_shape=jax.ShapeDtypeStruct((tokens, width), jn...  62.7 us
    dot_general x13, matrix products, times_transposed(): jnp.einsum('ta,ba->tb', left, right, preferred_element_type=jnp.float32)  58.9 us
    dot_general x4, matrix products, inner_product(): jnp.einsum('ta,tb->ab', left, right, preferred_element_type=jnp.float32)  57.8 us
  transfers between devices with their start and end apart: 173, of which 69 were waited for; matrix products, arithmetic and copies ran while one was open for 21% of the time, Pallas kernels for 8%

profile of v1, /device:TPU:0, one launch (start us, length us, event | category | flops | bytes accessed | tf_op | source)
XLA Modules:
  0.0 1136.7 jit_solution(9611832267900326176)
XLA Ops:
  102.0 8.0 collective-permute-done.11
  113.5 7.7 collective-permute-done.34
  149.0 21.2 %collective-permute-done.39 = bf16[128,2048]{1,0:T(8,128)(2,1)S(1)} collective-permute-done((bf16[128,2048]{1,0:T(8,128)(2,1)S(1)}, bf16[128,2048]{1,0:T(8,128)(2,1)S(1)}, u32[]{:S(2)}, u32[]{:S(2)}) %collective-permute-start.39) | collective-permute-done | bytes 524320 | tf_op jit(solution)/shard_map/ppermute | solution.py:308
  187.5 8.6 collective-permute-done.95
  198.6 12.2 %collective-permute-done.87 = bf16[192,2048]{1,0:T(8,128)(2,1)S(1)} collective-permute-done((bf16[192,2048]{1,0:T(8,128)(2,1)S(1)}, bf16[192,2048]{1,0:T(8,128)(2,1)S(1)}, u32[]{:S(2)}, u32[]{:S(2)}) %collective-permute-start.87) | collective-permute-done | bytes 786464 | tf_op jit(solution)/shard_map/ppermute | solution.py:308
  214.3 18.4 %collective-permute-done.88 = bf16[96,2048]{1,0:T(8,128)(2,1)S(1)} collective-permute-done((bf16[96,2048]{1,0:T(8,128)(2,1)S(1)}, bf16[96,2048]{1,0:T(8,128)(2,1)S(1)}, u32[]{:S(2)}, u32[]{:S(2)}) %collective-permute-start.88) | collective-permute-done | bytes 393248 | tf_op jit(solution)/shard_map/ppermute | solution.py:304
  233.5 13.4 %collective-permute-start.105 = (bf16[192,2048]{1,0:T(8,128)(2,1)S(1)}, bf16[192,2048]{1,0:T(8,128)(2,1)}, u32[]{:S(2)}, u32[]{:S(2)}) collective-permute-start(bf16[192,2048]{1,0:T(8,128)(2,1)S(1)} %collective-permute-done.95), channel_id=1, source_target_pairs={{0,4},{1,5},{2,6},{3,7},{4,8},{5,9},{6,10},{7,11},{8,12},{9,13},{1... | collective-permute-start | bytes 2359304 | tf_op jit(solution)/shard_map/ppermute | solution.py:312
  247.3 19.8 %collective-permute-done.105 = bf16[192,2048]{1,0:T(8,128)(2,1)} collective-permute-done((bf16[192,2048]{1,0:T(8,128)(2,1)S(1)}, bf16[192,2048]{1,0:T(8,128)(2,1)}, u32[]{:S(2)}, u32[]{:S(2)}) %collective-permute-start.105) | collective-permute-done | bytes 786464 | tf_op jit(solution)/shard_map/ppermute | solution.py:312
  268.7 8.9 collective-permute-done.98
  294.0 8.2 shard_map.264
  302.4 8.2 shard_map.265
  318.6 8.2 shard_map.263
  328.2 8.2 shard_map.266
  346.0 19.3 %collective-permute-done.108 = bf16[96,2048]{1,0:T(8,128)(2,1)S(1)} collective-permute-done((bf16[96,2048]{1,0:T(8,128)(2,1)S(1)}, bf16[96,2048]{1,0:T(8,128)(2,1)S(1)}, u32[]{:S(2)}, u32[]{:S(2)}) %collective-permute-start.108) | collective-permute-done | bytes 393248 | tf_op jit(solution)/shard_map/ppermute | solution.py:304
  487.6 9.5 multiply_convert_fusion.2
  503.8 9.0 multiply_convert_fusion.8
  539.9 20.9 %convert_bitcast_fusion = bf16[1,1024,2048]{2,1,0:T(8,128)(2,1)} fusion(bf16[768,2048]{1,0:T(8,128)(2,1)} %copy-done.72, bf16[768,2048]{1,0:T(8,128)(2,1)} %copy-done.71, bf16[768,2048]{1,0:T(8,128)(2,1)} %copy-done.70, bf16[768,2048]{1,0:T(8,128)(2,1)} %copy-done.73, bf16[768,1024]{1,0:T(8,128)(2,1)} %get-tuple-element.148, ...), kind=kOutput, calls=%fused_computation.109 | convolution fusion | flops 12962496512 | bytes 23068672 | tf_op jit(solution)/shard_map/ta,tb->ab/dot_general | solution.py:54
  560.8 8.5 fusion.17
  604.7 18.3 %convert_bitcast_fusion.1 = bf16[1,2048,1024]{2,1,0:T(8,128)(2,1)} fusion(bf16[3072,2048]{1,0:T(8,128)(2,1)} %get-tuple-element.255, bf16[768,1024]{1,0:T(8,128)(2,1)S(1)} %copy-done.167, bf16[768,1024]{1,0:T(8,128)(2,1)S(1)} %copy-done.166, bf16[768,1024]{1,0:T(8,128)(2,1)S(1)} %copy-done.165, bf16[768,1024]{1,0:T(8,128)(2,1)S(1)} %copy-done.163), kind=kOutput, calls=%fused_computation.110 | convolution fusion | flops 12912164864 | bytes 23068672 | tf_op jit(solution)/shard_map/ta,tb->ab/dot_general | solution.py:54
  623.0 8.1 add_convert_fusion.1
  649.2 18.2 %convert_bitcast_fusion.2 = bf16[1,2048,1024]{2,1,0:T(8,128)(2,1)} fusion(bf16[3072,2048]{1,0:T(8,128)(2,1)} %get-tuple-element.255, bf16[768,1024]{1,0:T(8,128)(2,1)S(1)} %copy-done.174, bf16[768,1024]{1,0:T(8,128)(2,1)S(1)} %copy-done.173, bf16[768,1024]{1,0:T(8,128)(2,1)S(1)} %copy-done.171, bf16[768,1024]{1,0:T(8,128)(2,1)S(1)} %copy-done.169), kind=kOutput, calls=%fused_computation.111 | convolution fusion | flops 12912164864 | bytes 23068672 | tf_op jit(solution)/shard_map/ta,tb->ab/dot_general | solution.py:54
  729.1 14.0 %collective-permute-done.91 = bf16[192,2048]{1,0:T(8,128)(2,1)S(1)} collective-permute-done((bf16[192,2048]{1,0:T(8,128)(2,1)S(1)}, bf16[192,2048]{1,0:T(8,128)(2,1)S(1)}, u32[]{:S(2)}, u32[]{:S(2)}) %collective-permute-start.91) | collective-permute-done | bytes 786464 | tf_op jit(solution)/shard_map/ppermute | solution.py:304
  747.2 26.9 %collective-permute-done.53 = bf16[192,2048]{1,0:T(8,128)(2,1)S(1)} collective-permute-done((bf16[192,2048]{1,0:T(8,128)(2,1)S(1)}, bf16[192,2048]{1,0:T(8,128)(2,1)S(1)}, u32[]{:S(2)}, u32[]{:S(2)}) %collective-permute-start.53) | collective-permute-done | bytes 786464 | tf_op jit(solution)/shard_map/ppermute | solution.py:304
  780.6 25.8 %collective-permute-done.63 = bf16[192,2048]{1,0:T(8,128)(2,1)S(1)} collective-permute-done((bf16[192,2048]{1,0:T(8,128)(2,1)S(1)}, bf16[192,2048]{1,0:T(8,128)(2,1)S(1)}, u32[]{:S(2)}, u32[]{:S(2)}) %collective-permute-start.63) | collective-permute-done | bytes 786464 | tf_op jit(solution)/shard_map/ppermute | solution.py:304
  813.6 12.1 %collective-permute-done.104 = bf16[192,2048]{1,0:T(8,128)(2,1)S(1)} collective-permute-done((bf16[192,2048]{1,0:T(8,128)(2,1)S(1)}, bf16[192,2048]{1,0:T(8,128)(2,1)S(1)}, u32[]{:S(2)}, u32[]{:S(2)}) %collective-permute-start.104) | collective-permute-done | bytes 786464 | tf_op jit(solution)/shard_map/ppermute | solution.py:312
  826.3 9.0 collective-permute-done.73
  837.7 8.2 collective-permute-done.66
  932.4 22.4 %shard_map.271 = (bf16[192,2048]{1,0:T(8,128)(2,1)S(1)}, bf16[192,2048]{1,0:T(8,128)(2,1)S(1)}, bf16[192,2048]{1,0:T(8,128)(2,1)S(1)}, bf16[192,2048]{1,0:T(8,12...) custom-call(s32[4]{0:T(128)S(1)} %copy-done.17, ...), custom_call_target="tpu_custom_call" | custom-call | flops 4831838208 | bytes 18874368 | tf_op jit(solution)/shard_map/pallas_call | solution.py:488
  997.2 13.1 %collective-permute-done.149 = bf16[64,2048]{1,0:T(8,128)(2,1)S(1)} collective-permute-done((bf16[64,2048]{1,0:T(8,128)(2,1)S(1)}, bf16[64,2048]{1,0:T(8,128)(2,1)S(1)}, u32[]{:S(2)}, u32[]{:S(2)}) %collective-permute-start.149) | collective-permute-done | bytes 262176 | tf_op jit(solution)/shard_map/ppermute | solution.py:304
  1015.1 15.3 %collective-permute-done.128 = bf16[192,2048]{1,0:T(8,128)(2,1)S(1)} collective-permute-done((bf16[192,2048]{1,0:T(8,128)(2,1)S(1)}, bf16[192,2048]{1,0:T(8,128)(2,1)S(1)}, u32[]{:S(2)}, u32[]{:S(2)}) %collective-permute-start.128) | collective-permute-done | bytes 786464 | tf_op jit(solution)/shard_map/ppermute | solution.py:304
  1036.9 14.0 %collective-permute-done.133 = bf16[192,2048]{1,0:T(8,128)(2,1)S(1)} collective-permute-done((bf16[192,2048]{1,0:T(8,128)(2,1)S(1)}, bf16[192,2048]{1,0:T(8,128)(2,1)S(1)}, u32[]{:S(2)}, u32[]{:S(2)}) %collective-permute-start.133) | collective-permute-done | bytes 786464 | tf_op jit(solution)/shard_map/ppermute | solution.py:304
  1065.2 8.2 collective-permute-done.138
  (1019 shorter events, 686.2 us)
Async XLA Ops:
  10.6 39.3 %collective-permute-start.4 = (bf16[128,2048]{1,0:T(8,128)(2,1)}, bf16[128,2048]{1,0:T(8,128)(2,1)}, u32[]{:S(2)}, u32[]{:S(2)}) collective-permute-start(bf16[128,2048]{1,0:T(8,128)(2,1)} %constant_dynamic-update-slice_fusion), channel_id=1, source_target_pairs={{0,4},{1,5},{2,6},{3,7},{4,8},{5,9},{6,10},{7,11},{8,12},{9,13},{1... | collective-permute-start | bytes 1572872 | tf_op jit(solution)/shard_map/ppermute | solution.py:312
  29.3 1088.1 %reduce-scatter.8.cloned.1.call-start = ((), (), s32[]{:S(2)}) async-start(), calls=%async_computation.8 | async-start | bytes 6291456 | tf_op jit(solution)/shard_map/reduce_scatter | solution.py:760
  133.7 38.6 %collective-permute-start.85 = (bf16[192,2048]{1,0:T(8,128)(2,1)S(1)}, bf16[192,2048]{1,0:T(8,128)(2,1)S(1)}, u32[]{:S(2)}, u32[]{:S(2)}) collective-permute-start(bf16[192,2048]{1,0:T(8,128)(2,1)S(1)} %get-tuple-element.137), channel_id=1, source_target_pairs={{0,4},{1,5},{2,6},{3,7},{4,8},{5,9},{6,10},{7,11},{8,12},{9,13},{1... | collective-permute-start | bytes 2359304 | tf_op jit(solution)/shard_map/ppermute | solution.py:312
  134.4 40.2 %collective-permute-start.115 = (bf16[192,2048]{1,0:T(8,128)(2,1)S(1)}, bf16[192,2048]{1,0:T(8,128)(2,1)S(1)}, u32[]{:S(2)}, u32[]{:S(2)}) collective-permute-start(bf16[192,2048]{1,0:T(8,128)(2,1)S(1)} %get-tuple-element.137), channel_id=1, source_target_pairs={{0,1},{1,0},{2,3},{3,2},{4,5},{5,4},{6,7},{7,6},{8,9},{9,8},{10,11... | collective-permute-start | bytes 2359304 | tf_op jit(solution)/shard_map/ppermute | solution.py:304
  135.0 39.0 %collective-permute-start.116 = (bf16[192,2048]{1,0:T(8,128)(2,1)S(1)}, bf16[192,2048]{1,0:T(8,128)(2,1)S(1)}, u32[]{:S(2)}, u32[]{:S(2)}) collective-permute-start(bf16[192,2048]{1,0:T(8,128)(2,1)S(1)} %get-tuple-element.137), channel_id=1, source_target_pairs={{0,2},{1,3},{2,0},{3,1},{4,6},{5,7},{6,4},{7,5},{8,10},{9,11},{10,... | collective-permute-start | bytes 2359304 | tf_op jit(solution)/shard_map/ppermute | solution.py:308
  196.1 37.1 %collective-permute-start.96 = (bf16[192,2048]{1,0:T(8,128)(2,1)S(1)}, bf16[192,2048]{1,0:T(8,128)(2,1)S(1)}, u32[]{:S(2)}, u32[]{:S(2)}) collective-permute-start(bf16[192,2048]{1,0:T(8,128)(2,1)S(1)} %collective-permute-done.95), channel_id=1, source_target_pairs={{0,1},{1,0},{2,3},{3,2},{4,5},{5,4},{6,7},{7,6},{8,9},{9,8},{10,11... | collective-permute-start | bytes 2359304 | tf_op jit(solution)/shard_map/ppermute | solution.py:304
  196.9 36.7 %collective-permute-start.97 = (bf16[192,2048]{1,0:T(8,128)(2,1)S(1)}, bf16[192,2048]{1,0:T(8,128)(2,1)S(1)}, u32[]{:S(2)}, u32[]{:S(2)}) collective-permute-start(bf16[192,2048]{1,0:T(8,128)(2,1)S(1)} %collective-permute-done.95), channel_id=1, source_target_pairs={{0,2},{1,3},{2,0},{3,1},{4,6},{5,7},{6,4},{7,5},{8,10},{9,11},{10,... | collective-permute-start | bytes 2359304 | tf_op jit(solution)/shard_map/ppermute | solution.py:308
  210.9 76.5 %collective-permute-start.42 = (bf16[4,128,2048]{2,1,0:T(8,128)(2,1)S(1)}, bf16[4,128,2048]{2,1,0:T(8,128)(2,1)S(1)}, u32[]{:S(2)}, u32[]{:S(2)}) collective-permute-start(bf16[4,128,2048]{2,1,0:T(8,128)(2,1)S(1)} %pad_maximum_fusion.4.refs_0_), channel_id=1, source_target_pairs={{0,16},{16,0},{1,17},{17,1},{2,18},{18,2},{3,19},{19,3},{4,20},{20... | collective-permute-start | bytes 6291464 | tf_op jit(solution)/shard_map/ppermute | solution.py:316
  232.7 55.3 %collective-permute-start.43 = (bf16[4,128,2048]{2,1,0:T(8,128)(2,1)S(1)}, bf16[4,128,2048]{2,1,0:T(8,128)(2,1)S(1)}, u32[]{:S(2)}, u32[]{:S(2)}) collective-permute-start(bf16[4,128,2048]{2,1,0:T(8,128)(2,1)S(1)} %pad_maximum_fusion.5.refs_1_), channel_id=1, source_target_pairs={{0,16},{16,0},{1,17},{17,1},{2,18},{18,2},{3,19},{19,3},{4,20},{20... | collective-permute-start | bytes 6291464 | tf_op jit(solution)/shard_map/ppermute | solution.py:316
  233.0 55.0 %collective-permute-start.44 = (bf16[4,128,2048]{2,1,0:T(8,128)(2,1)S(1)}, bf16[4,128,2048]{2,1,0:T(8,128)(2,1)S(1)}, u32[]{:S(2)}, u32[]{:S(2)}) collective-permute-start(bf16[4,128,2048]{2,1,0:T(8,128)(2,1)S(1)} %pad_maximum_fusion.6.refs_2_), channel_id=1, source_target_pairs={{0,16},{16,0},{1,17},{17,1},{2,18},{18,2},{3,19},{19,3},{4,20},{20... | collective-permute-start | bytes 6291464 | tf_op jit(solution)/shard_map/ppermute | solution.py:316
  233.2 55.3 %collective-permute-start.45 = (bf16[4,128,2048]{2,1,0:T(8,128)(2,1)S(1)}, bf16[4,128,2048]{2,1,0:T(8,128)(2,1)S(1)}, u32[]{:S(2)}, u32[]{:S(2)}) collective-permute-start(bf16[4,128,2048]{2,1,0:T(8,128)(2,1)S(1)} %pad_maximum_fusion.7.refs_3_), channel_id=1, source_target_pairs={{0,16},{16,0},{1,17},{17,1},{2,18},{18,2},{3,19},{19,3},{4,20},{20... | collective-permute-start | bytes 6291464 | tf_op jit(solution)/shard_map/ppermute | solution.py:316
  292.3 49.8 %collective-permute-start.106 = (bf16[192,2048]{1,0:T(8,128)(2,1)}, bf16[192,2048]{1,0:T(8,128)(2,1)}, u32[]{:S(2)}, u32[]{:S(2)}) collective-permute-start(bf16[192,2048]{1,0:T(8,128)(2,1)} %collective-permute-done.105), channel_id=1, source_target_pairs={{0,1},{1,0},{2,3},{3,2},{4,5},{5,4},{6,7},{7,6},{8,9},{9,8},{10,11... | collective-permute-start | bytes 2359304 | tf_op jit(solution)/shard_map/ppermute | solution.py:304
  571.6 98.4 %all-to-all-start.1 = ((f32[16,1,192]{2,1,0:T(1,128)}), f32[16,1,192]{2,1,0:T(1,128)S(1)}, u32[]{:S(2)}, u32[]{:S(2)}) async-start(f32[16,1,192]{2,1,0:T(1,128)} %all_to_all.25), calls=%async_computation.1 | async-start | bytes 32768 | tf_op jit(solution)/shard_map/all_to_all | solution.py:653
  575.0 546.5 %reduce-scatter.6.cloned.1.call-start = ((), (), s32[]{:S(2)}) async-start(), calls=%async_computation.7 | async-start | bytes 6291456 | tf_op jit(solution)/shard_map/reduce_scatter | solution.py:757
  586.2 85.6 %collective-permute-start.90 = (bf16[96,2048]{1,0:T(8,128)(2,1)}, bf16[96,2048]{1,0:T(8,128)(2,1)}, u32[]{:S(2)}, u32[]{:S(2)}) collective-permute-start(bf16[96,2048]{1,0:T(8,128)(2,1)} %get-tuple-element.155), channel_id=1, source_target_pairs={{0,2},{1,3},{2,0},{3,1},{4,6},{5,7},{6,4},{7,5},{8,10},{9,11},{10,... | collective-permute-start | bytes 1179656 | tf_op jit(solution)/shard_map/ppermute | solution.py:308
  588.0 85.4 %collective-permute-start.92 = (bf16[96,2048]{1,0:T(8,128)(2,1)}, bf16[96,2048]{1,0:T(8,128)(2,1)}, u32[]{:S(2)}, u32[]{:S(2)}) collective-permute-start(bf16[96,2048]{1,0:T(8,128)(2,1)} %get-tuple-element.154), channel_id=1, source_target_pairs={{0,1},{1,0},{2,3},{3,2},{4,5},{5,4},{6,7},{7,6},{8,9},{9,8},{10,11... | collective-permute-start | bytes 1179656 | tf_op jit(solution)/shard_map/ppermute | solution.py:304
  597.9 79.1 %collective-permute-start.100 = (bf16[96,2048]{1,0:T(8,128)(2,1)}, bf16[96,2048]{1,0:T(8,128)(2,1)}, u32[]{:S(2)}, u32[]{:S(2)}) collective-permute-start(bf16[96,2048]{1,0:T(8,128)(2,1)} %get-tuple-element.161), channel_id=1, source_target_pairs={{0,2},{1,3},{2,0},{3,1},{4,6},{5,7},{6,4},{7,5},{8,10},{9,11},{10,... | collective-permute-start | bytes 1179656 | tf_op jit(solution)/shard_map/ppermute | solution.py:308
  598.4 79.3 %collective-permute-start.102 = (bf16[96,2048]{1,0:T(8,128)(2,1)}, bf16[96,2048]{1,0:T(8,128)(2,1)}, u32[]{:S(2)}, u32[]{:S(2)}) collective-permute-start(bf16[96,2048]{1,0:T(8,128)(2,1)} %get-tuple-element.160), channel_id=1, source_target_pairs={{0,1},{1,0},{2,3},{3,2},{4,5},{5,4},{6,7},{7,6},{8,9},{9,8},{10,11... | collective-permute-start | bytes 1179656 | tf_op jit(solution)/shard_map/ppermute | solution.py:304
  623.0 502.7 %reduce-scatter.4.cloned.1.call-start = ((), (), s32[]{:S(2)}) async-start(), calls=%async_computation.6 | async-start | bytes 6291456 | tf_op jit(solution)/shard_map/reduce_scatter | solution.py:754
  632.5 48.2 %collective-permute-start.110 = (bf16[96,2048]{1,0:T(8,128)(2,1)}, bf16[96,2048]{1,0:T(8,128)(2,1)}, u32[]{:S(2)}, u32[]{:S(2)}) collective-permute-start(bf16[96,2048]{1,0:T(8,128)(2,1)} %get-tuple-element.167), channel_id=1, source_target_pairs={{0,2},{1,3},{2,0},{3,1},{4,6},{5,7},{6,4},{7,5},{8,10},{9,11},{10,... | collective-permute-start | bytes 1179656 | tf_op jit(solution)/shard_map/ppermute | solution.py:308
  717.8 58.6 %collective-permute-start.101 = (bf16[192,2048]{1,0:T(8,128)(2,1)S(1)}, bf16[192,2048]{1,0:T(8,128)(2,1)S(1)}, u32[]{:S(2)}, u32[]{:S(2)}) collective-permute-start(bf16[192,2048]{1,0:T(8,128)(2,1)S(1)} %pad_maximum_fusion.18), channel_id=1, source_target_pairs={{0,1},{1,0},{2,3},{3,2},{4,5},{5,4},{6,7},{7,6},{8,9},{9,8},{10,11... | collective-permute-start | bytes 2359304 | tf_op jit(solution)/shard_map/ppermute | solution.py:304
  719.8 57.6 %collective-permute-start.103 = (bf16[192,2048]{1,0:T(8,128)(2,1)S(1)}, bf16[192,2048]{1,0:T(8,128)(2,1)S(1)}, u32[]{:S(2)}, u32[]{:S(2)}) collective-permute-start(bf16[192,2048]{1,0:T(8,128)(2,1)S(1)} %pad_maximum_fusion.19), channel_id=1, source_target_pairs={{0,2},{1,3},{2,0},{3,1},{4,6},{5,7},{6,4},{7,5},{8,10},{9,11},{10,... | collective-permute-start | bytes 2359304 | tf_op jit(solution)/shard_map/ppermute | solution.py:308
  726.3 47.8 %collective-permute-start.53 = (bf16[192,2048]{1,0:T(8,128)(2,1)S(1)}, bf16[192,2048]{1,0:T(8,128)(2,1)S(1)}, u32[]{:S(2)}, u32[]{:S(2)}) collective-permute-start(bf16[192,2048]{1,0:T(8,128)(2,1)S(1)} %pad_maximum_fusion.8), channel_id=1, source_target_pairs={{0,1},{1,0},{2,3},{3,2},{4,5},{5,4},{6,7},{7,6},{8,9},{9,8},{10,11... | collective-permute-start | bytes 2359304 | tf_op jit(solution)/shard_map/ppermute | solution.py:304
  774.1 37.4 %collective-permute-start.111 = (bf16[192,2048]{1,0:T(8,128)(2,1)S(1)}, bf16[192,2048]{1,0:T(8,128)(2,1)S(1)}, u32[]{:S(2)}, u32[]{:S(2)}) collective-permute-start(bf16[192,2048]{1,0:T(8,128)(2,1)S(1)} %pad_maximum_fusion.20), channel_id=1, source_target_pairs={{0,1},{1,0},{2,3},{3,2},{4,5},{5,4},{6,7},{7,6},{8,9},{9,8},{10,11... | collective-permute-start | bytes 2359304 | tf_op jit(solution)/shard_map/ppermute | solution.py:304
  808.9 38.4 %collective-permute-start.120 = (bf16[192,2048]{1,0:T(8,128)(2,1)S(1)}, bf16[192,2048]{1,0:T(8,128)(2,1)S(1)}, u32[]{:S(2)}, u32[]{:S(2)}) collective-permute-start(bf16[192,2048]{1,0:T(8,128)(2,1)S(1)} %pad_maximum_fusion.22), channel_id=1, source_target_pairs={{0,1},{1,0},{2,3},{3,2},{4,5},{5,4},{6,7},{7,6},{8,9},{9,8},{10,11... | collective-permute-start | bytes 2359304 | tf_op jit(solution)/shard_map/ppermute | solution.py:304
  837.7 90.6 %collective-permute-start.123 = (bf16[192,1024]{1,0:T(8,128)(2,1)}, bf16[192,1024]{1,0:T(8,128)(2,1)}, u32[]{:S(2)}, u32[]{:S(2)}) collective-permute-start(bf16[192,1024]{1,0:T(8,128)(2,1)} %get-tuple-element.253), channel_id=1, source_target_pairs={{0,16},{16,0},{1,17},{17,1},{2,18},{18,2},{3,19},{19,3},{4,20},{20... | collective-permute-start | bytes 1179656 | tf_op jit(solution)/shard_map/ppermute | solution.py:316
  845.9 70.2 %collective-permute-start.146 = (bf16[192,1024]{1,0:T(8,128)(2,1)}, bf16[192,1024]{1,0:T(8,128)(2,1)}, u32[]{:S(2)}, u32[]{:S(2)}) collective-permute-start(bf16[192,1024]{1,0:T(8,128)(2,1)} %get-tuple-element.243), channel_id=1, source_target_pairs={{0,16},{16,0},{1,17},{17,1},{2,18},{18,2},{3,19},{19,3},{4,20},{20... | collective-permute-start | bytes 1179656 | tf_op jit(solution)/shard_map/ppermute | solution.py:316
  857.9 58.5 %collective-permute-start.147 = (bf16[192,2048]{1,0:T(8,128)(2,1)S(1)}, bf16[192,2048]{1,0:T(8,128)(2,1)}, u32[]{:S(2)}, u32[]{:S(2)}) collective-permute-start(bf16[192,2048]{1,0:T(8,128)(2,1)S(1)} %fusion.184.grads.refs_0_), channel_id=1, source_target_pairs={{0,16},{16,0},{1,17},{17,1},{2,18},{18,2},{3,19},{19,3},{4,20},{20... | collective-permute-start | bytes 2359304 | tf_op jit(solution)/shard_map/ppermute | solution.py:316
  876.2 53.6 %collective-permute-start.125 = (bf16[192,2048]{1,0:T(8,128)(2,1)S(1)}, bf16[192,2048]{1,0:T(8,128)(2,1)}, u32[]{:S(2)}, u32[]{:S(2)}) collective-permute-start(bf16[192,2048]{1,0:T(8,128)(2,1)S(1)} %multiply_convert_fusion.13.grads.refs_2_), channel_id=1, source_target_pairs={{0,16},{16,0},{1,17},{17,1},{2,18},{18,2},{3,19},{19,3},{4,20},{20... | collective-permute-start | bytes 2359304 | tf_op jit(solution)/shard_map/ppermute | solution.py:316
  878.0 52.3 %collective-permute-start.124 = (bf16[192,2048]{1,0:T(8,128)(2,1)S(1)}, bf16[192,2048]{1,0:T(8,128)(2,1)}, u32[]{:S(2)}, u32[]{:S(2)}) collective-permute-start(bf16[192,2048]{1,0:T(8,128)(2,1)S(1)} %multiply_convert_fusion.14.grads.refs_0_), channel_id=1, source_target_pairs={{0,16},{16,0},{1,17},{17,1},{2,18},{18,2},{3,19},{19,3},{4,20},{20... | collective-permute-start | bytes 2359304 | tf_op jit(solution)/shard_map/ppermute | solution.py:316
  912.1 189.7 %all-to-all-start.2 = ((f32[32,1,1280]{2,1,0:T(1,128)}), f32[32,1,1280]{2,1,0:T(1,128)}, u32[]{:S(2)}, u32[]{:S(2)}) async-start(f32[32,1,1280]{2,1,0:T(1,128)} %copy.114), calls=%async_computation.2 | async-start | bytes 327680 | tf_op jit(solution)/shard_map/all_to_all | solution.py:736
  996.3 36.9 %collective-permute-start.154 = (bf16[64,2048]{1,0:T(8,128)(2,1)S(1)}, bf16[64,2048]{1,0:T(8,128)(2,1)S(1)}, u32[]{:S(2)}, u32[]{:S(2)}) collective-permute-start(bf16[64,2048]{1,0:T(8,128)(2,1)S(1)} %pad_maximum_fusion.34), channel_id=1, source_target_pairs={{0,1},{1,0},{2,3},{3,2},{4,5},{5,4},{6,7},{7,6},{8,9},{9,8},{10,11... | collective-permute-start | bytes 786440 | tf_op jit(solution)/shard_map/ppermute | solution.py:304
  (316 other events, 6424.0 us)
Sparse Core Ops, SparseCore 0:
  569.5 9.0 reduce-scatter.7
  623.1 12.7 reduce-scatter.5
  670.0 12.0 reduce-scatter.3

commit v2 on v1

--- a/solution.py
+++ b/solution.py
@@ -1,4 +1,5 @@
 import functools
+import itertools
 
 import jax
 import jax.numpy as jnp
@@ -287,6 +288,9 @@
 
 NZ, NY, NX = 4, 2, 2
 VMEM_LIMIT = 48 * 1024 * 1024
+EXPERT_VMEM = 60 * 1024 * 1024
+WINDOW = 5
+UPSTREAM_AT = 1
 
 
 def chip(z, y, x):
@@ -318,6 +322,27 @@
 
 def split_row(rows):
     return (rows // 2 + 15) // 16 * 16
+
+
+def after(values, *earlier):
+    return lax.optimization_barrier((values, *earlier))[0]
+
+
+class Line:
+    def __init__(self):
+        self.sent, self.held = [], []
+
+    def hold(self, *earlier):
+        self.held += earlier
+
+    def send(self, move, values):
+        if len(self.sent) >= WINDOW:
+            self.held.append(self.sent[-WINDOW])
+        if self.held:
+            values = after(values, *self.held)
+            self.held = []
+        self.sent.append(move(values))
+        return self.sent[-1]
 
 
 def gather_z(block):
@@ -343,104 +368,123 @@
     return left.astype(jnp.float32) + right.astype(jnp.float32)
 
 
-def reduce_plane(parts):
-    own, for_x, for_y, for_across = parts
-    low = own.dtype
-    cut = split_row(own.shape[0])
-    by_x = move_x(for_across[:cut])
-    by_y = move_y(for_across[cut:])
-    for_y = jnp.concatenate([add_f32(for_y[:cut], by_x).astype(low), for_y[cut:]], axis=0)
-    for_x = jnp.concatenate([for_x[:cut], add_f32(for_x[cut:], by_y).astype(low)], axis=0)
-    return add_f32(own, move_x(for_x)) + move_y(for_y).astype(jnp.float32)
-
-
-def reduce_z(ring):
-    total = ring[1].astype(jnp.bfloat16)
-    for step in range(2, NZ):
-        total = add_f32(move_z(total), ring[step]).astype(jnp.bfloat16)
-    return add_f32(move_z(total), ring[0])
-
-
-def reduce_chips(parts):
-    return reduce_z([reduce_plane(part) for part in parts])
+class Reduce:
+    def __init__(self, line):
+        self.line, self.planes, self.open, self.steps = line, {}, None, 0
+        self.total = None
+
+    def add(self, step, parts):
+        by_x = self.line.send(move_x, parts[3])
+        by_y = self.line.send(move_y, parts[4])
+        self.finish_plane()
+        self.open = (step, parts, by_x, by_y)
+        self.push()
+
+    def ways(self):
+        return self.open[2:]
+
+    def finish_plane(self):
+        if self.open is None:
+            return
+        step, (own, for_x, for_y, *_), by_x, by_y = self.open
+        low = own.dtype
+        cut = by_x.shape[0]
+        for_y = jnp.concatenate([add_f32(for_y[:cut], by_x).astype(low), for_y[cut:]], axis=0)
+        for_x = jnp.concatenate([for_x[:cut], add_f32(for_x[cut:], by_y).astype(low)], axis=0)
+        from_x = self.line.send(move_x, for_x)
+        from_y = self.line.send(move_y, for_y)
+        self.planes[step] = add_f32(own, from_x) + from_y.astype(jnp.float32)
+        self.open = None
+
+    def push(self):
+        while self.steps + 1 < NZ and self.steps + 1 in self.planes:
+            self.steps += 1
+            total = self.planes[self.steps]
+            if self.total is not None:
+                total = add_f32(self.total, total)
+            self.total = self.line.send(move_z, total.astype(jnp.bfloat16))
+
+    def result(self):
+        self.finish_plane()
+        self.push()
+        return add_f32(self.total, self.planes[0])
 
 
 def place_of(position, k):
     return (position[2] ^ (k >> 1)) * NX + (position[3] ^ (k & 1))
 
 
-def chunk_copies(position, pieces, rows, slot, held, sems, chunk):
+def weight_copies(position, pieces, rows, slot, held, sems, other):
     out = []
-    for k in range(NY * NX):
-        place = pl.multiple_of(place_of(position, k) * rows, rows)
-        out.append(
-            pltpu.make_async_copy(
-                pieces[chunk].at[k, pl.ds(slot * rows, rows)],
-                held.at[chunk, pl.ds(place, rows)],
-                sems.at[chunk, k],
+    for step in range(NZ):
+        z_of = (position[1] + NZ - step) % NZ
+        for k in range(NY * NX):
+            place = pl.multiple_of((z_of * NY * NX + place_of(position, k)) * rows, rows)
+            out.append(
+                pltpu.make_async_copy(
+                    pieces[other * NZ + step].at[k, pl.ds(slot * rows, rows)],
+                    held.at[other, pl.ds(place, rows)],
+                    sems.at[other * NZ + step, k],
+                )
             )
-        )
     return out
-
-
-def chunk_base(position, rows, chunk):
-    other, step = chunk // NZ, chunk % NZ
-    half = position[0] ^ other
-    z_of = (position[1] + NZ - step) % NZ
-    span = NY * NX * rows
-    return pl.multiple_of((half * NZ + z_of) * span, span)
 
 
 def apply_kernel(position, acts, *refs, rows, slot, tile):
     pieces, (out, held, sems) = refs[: 2 * NZ], refs[2 * NZ :]
-    for chunk in range(2 * NZ):
-        for copy in chunk_copies(position, pieces, rows, slot, held, sems, chunk):
+    for other in range(2):
+        for copy in weight_copies(position, pieces, rows, slot, held, sems, other):
             copy.start()
-    span = NY * NX * rows
-    for chunk in range(2 * NZ):
-        for copy in chunk_copies(position, pieces, rows, slot, held, sems, chunk):
+    span = held.shape[1]
+    for other in range(2):
+        for copy in weight_copies(position, pieces, rows, slot, held, sems, other):
             copy.wait()
-        left = acts[:, pl.ds(chunk_base(position, rows, chunk), span)]
+        left = acts[:, pl.ds(pl.multiple_of((position[0] ^ other) * span, span), span)]
 
         @pl.loop(0, out.shape[1] // tile)
         def _(i):
             columns = pl.ds(pl.multiple_of(i * tile, tile), tile)
-            part = jnp.dot(left, held[chunk, :, columns], preferred_element_type=jnp.float32)
-            if chunk == 0:
+            part = jnp.dot(left, held[other, :, columns], preferred_element_type=jnp.float32)
+            if other == 0:
                 out[:, columns] = part
             else:
                 out[:, columns] += part
 
 
-def apply_back_kernel(position, grads, *refs, rows, slot):
+def apply_back_kernel(position, grads, *refs, rows, slot, tile):
     pieces, (out, held, sems) = refs[: 2 * NZ], refs[2 * NZ :]
-    for chunk in range(2 * NZ):
-        for copy in chunk_copies(position, pieces, rows, slot, held, sems, chunk):
+    for other in range(2):
+        for copy in weight_copies(position, pieces, rows, slot, held, sems, other):
             copy.start()
-    span = NY * NX * rows
-    for chunk in range(2 * NZ):
-        for copy in chunk_copies(position, pieces, rows, slot, held, sems, chunk):
+    span = held.shape[1]
+    for other in range(2):
+        for copy in weight_copies(position, pieces, rows, slot, held, sems, other):
             copy.wait()
-        out[:, pl.ds(chunk_base(position, rows, chunk), span)] = lax.dot_general(
-            grads[...], held[chunk], (((1,), (1,)), ((), ())), preferred_element_type=jnp.float32
-        )
+
+        @pl.loop(0, span // tile)
+        def _(i):
+            lines = pl.ds(pl.multiple_of(i * tile, tile), tile)
+            low = pl.multiple_of((position[0] ^ other) * span + i * tile, tile)
+            out[:, pl.ds(low, tile)] = lax.dot_general(
+                grads[...],
+                held[other, lines, :],
+                (((1,), (1,)), ((), ())),
+                preferred_element_type=jnp.float32,
+            )
 
 
 def apply_weight(position, values, pieces, rows, slot, back=False):
     tokens, width = values.shape
-    kernel = (
-        functools.partial(apply_back_kernel, rows=rows, slot=slot)
-        if back
-        else functools.partial(apply_kernel, rows=rows, slot=slot, tile=512)
-    )
     return pl.pallas_call(
-        kernel,
+        functools.partial(
+            apply_back_kernel if back else apply_kernel, rows=rows, slot=slot, tile=512
+        ),
         out_shape=jax.ShapeDtypeStruct((tokens, width), jnp.float32),
         in_specs=[pl.BlockSpec(memory_space=pltpu.SMEM), pl.BlockSpec(memory_space=pltpu.VMEM)]
         + [pl.BlockSpec(memory_space=pl.ANY)] * len(pieces),
         out_specs=pl.BlockSpec(memory_space=pltpu.VMEM),
         scratch_shapes=[
-            pltpu.VMEM((2 * NZ, NY * NX * rows, width), jnp.bfloat16),
+            pltpu.VMEM((2, width // 2, width), jnp.bfloat16),
             pltpu.SemaphoreType.DMA((2 * NZ, NY * NX)),
         ],
         compiler_params=pltpu.CompilerParams(vmem_limit_bytes=VMEM_LIMIT),
@@ -452,63 +496,155 @@
     )(position, values, *pieces)
 
 
-def weight_grad_kernel(position, own_left, other_left, *refs, rows, count, tile):
+def weight_grad_kernel(position, own_left, other_left, *refs, rows, count, tile, step):
     grads, outs, stage = refs[: 2 * count], refs[2 * count : -1], refs[-1]
     span = NY * NX * rows
-    for step in range(NZ):
-        z_of = (position[1] + NZ - step) % NZ
-        columns = pl.ds(pl.multiple_of(z_of * span, span), span)
-        own, other = own_left[:, columns], other_left[:, columns]
-        for i in range(count):
-
-            @pl.loop(0, grads[0].shape[1] // tile)
-            def _(j):
-                part = pl.ds(pl.multiple_of(j * tile, tile), tile)
-                product = lax.dot_general(
-                    own,
-                    grads[2 * i][:, part],
-                    (((0,), (0,)), ((), ())),
-                    preferred_element_type=jnp.float32,
-                ) + lax.dot_general(
-                    other,
-                    grads[2 * i + 1][:, part],
-                    (((0,), (0,)), ((), ())),
-                    preferred_element_type=jnp.float32,
-                )
-                stage[...] = product.astype(stage.dtype)
-                for k in range(NY * NX):
-                    place = pl.multiple_of(place_of(position, k) * rows, rows)
-                    outs[step * NY * NX + k][pl.ds(i * rows, rows), part] = stage[pl.ds(place, rows), :]
-
-
-def weight_grad_parts(position, own_left, other_left, grads, rows):
+    z_of = (position[1] + NZ - step) % NZ
+    lines = pl.ds(pl.multiple_of(z_of * span, span), span)
+    own, other = own_left[lines, :], other_left[lines, :]
+    for i in range(count):
+
+        @pl.loop(0, grads[0].shape[1] // tile)
+        def _(j):
+            part = pl.ds(pl.multiple_of(j * tile, tile), tile)
+            product = jnp.dot(
+                own, grads[2 * i][:, part], preferred_element_type=jnp.float32
+            ) + jnp.dot(other, grads[2 * i + 1][:, part], preferred_element_type=jnp.float32)
+            stage[...] = product.astype(stage.dtype)
+            for k in range(NY * NX):
+                place = pl.multiple_of(place_of(position, k) * rows, rows)
+                outs[k][pl.ds(i * rows, rows), part] = stage[pl.ds(place, rows), :]
+
+
+def weight_grad_parts(position, own_left, other_left, grads, rows, step):
     count, width = len(grads) // 2, grads[0].shape[1]
-    tokens, tile = own_left.shape[0], 512
+    tokens, tile = own_left.shape[1], 512
     block = jax.ShapeDtypeStruct((count * rows, width), jnp.bfloat16)
-    outs = pl.pallas_call(
-        functools.partial(weight_grad_kernel, rows=rows, count=count, tile=tile),
-        out_shape=[block] * (NZ * NY * NX),
+    return pl.pallas_call(
+        functools.partial(weight_grad_kernel, rows=rows, count=count, tile=tile, step=step),
+        out_shape=[block] * (NY * NX),
         in_specs=[pl.BlockSpec(memory_space=pltpu.SMEM)]
         + [pl.BlockSpec(memory_space=pltpu.VMEM)] * (2 + len(grads)),
-        out_specs=[pl.BlockSpec(memory_space=pltpu.VMEM)] * (NZ * NY * NX),
+        out_specs=[pl.BlockSpec(memory_space=pltpu.VMEM)] * (NY * NX),
         scratch_shapes=[pltpu.VMEM((NY * NX * rows, tile), jnp.bfloat16)],
         compiler_params=pltpu.CompilerParams(vmem_limit_bytes=VMEM_LIMIT),
         cost_estimate=pl.CostEstimate(
-            flops=4 * count * tokens * NZ * NY * NX * rows * width,
-            bytes_accessed=2 * count * NZ * NY * NX * rows * width + 4 * tokens * width * (count + 1),
+            flops=4 * count * tokens * NY * NX * rows * width,
+            bytes_accessed=2 * count * NY * NX * rows * width + 4 * tokens * width * (count + 1),
             transcendentals=0,
         ),
     )(position, own_left, other_left, *grads)
-    return [outs[s * NY * NX : (s + 1) * NY * NX] for s in range(NZ)]
+
+
+def column_grad_kernel(position, *refs):
+    parts = (len(refs) - 2) // 2
+    acts, grads, outs = refs[:parts], refs[parts:-2], refs[-2:]
+    half = outs[0].shape[1]
+    turned = [act[...].T for act in acts]
+    for side, out in enumerate(outs):
+        columns = pl.ds(pl.multiple_of((position[0] ^ side) * half, half), half)
+        total = None
+        for act, grad in zip(turned, grads, strict=True):
+            more = jnp.dot(act, grad[:, columns], preferred_element_type=jnp.float32)
+            total = more if total is None else total + more
+        out[...] = total.astype(out.dtype)
+
+
+def column_grads(position, acts, grads):
+    parts = len(acts)
+    count, width = acts[0].shape
+    units = grads[0].shape[1]
+    tile = 256
+    whole = pl.BlockSpec((count, units), lambda i: (0, 0), pipeline_mode=pl.Buffered(1))
+    out = pl.BlockSpec((tile, units // 2), lambda i: (i, 0))
+    return pl.pallas_call(
+        column_grad_kernel,
+        grid=(width // tile,),
+        out_shape=[jax.ShapeDtypeStruct((width, units // 2), t) for t in (jnp.float32, jnp.bfloat16)],
+        in_specs=[pl.BlockSpec(memory_space=pltpu.SMEM)]
+        + [pl.BlockSpec((count, tile), lambda i: (0, i))] * parts
+        + [whole] * parts,
+        out_specs=[out] * 2,
+        compiler_params=pltpu.CompilerParams(vmem_limit_bytes=EXPERT_VMEM),
+        cost_estimate=pl.CostEstimate(
+            flops=2 * parts * count * width * units,
+            bytes_accessed=2 * parts * count * (width + units) + 3 * width * units,
+            transcendentals=0,
+        ),
+    )(position, *acts, *grads)
+
+
+def down_grad_kernel(position, *refs):
+    parts = (len(refs) - 3) // 2
+    hiddens, grads, (own, other, turned) = refs[:parts], refs[parts:-3], refs[-3:]
+    tile = 512
+    for s, hidden in enumerate(hiddens):
+        turned[s] = hidden[...].T
+
+    def part_of(j):
+        columns = pl.ds(pl.multiple_of(j * tile, tile), tile)
+        total = None
+        for s, grad in enumerate(grads):
+            more = jnp.dot(turned[s], grad[:, columns], preferred_element_type=jnp.float32)
+            total = more if total is None else total + more
+        return columns, total
+
+    steps = grads[0].shape[1] // tile
+
+    @pl.when(pl.program_id(0) < pl.num_programs(0) // 2)
+    def _():
+        @pl.loop(0, steps)
+        def _(j):
+            columns, total = part_of(j)
+            own[:, columns] = total
+
+    @pl.when(pl.program_id(0) >= pl.num_programs(0) // 2)
+    def _():
+        @pl.loop(0, steps)
+        def _(j):
+            columns, total = part_of(j)
+            other[:, columns] = total.astype(other.dtype)
+
+
+def down_grads(position, hiddens, grads):
+    parts = len(hiddens)
+    count, units = hiddens[0].shape
+    width = grads[0].shape[1]
+    tile = 256
+    half = units // 2 // tile
+    whole = pl.BlockSpec((count, width), lambda i, at: (0, 0), pipeline_mode=pl.Buffered(1))
+    return pl.pallas_call(
+        down_grad_kernel,
+        grid_spec=pltpu.PrefetchScalarGridSpec(
+            num_scalar_prefetch=1,
+            grid=(2 * half,),
+            in_specs=[
+                pl.BlockSpec((count, tile), lambda i, at: (0, (i + at[0] * half) % (2 * half)))
+            ]
+            * parts
+            + [whole] * parts,
+            out_specs=[
+                pl.BlockSpec((tile, width), lambda i, at: (jnp.minimum(i, half - 1), 0)),
+                pl.BlockSpec((tile, width), lambda i, at: (jnp.maximum(i - half, 0), 0)),
+            ],
+            scratch_shapes=[pltpu.VMEM((parts, tile, count), jnp.bfloat16)],
+        ),
+        out_shape=[
+            jax.ShapeDtypeStruct((units // 2, width), jnp.float32),
+            jax.ShapeDtypeStruct((units // 2, width), jnp.bfloat16),
+        ],
+        compiler_params=pltpu.CompilerParams(vmem_limit_bytes=EXPERT_VMEM),
+        cost_estimate=pl.CostEstimate(
+            flops=2 * parts * count * width * units,
+            bytes_accessed=2 * parts * count * (width + units) + 3 * width * units,
+            transcendentals=0,
+        ),
+    )(position, *hiddens, *grads)
 
 
 def gather_weights(blocks):
     ring = [jnp.stack(part) for part in gather_chips(jnp.concatenate(blocks, axis=0))]
     return ring + [move_core(part) for part in ring]
-
-
-def after(values, earlier):
-    return values + (earlier[(0,) * earlier.ndim] * 0).astype(values.dtype)
 
 
 def body_dense(
@@ -540,24 +676,28 @@
     core = lax.axis_index("dp")
     here = lax.axis_index("expert")
     z_at, y_at, x_at = here // (NY * NX), here // NX % NY, here % NX
-    position = jnp.stack([core, z_at, y_at, x_at]).astype(jnp.int32)
+    position = jnp.stack([core, z_at, y_at, x_at, here]).astype(jnp.int32)
     half_width = model_width // 2
-    order = jnp.stack(
-        [
-            chip((z_at + NZ - s) % NZ, y_at ^ (k >> 1), x_at ^ (k & 1))
-            for s in range(NZ)
-            for k in range(NY * NX)
-        ]
-    )
+    plane = NY * NX
+    places = [(y_at ^ (k >> 1)) * NX + (x_at ^ (k & 1)) for k in range(plane)]
+    planes = [(z_at + NZ - s) % NZ for s in range(NZ)]
+
+    line = Line()
+    pieces_qk = gather_weights([w_query, w_key])
+    pieces_vo = gather_weights([w_value, w_output])
+    upstream_all = lax.all_gather(
+        after(cotangent, pieces_vo[UPSTREAM_AT]), "expert", axis=0, tiled=True
+    ).reshape(NZ, plane * tokens_here, model_width)
 
     expert_ids = jnp.arange(experts_all, dtype=jnp.int32)
     chosen = routes[:, :, None] == expert_ids[None, None, :]
     uses = jnp.any(chosen, axis=1).astype(f32)
     router_block = jnp.broadcast_to(w_router.astype(f32).reshape(1, -1), (owners, w_router.size))
+    small = jnp.concatenate([uses.T, router_block], axis=1)
     small = lax.all_to_all(
-        jnp.concatenate([uses.T, router_block], axis=1), "expert", split_axis=0, concat_axis=0, tiled=True
-    )
-    used_here = small[:, :tokens_here][order].reshape(NZ, NY * NX * tokens_here, 1)
+        small, "expert", split_axis=0, concat_axis=0, tiled=True
+    )
+    used_here = small[:, :tokens_here].reshape(NZ, plane * tokens_here, 1)
     own_router = small[:, tokens_here:].reshape(-1, experts_all)
     other_router = move_core(own_router)
     full_router = jnp.where(
@@ -566,19 +706,16 @@
         jnp.concatenate([other_router, own_router], axis=0),
     ).astype(bf16)
 
-    pieces_qk = gather_weights([w_query, w_key])
-    pieces_vo = gather_weights([w_value, w_output])
-
     inputs_f32 = hidden_in.astype(f32)
     normed_attn, inverse_attn = norm_forward(inputs_f32, attn_gain)
     act_attn = normed_attn.astype(bf16)
-    own_act = lax.dynamic_slice_in_dim(act_attn, core * half_width, half_width, axis=1)
+    own_act = lax.dynamic_slice_in_dim(act_attn, core * half_width, half_width, axis=1).T
     other_act = move_core(
         lax.dynamic_slice_in_dim(act_attn, (1 - core) * half_width, half_width, axis=1)
-    )
+    ).T
     query_pre = apply_weight(position, act_attn, pieces_qk, rows, 0)
     key_pre = apply_weight(position, act_attn, pieces_qk, rows, 1)
-    value_low = apply_weight(position, act_attn, pieces_vo, rows, 0).astype(bf16)
+    value_low = apply_weight(after(position, small), act_attn, pieces_vo, rows, 0).astype(bf16)
     query_normed, query_inverse = norm_forward(query_pre, query_gain)
     key_normed, key_inverse = norm_forward(key_pre, key_gain)
     cosine, sine_table = rotary_tables(tokens_here, head_dim)
@@ -606,22 +743,25 @@
     normed_moe, inverse_moe = norm_forward(middle, moe_gain)
     act_moe = normed_moe.astype(bf16)
 
-    acts = gather_chips(act_moe)
-    grads_out = gather_chips(after(cotangent, pieces_vo[NZ - 1]))
-
     logits = jnp.dot(act_moe, full_router, preferred_element_type=f32)
     router_probs = jax.nn.softmax(logits, axis=-1)
 
     gate_w, up_w, down_w = w_gate[0], w_up[0], w_down[0]
     mine = (expert_ids == here).astype(f32)
-    out_parts, row_parts, dots = [], [], []
-    all_acts, all_hidden, all_out_grads, all_gate_grads, all_up_grads = [], [], [], [], []
-    for s in range(NZ):
-        act_rows = jnp.concatenate(acts[s], axis=0)
+    forward, backward, ways = [], [], []
+    all_outs = jnp.zeros((NZ, plane * tokens_here, model_width), bf16)
+    for s, pieces in enumerate(gather_chips(act_moe)):
+        act_rows = jnp.zeros((plane, tokens_here, model_width), bf16)
+        for k in range(plane):
+            act_rows = lax.dynamic_update_slice(act_rows, pieces[k][None], (places[k], 0, 0))
+        act_rows = act_rows.reshape(plane * tokens_here, model_width)
+        if s:
+            act_rows = after(act_rows, expert_out)
+        used = lax.dynamic_index_in_dim(used_here, planes[s], axis=0, keepdims=False)
         probs_rows = jax.nn.softmax(
             jnp.dot(act_rows, full_router, preferred_element_type=f32), axis=-1
         )
-        gate_rows = jnp.sum(probs_rows * mine[None, :], axis=-1, keepdims=True) * used_here[s]
+        gate_rows = jnp.sum(probs_rows * mine[None, :], axis=-1, keepdims=True) * used
         gate_pre = jnp.dot(act_rows, gate_w, preferred_element_type=f32)
         up_pre = jnp.dot(act_rows, up_w, preferred_element_type=f32)
         sigmoid = jax.nn.sigmoid(gate_pre)
@@ -629,31 +769,43 @@
         hidden_low = (swish * up_pre).astype(bf16)
         expert_out = jnp.dot(hidden_low, down_w, preferred_element_type=f32).astype(bf16)
         out_low = (gate_rows * expert_out.astype(f32)).astype(bf16)
-        out_parts.append(jnp.split(out_low, NY * NX, axis=0))
-        upstream_rows = jnp.concatenate(grads_out[s], axis=0)
+        all_outs = lax.dynamic_update_slice(all_outs, out_low[None], (planes[s], 0, 0))
+        forward.append((act_rows, used, gate_rows, gate_pre, up_pre, hidden_low, expert_out))
+    rows_reduce = Reduce(line)
+    choice_rows = jnp.zeros((NZ, plane * tokens_here, 1), f32)
+    for s in range(NZ):
+        act_rows, used, gate_rows, gate_pre, up_pre, hidden_low, expert_out = forward[s]
+        upstream_rows = lax.dynamic_index_in_dim(upstream_all, planes[s], axis=0, keepdims=False)
+        if s:
+            upstream_rows = after(upstream_rows, row_grad)
         upstream_f32 = upstream_rows.astype(f32)
-        dots.append(jnp.sum(upstream_f32 * expert_out.astype(f32), axis=-1, keepdims=True) * used_here[s])
+        dots = jnp.sum(upstream_f32 * expert_out.astype(f32), axis=-1, keepdims=True) * used
+        choice_rows = lax.dynamic_update_slice(choice_rows, dots[None], (planes[s], 0, 0))
         out_grad = (gate_rows * upstream_f32).astype(bf16)
         hidden_grad = times_transposed(out_grad, down_w)
+        sigmoid = jax.nn.sigmoid(gate_pre)
         slope = sigmoid * (1.0 + gate_pre * (1.0 - sigmoid))
         gate_pre_grad = (hidden_grad * up_pre * slope).astype(bf16)
-        up_pre_grad = (hidden_grad * swish).astype(bf16)
+        up_pre_grad = (hidden_grad * (gate_pre * sigmoid)).astype(bf16)
         row_grad = (
             times_transposed(gate_pre_grad, gate_w) + times_transposed(up_pre_grad, up_w)
         ).astype(bf16)
-        row_parts.append(jnp.split(row_grad, NY * NX, axis=0))
-        all_acts.append(act_rows)
-        all_hidden.append(hidden_low)
-        all_out_grads.append(out_grad)
-        all_gate_grads.append(gate_pre_grad)
-        all_up_grads.append(up_pre_grad)
-    choice_rows = jnp.zeros((owners, tokens_here), f32).at[order].set(
-        jnp.concatenate(dots, axis=0).reshape(owners, tokens_here)
-    )
+        blocks = row_grad.reshape(plane, tokens_here, model_width)
+        own, for_x, for_y, across = [
+            lax.dynamic_index_in_dim(blocks, places[k], axis=0, keepdims=False)
+            for k in range(plane)
+        ]
+        cut = split_row(tokens_here)
+        backward.append((out_grad, gate_pre_grad, up_pre_grad))
+        rows_reduce.add(s, [own, for_x, for_y, across[:cut], across[cut:]])
+        ways.append(rows_reduce.ways())
     choice_grad = lax.all_to_all(
-        choice_rows, "expert", split_axis=0, concat_axis=0, tiled=True
+        choice_rows.reshape(owners, tokens_here), "expert", split_axis=0, concat_axis=0, tiled=True
     ).T
-    moe_in_grad = reduce_chips(row_parts)
+    own_down, other_down = down_grads(
+        after(position, *ways[3]), [chunk[5] for chunk in forward], [chunk[0] for chunk in backward]
+    )
+    moe_in_grad = after(rows_reduce.result(), own_down, other_down)
 
     logit_grad = router_probs * (
         choice_grad - jnp.sum(router_probs * choice_grad, axis=-1, keepdims=True)
@@ -665,16 +817,13 @@
     mid_norm_grad, moe_gain_grad = norm_backward(middle, inverse_moe, moe_gain, moe_in_grad)
     mid_grad = upstream + mid_norm_grad
     mid_low = mid_grad.astype(bf16)
-
-    own_attended = lax.dynamic_slice_in_dim(attended_low, core * half_width, half_width, axis=1)
+    moe_term = lax.psum_scatter(
+        after(all_outs, moe_in_grad).reshape(-1, model_width), "expert", scatter_dimension=0, tiled=True
+    ).astype(f32)
+    own_attended = lax.dynamic_slice_in_dim(attended_low, core * half_width, half_width, axis=1).T
     other_attended = move_core(
         lax.dynamic_slice_in_dim(attended_low, (1 - core) * half_width, half_width, axis=1)
-    )
-    output_grad = reduce_chips(
-        weight_grad_parts(
-            position, own_attended, other_attended, [mid_low, move_core(mid_low)], rows
-        )
-    )
+    ).T
     attended_grad = (
         apply_weight(position, mid_low, pieces_vo, rows, 1, back=True)
         .astype(bf16)
@@ -699,27 +848,37 @@
     key_pre_grad, key_gain_grad = norm_backward(key_pre, key_inverse, key_gain, key_back)
     query_low = query_pre_grad.astype(bf16)
     key_low = key_pre_grad.astype(bf16)
-    attn_weight_grads = reduce_chips(
-        weight_grad_parts(
-            position,
-            own_act,
-            other_act,
-            [
-                query_low,
-                move_core(query_low),
-                key_low,
-                move_core(key_low),
-                value_grad,
-                move_core(value_grad),
-            ],
-            rows,
-        )
-    )
-    query_weight_grad, key_weight_grad, value_weight_grad = jnp.split(attn_weight_grads, 3, axis=0)
+    attn_grads = []
+    for low in (query_low, key_low, value_grad):
+        attn_grads += [low, move_core(low)]
+    output_grads = [mid_low, move_core(mid_low)]
+    weights_reduce = Reduce(line)
+    ways = []
+    for s in (1, 2, 3, 0):
+        at = after(position, *ways[-2]) if len(ways) > 1 else position
+        attn_parts = weight_grad_parts(at, own_act, other_act, attn_grads, rows, s)
+        output_parts = weight_grad_parts(at, own_attended, other_attended, output_grads, rows, s)
+        own_part, for_x, for_y, across = [
+            jnp.concatenate(pair, axis=0) for pair in zip(attn_parts, output_parts, strict=True)
+        ]
+        weights_reduce.add(s, [own_part, for_x, for_y, *jnp.split(across, 2, axis=0)])
+        ways.append(weights_reduce.ways())
+    query_weight_grad, key_weight_grad, value_weight_grad, output_grad = jnp.split(
+        weights_reduce.result(), 4, axis=0
+    )
+    sums = weights_reduce.planes
+    later = after(position, *attn_parts, *output_parts, sums[1])
     act_grad = (
-        apply_weight(position, query_low, pieces_qk, rows, 0, back=True)
-        + apply_weight(position, key_low, pieces_qk, rows, 1, back=True)
-        + apply_weight(position, value_grad, pieces_vo, rows, 0, back=True)
+        apply_weight(later, query_low, pieces_qk, rows, 0, back=True)
+        + apply_weight(later, key_low, pieces_qk, rows, 1, back=True)
+        + apply_weight(later, value_grad, pieces_vo, rows, 0, back=True)
+    )
+    expert_acts = [chunk[0] for chunk in forward]
+    own_gate, other_gate = column_grads(
+        after(later, act_grad, sums[2]), expert_acts, [chunk[1] for chunk in backward]
+    )
+    own_up, other_up = column_grads(
+        after(later, own_gate, sums[3]), expert_acts, [chunk[2] for chunk in backward]
     )
     input_norm_grad, attn_gain_grad = norm_backward(inputs_f32, inverse_attn, attn_gain, act_grad)
     input_grad = (mid_grad + input_norm_grad).astype(bf16)
@@ -742,25 +901,10 @@
         small_grads, [rows, 2 * rows, 3 * rows, 4 * rows]
     )
 
-    moe_term = reduce_chips(out_parts)
     block_out = (middle + moe_term).astype(bf16)
-    expert_acts = jnp.concatenate(all_acts, axis=0)
-    gate_weight_grad = inner_product(expert_acts, jnp.concatenate(all_gate_grads, axis=0))
-    up_weight_grad = inner_product(expert_acts, jnp.concatenate(all_up_grads, axis=0))
-    down_grad = inner_product(
-        jnp.concatenate(all_hidden, axis=0), jnp.concatenate(all_out_grads, axis=0)
-    )
-    gate_weight_grad, up_weight_grad, down_grad = (
-        lax.psum_scatter(
-            gate_weight_grad.astype(bf16)[None], "dp", scatter_dimension=2, tiled=True
-        ).astype(f32),
-        lax.psum_scatter(
-            up_weight_grad.astype(bf16)[None], "dp", scatter_dimension=2, tiled=True
-        ).astype(f32),
-        lax.psum_scatter(
-            down_grad.astype(bf16)[None], "dp", scatter_dimension=1, tiled=True
-        ).astype(f32),
-    )
+    down_grad = after(own_down, sums[2]) + move_core(after(other_down, sums[1])).astype(f32)
+    gate_weight_grad = own_gate + move_core(other_gate).astype(f32)
+    up_weight_grad = own_up + move_core(other_up).astype(f32)
     return (
         block_out,
         input_grad,
@@ -773,9 +917,9 @@
         output_grad,
         moe_gain_grad,
         router_grad.reshape(w_router.shape),
-        gate_weight_grad,
-        up_weight_grad,
-        down_grad,
+        gate_weight_grad[None],
+        up_weight_grad[None],
+        down_grad[None],
     )
 
 

time: 1140 us -> 987 us (0.87)
  waiting for transfers between devices: 447 us -> 328 us
  matrix products: 208 us -> 141 us
  Pallas kernels: 92.1 us -> 152 us
  starting transfers between devices: 200 us -> 143 us
  other arithmetic: 79 us -> 123 us
  local copies, waits for them, and re-layouts: 93.1 us -> 73.9 us
    ppermute x64 -> x40, waiting for transfers between devices: 254 us -> 110 us  [move_x(): return lax.ppermute(values, 'expert', X_PAIRS)]
    ppermute x64 -> x40, waiting for transfers between devices: 112 us -> 193 us  [move_y(): return lax.ppermute(values, 'expert', Y_PAIRS)]
    ppermute x24 -> x15, waiting for transfers between devices: 73.7 us -> 17.8 us  [move_z(): return lax.ppermute(values, 'expert', Z_PAIRS)]
    dot_general x4 -> x1, matrix products: 57.8 us -> 2.6 us  [inner_product(): jnp.einsum('ta,tb->ab', left, right, preferred_element_type=jnp.float32)]
    pallas_call x8 -> x11, Pallas kernels: 62.7 us -> 116 us  [the longest x8 52.3 us: apply_weight(): pl.pallas_call(functools.partial(apply_back_kernel if back else apply_ker...]
    ppermute x64 -> x40, starting transfers between devices: 72.5 us -> 46.5 us  [move_x(): return lax.ppermute(values, 'expert', X_PAIRS)]
    ppermute x64 -> x40, starting transfers between devices: 67.5 us -> 47.2 us  [move_y(): return lax.ppermute(values, 'expert', Y_PAIRS)]
    unnamed x388 -> x334, local copies, waits for them, and re-layouts: 42.8 us -> 24 us
  transfers between devices with their start and end apart: 173 -> 118, of which waited for: 69 -> 53; matrix products, arithmetic and copies ran while one was open for 21% -> 27% of each run, Pallas kernels for 8% -> 16%
where the time goes in v2:
time: 987 us; the launch traced here: 978 us
  waiting for transfers between devices  328 us (33%)
  Pallas kernels  152 us (15%)
  starting transfers between devices  143 us (14%)
  matrix products  141 us (14%)
  other arithmetic  123 us (12%)
  local copies, waits for them, and re-layouts  73.9 us (7%)
  between operations  17.5 us (2%)
    ppermute x40, waiting for transfers between devices, move_y(): return lax.ppermute(values, 'expert', Y_PAIRS)  193 us
    ppermute x40, waiting for transfers between devices, move_x(): return lax.ppermute(values, 'expert', X_PAIRS)  110 us
    dot_general x13, matrix products, times_transposed(): jnp.einsum('ta,ba->tb', left, right, preferred_element_type=jnp.float32)  71.7 us
    pallas_call x8, Pallas kernels, apply_weight(): pl.pallas_call(functools.partial(apply_back_kernel if back else apply_ker...  52.3 us
    ppermute x40, starting transfers between devices, move_y(): return lax.ppermute(values, 'expert', Y_PAIRS)  47.2 us
    ppermute x40, starting transfers between devices, move_x(): return lax.ppermute(values, 'expert', X_PAIRS)  46.5 us
    pallas_call x2, Pallas kernels, column_grads(): pl.pallas_call(column_grad_kernel, grid=(width // tile,), out_shape=[jax....  38.4 us
    pallas_call x8, Pallas kernels, weight_grad_parts(): pl.pallas_call(functools.partial(weight_grad_kernel, rows=rows, count=cou...  35.8 us
  transfers between devices with their start and end apart: 118, of which 53 were waited for; matrix products, arithmetic and copies ran while one was open for 27% of the time, Pallas kernels for 16%

profile of v2, /device:TPU:0, one launch (start us, length us, event | category | flops | bytes accessed | tf_op | source)
XLA Modules:
  0.0 978.4 jit_solution(7305052560824114800)
XLA Ops:
  18.4 6.6 collective-permute-done.1
  28.8 6.7 collective-permute-done.24
  105.4 13.2 %collective-permute-done.36 = bf16[64,2048]{1,0:T(8,128)(2,1)S(1)} collective-permute-done((bf16[64,2048]{1,0:T(8,128)(2,1)S(1)}, bf16[64,2048]{1,0:T(8,128)(2,1)S(1)}, u32[]{:S(2)}, u32[]{:S(2)}) %collective-permute-start.36) | collective-permute-done | bytes 262176 | tf_op jit(solution)/shard_map/ppermute | solution.py:312
  126.8 7.0 collective-permute-done.8
  220.3 20.1 %collective-permute-done.47 = bf16[192,2048]{1,0:T(8,128)(2,1)} collective-permute-done((bf16[192,2048]{1,0:T(8,128)(2,1)S(1)}, bf16[192,2048]{1,0:T(8,128)(2,1)}, u32[]{:S(2)}, u32[]{:S(2)}) %collective-permute-start.47) | collective-permute-done | bytes 786464 | tf_op jit(solution)/shard_map/ppermute | solution.py:312
  242.9 8.7 collective-permute-done.46
  288.6 13.6 %collective-permute-done.54 = bf16[96,2048]{1,0:T(8,128)(2,1)S(1)} collective-permute-done((bf16[96,2048]{1,0:T(8,128)(2,1)S(1)}, bf16[96,2048]{1,0:T(8,128)(2,1)S(1)}, u32[]{:S(2)}, u32[]{:S(2)}) %collective-permute-start.54) | collective-permute-done | bytes 393248 | tf_op jit(solution)/shard_map/ppermute | solution.py:308
  317.5 17.2 %collective-permute-done.58 = bf16[192,2048]{1,0:T(8,128)(2,1)S(1)} collective-permute-done((bf16[192,2048]{1,0:T(8,128)(2,1)S(1)}, bf16[192,2048]{1,0:T(8,128)(2,1)S(1)}, u32[]{:S(2)}, u32[]{:S(2)}) %collective-permute-start.58) | collective-permute-done | bytes 786464 | tf_op jit(solution)/shard_map/ppermute | solution.py:312
  340.1 15.0 %collective-permute-done.59 = bf16[96,2048]{1,0:T(8,128)(2,1)S(1)} collective-permute-done((bf16[96,2048]{1,0:T(8,128)(2,1)S(1)}, bf16[96,2048]{1,0:T(8,128)(2,1)S(1)}, u32[]{:S(2)}, u32[]{:S(2)}) %collective-permute-start.59) | collective-permute-done | bytes 393248 | tf_op jit(solution)/shard_map/ppermute | solution.py:308
  370.6 6.7 collective-permute-done.63
  379.7 7.1 collective-permute-done.64
  422.1 11.1 %multiply_convert_fusion.8 = (bf16[768,1024]{1,0:T(8,128)(2,1)}, bf16[768,1024]{1,0:T(8,128)(2,1)S(1)}) fusion(f32[768,1024]{1,0:T(8,128)} %copy-done.153, f32[768,1024]{1,0:T(8,128)} %get-tuple-element.349, bf16[1,1024,2048]{2,1,0:T(8,128)(2,1)} %param.31, f32[768]{0:T(1024)S(1)} %mul.655, bf16[4,768,2048]{2,1,0:T(8,128)(2,1)} %bitcast.483, s32[]{:T(128)S(6)} %select_n.133), kind=kOutput, calls=%fused_computation.112 | convolution fusion | flops 3236167680 | bytes 16780292 | tf_op jit(solution)/shard_map/ta,ba->tb/dot_general | solution.py:51
  450.5 7.3 multiply_convert_fusion.6
  463.3 7.1 add_convert_fusion.2
  475.2 8.2 multiply_convert_fusion.4
  498.9 6.6 multiply_convert_fusion.2
  538.0 17.3 %collective-permute-done.75 = bf16[96,2048]{1,0:T(8,128)(2,1)S(1)} collective-permute-done((bf16[96,2048]{1,0:T(8,128)(2,1)S(1)}, bf16[96,2048]{1,0:T(8,128)(2,1)S(1)}, u32[]{:S(2)}, u32[]{:S(2)}) %collective-permute-start.75) | collective-permute-done | bytes 393248 | tf_op jit(solution)/shard_map/ppermute | solution.py:312
  565.2 12.9 %collective-permute-done.67 = bf16[192,2048]{1,0:T(8,128)(2,1)S(1)} collective-permute-done((bf16[192,2048]{1,0:T(8,128)(2,1)S(1)}, bf16[192,2048]{1,0:T(8,128)(2,1)S(1)}, u32[]{:S(2)}, u32[]{:S(2)}) %collective-permute-start.67) | collective-permute-done | bytes 786464 | tf_op jit(solution)/shard_map/ppermute | solution.py:308
  579.6 7.7 collective-permute-done.71
  593.3 10.1 %collective-permute-done.76 = bf16[192,2048]{1,0:T(8,128)(2,1)S(1)} collective-permute-done((bf16[192,2048]{1,0:T(8,128)(2,1)S(1)}, bf16[192,2048]{1,0:T(8,128)(2,1)S(1)}, u32[]{:S(2)}, u32[]{:S(2)}) %collective-permute-start.76) | collective-permute-done | bytes 786464 | tf_op jit(solution)/shard_map/ppermute | solution.py:308
  615.9 9.1 collective-permute-done.79
  628.3 25.8 %shard_map.267 = (f32[512,2048]{1,0:T(8,128)}, bf16[512,2048]{1,0:T(8,128)(2,1)}) custom-call(s32[5]{0:T(128)} %copy-done.27, bf16[768,1024]{1,0:T(8,128)(2,1)} %copy-done.159, bf16[768,1024]{1,0:T(8,128)(2,1)} %copy-done.160, bf16[768,1024]{1,0:T(8,128)(2,1)} %copy-done.161, bf16[768,1024]{1,0:T(8,128)(2,1)} %copy-done.149, ...), custom_call_target="tpu_custom_call" | custom-call | flops 12884901888 | bytes 25165824 | tf_op jit(solution)/shard_map/pallas_call | solution.py:616
  661.7 6.8 shard_map.268
  762.5 29.2 %collective-permute-done.101 = bf16[128,2048]{1,0:T(8,128)(2,1)S(1)} collective-permute-done((bf16[128,2048]{1,0:T(8,128)(2,1)}, bf16[128,2048]{1,0:T(8,128)(2,1)S(1)}, u32[]{:S(2)}, u32[]{:S(2)}) %collective-permute-start.101) | collective-permute-done | bytes 524320 | tf_op jit(solution)/shard_map/ppermute | solution.py:312
  802.9 7.1 shard_map.277
  810.0 7.0 shard_map.276
  817.1 6.9 shard_map.275
  850.0 10.2 %collective-permute-done.98 = bf16[256,2048]{1,0:T(8,128)(2,1)} collective-permute-done((bf16[256,2048]{1,0:T(8,128)(2,1)}, bf16[256,2048]{1,0:T(8,128)(2,1)}, u32[]{:S(2)}, u32[]{:S(2)}) %collective-permute-start.98) | collective-permute-done | bytes 1048608 | tf_op jit(solution)/shard_map/ppermute | solution.py:308
  869.1 6.6 collective-permute-start.100
  875.8 19.2 %shard_map.280 = (f32[2048,512]{1,0:T(8,128)}, bf16[2048,512]{1,0:T(8,128)(2,1)}) custom-call(s32[5]{0:T(128)} %copy-done.27, bf16[768,2048]{1,0:T(8,128)(2,1)} %bitcast.464, bf16[768,2048]{1,0:T(8,128)(2,1)} %bitcast.469, bf16[768,2048]{1,0:T(8,128)(2,1)} %bitcast.474, bf16[768,2048]{1,0:T(8,128)(2,1)} %bitcast.478, ...), custom_call_target="tpu_custom_call" | custom-call | flops 12884901888 | bytes 25165824 | tf_op jit(solution)/shard_map/pallas_call | solution.py:560
  895.0 28.1 %collective-permute-done.104 = bf16[256,2048]{1,0:T(8,128)(2,1)} collective-permute-done((bf16[256,2048]{1,0:T(8,128)(2,1)}, bf16[256,2048]{1,0:T(8,128)(2,1)}, u32[]{:S(2)}, u32[]{:S(2)}) %collective-permute-start.104) | collective-permute-done | bytes 1048608 | tf_op jit(solution)/shard_map/ppermute | solution.py:312
  928.0 19.2 %shard_map.281 = (f32[2048,512]{1,0:T(8,128)}, bf16[2048,512]{1,0:T(8,128)(2,1)}) custom-call(s32[5]{0:T(128)} %copy-done.27, bf16[768,2048]{1,0:T(8,128)(2,1)} %bitcast.465, bf16[768,2048]{1,0:T(8,128)(2,1)} %bitcast.470, bf16[768,2048]{1,0:T(8,128)(2,1)} %bitcast.475, bf16[768,2048]{1,0:T(8,128)(2,1)} %bitcast.479, bf16[768,1024]{1,0:T(8,128)(2,1)} %copy-done.150, ...), custom_call_target="tpu_custom_call" | custom-call | flops 12884901888 | bytes 25165824 | tf_op jit(solution)/shard_map/pallas_call | solution.py:560
  (808 shorter events, 575.4 us)
Async XLA Ops:
  52.8 121.9 %all-to-all-start = ((f32[16,1,1216]{2,1,0:T(1,128)}), f32[16,1,1216]{2,1,0:T(1,128)S(1)}, u32[]{:S(2)}, u32[]{:S(2)}) async-start(f32[16,1,1216]{2,1,0:T(1,128)} %all_to_all.22), calls=%async_computation | async-start | bytes 163840 | tf_op jit(solution)/shard_map/all_to_all | solution.py:697
  58.8 352.0 %all-gather.2.cloned.1.call-start = ((), (), s32[]{:S(2)}) async-start(), calls=%async_computation.4 | async-start | bytes 13369344 | tf_op jit(solution)/shard_map/all_gather | solution.py:688
  126.8 43.7 %collective-permute-start.42 = (bf16[4,128,2048]{2,1,0:T(8,128)(2,1)S(1)}, bf16[4,128,2048]{2,1,0:T(8,128)(2,1)S(1)}, u32[]{:S(2)}, u32[]{:S(2)}) collective-permute-start(bf16[4,128,2048]{2,1,0:T(8,128)(2,1)S(1)} %pad_maximum_fusion.4.refs_0_), channel_id=1, source_target_pairs={{0,16},{16,0},{1,17},{17,1},{2,18},{18,2},{3,19},{19,3},{4,20},{20... | collective-permute-start | bytes 6291464 | tf_op jit(solution)/shard_map/ppermute | solution.py:320
  133.8 37.2 %collective-permute-start.43 = (bf16[4,128,2048]{2,1,0:T(8,128)(2,1)S(1)}, bf16[4,128,2048]{2,1,0:T(8,128)(2,1)S(1)}, u32[]{:S(2)}, u32[]{:S(2)}) collective-permute-start(bf16[4,128,2048]{2,1,0:T(8,128)(2,1)S(1)} %pad_maximum_fusion.5.refs_1_), channel_id=1, source_target_pairs={{0,16},{16,0},{1,17},{17,1},{2,18},{18,2},{3,19},{19,3},{4,20},{20... | collective-permute-start | bytes 6291464 | tf_op jit(solution)/shard_map/ppermute | solution.py:320
  133.8 37.3 %collective-permute-start.44 = (bf16[4,128,2048]{2,1,0:T(8,128)(2,1)S(1)}, bf16[4,128,2048]{2,1,0:T(8,128)(2,1)S(1)}, u32[]{:S(2)}, u32[]{:S(2)}) collective-permute-start(bf16[4,128,2048]{2,1,0:T(8,128)(2,1)S(1)} %pad_maximum_fusion.6.refs_2_), channel_id=1, source_target_pairs={{0,16},{16,0},{1,17},{17,1},{2,18},{18,2},{3,19},{19,3},{4,20},{20... | collective-permute-start | bytes 6291464 | tf_op jit(solution)/shard_map/ppermute | solution.py:320
  214.3 37.3 %collective-permute-start.46 = (bf16[192,2048]{1,0:T(8,128)(2,1)S(1)}, bf16[192,2048]{1,0:T(8,128)(2,1)}, u32[]{:S(2)}, u32[]{:S(2)}) collective-permute-start(bf16[192,2048]{1,0:T(8,128)(2,1)S(1)} %get-tuple-element.257), channel_id=1, source_target_pairs={{0,1},{1,0},{2,3},{3,2},{4,5},{5,4},{6,7},{7,6},{8,9},{9,8},{10,11... | collective-permute-start | bytes 2359304 | tf_op jit(solution)/shard_map/ppermute | solution.py:308
  215.1 38.7 %collective-permute-start.51 = (bf16[192,2048]{1,0:T(8,128)(2,1)S(1)}, bf16[192,2048]{1,0:T(8,128)(2,1)}, u32[]{:S(2)}, u32[]{:S(2)}) collective-permute-start(bf16[192,2048]{1,0:T(8,128)(2,1)S(1)} %get-tuple-element.257), channel_id=1, source_target_pairs={{0,4},{1,5},{2,6},{3,7},{4,8},{5,9},{6,10},{7,11},{8,12},{9,13},{1... | collective-permute-start | bytes 2359304 | tf_op jit(solution)/shard_map/ppermute | solution.py:316
  284.1 53.3 %collective-permute-start.61 = (bf16[192,2048]{1,0:T(8,128)(2,1)S(1)}, bf16[192,2048]{1,0:T(8,128)(2,1)S(1)}, u32[]{:S(2)}, u32[]{:S(2)}) collective-permute-start(bf16[192,2048]{1,0:T(8,128)(2,1)S(1)} %collective-permute-done.56), channel_id=1, source_target_pairs={{0,4},{1,5},{2,6},{3,7},{4,8},{5,9},{6,10},{7,11},{8,12},{9,13},{1... | collective-permute-start | bytes 2359304 | tf_op jit(solution)/shard_map/ppermute | solution.py:316
  286.1 48.6 %collective-permute-start.58 = (bf16[192,2048]{1,0:T(8,128)(2,1)S(1)}, bf16[192,2048]{1,0:T(8,128)(2,1)S(1)}, u32[]{:S(2)}, u32[]{:S(2)}) collective-permute-start(bf16[192,2048]{1,0:T(8,128)(2,1)S(1)} %collective-permute-done.56), channel_id=1, source_target_pairs={{0,2},{1,3},{2,0},{3,1},{4,6},{5,7},{6,4},{7,5},{8,10},{9,11},{10,... | collective-permute-start | bytes 2359304 | tf_op jit(solution)/shard_map/ppermute | solution.py:312
  286.5 48.8 %collective-permute-start.57 = (bf16[192,2048]{1,0:T(8,128)(2,1)S(1)}, bf16[192,2048]{1,0:T(8,128)(2,1)S(1)}, u32[]{:S(2)}, u32[]{:S(2)}) collective-permute-start(bf16[192,2048]{1,0:T(8,128)(2,1)S(1)} %collective-permute-done.56), channel_id=1, source_target_pairs={{0,1},{1,0},{2,3},{3,2},{4,5},{5,4},{6,7},{7,6},{8,9},{9,8},{10,11... | collective-permute-start | bytes 2359304 | tf_op jit(solution)/shard_map/ppermute | solution.py:308
  337.4 39.9 %collective-permute-start.63 = (bf16[192,2048]{1,0:T(8,128)(2,1)S(1)}, bf16[192,2048]{1,0:T(8,128)(2,1)S(1)}, u32[]{:S(2)}, u32[]{:S(2)}) collective-permute-start(bf16[192,2048]{1,0:T(8,128)(2,1)S(1)} %collective-permute-done.61), channel_id=1, source_target_pairs={{0,2},{1,3},{2,0},{3,1},{4,6},{5,7},{6,4},{7,5},{8,10},{9,11},{10,... | collective-permute-start | bytes 2359304 | tf_op jit(solution)/shard_map/ppermute | solution.py:312
  337.5 41.1 %collective-permute-start.62 = (bf16[192,2048]{1,0:T(8,128)(2,1)S(1)}, bf16[192,2048]{1,0:T(8,128)(2,1)S(1)}, u32[]{:S(2)}, u32[]{:S(2)}) collective-permute-start(bf16[192,2048]{1,0:T(8,128)(2,1)S(1)} %collective-permute-done.61), channel_id=1, source_target_pairs={{0,1},{1,0},{2,3},{3,2},{4,5},{5,4},{6,7},{7,6},{8,9},{9,8},{10,11... | collective-permute-start | bytes 2359304 | tf_op jit(solution)/shard_map/ppermute | solution.py:308
  447.8 79.5 %collective-permute-start.69 = (bf16[96,2048]{1,0:T(8,128)(2,1)}, bf16[96,2048]{1,0:T(8,128)(2,1)}, u32[]{:S(2)}, u32[]{:S(2)}) collective-permute-start(bf16[96,2048]{1,0:T(8,128)(2,1)} %get-tuple-element.297), channel_id=1, source_target_pairs={{0,2},{1,3},{2,0},{3,1},{4,6},{5,7},{6,4},{7,5},{8,10},{9,11},{10,... | collective-permute-start | bytes 1179656 | tf_op jit(solution)/shard_map/ppermute | solution.py:312
  448.8 78.6 %collective-permute-start.72 = (bf16[96,2048]{1,0:T(8,128)(2,1)}, bf16[96,2048]{1,0:T(8,128)(2,1)}, u32[]{:S(2)}, u32[]{:S(2)}) collective-permute-start(bf16[96,2048]{1,0:T(8,128)(2,1)} %get-tuple-element.299), channel_id=1, source_target_pairs={{0,1},{1,0},{2,3},{3,2},{4,5},{5,4},{6,7},{7,6},{8,9},{9,8},{10,11... | collective-permute-start | bytes 1179656 | tf_op jit(solution)/shard_map/ppermute | solution.py:308
  473.2 61.3 %collective-permute-start.66 = (bf16[96,2048]{1,0:T(8,128)(2,1)}, bf16[96,2048]{1,0:T(8,128)(2,1)}, u32[]{:S(2)}, u32[]{:S(2)}) collective-permute-start(bf16[96,2048]{1,0:T(8,128)(2,1)} %get-tuple-element.279), channel_id=1, source_target_pairs={{0,2},{1,3},{2,0},{3,1},{4,6},{5,7},{6,4},{7,5},{8,10},{9,11},{10,... | collective-permute-start | bytes 1179656 | tf_op jit(solution)/shard_map/ppermute | solution.py:312
  473.5 60.3 %collective-permute-start.68 = (bf16[96,2048]{1,0:T(8,128)(2,1)}, bf16[96,2048]{1,0:T(8,128)(2,1)}, u32[]{:S(2)}, u32[]{:S(2)}) collective-permute-start(bf16[96,2048]{1,0:T(8,128)(2,1)} %get-tuple-element.281), channel_id=1, source_target_pairs={{0,1},{1,0},{2,3},{3,2},{4,5},{5,4},{6,7},{7,6},{8,9},{9,8},{10,11... | collective-permute-start | bytes 1179656 | tf_op jit(solution)/shard_map/ppermute | solution.py:308
  511.5 100.5 %all-to-all-start.1 = ((f32[16,1,192]{2,1,0:T(1,128)}), f32[16,1,192]{2,1,0:T(1,128)S(1)}, u32[]{:S(2)}, u32[]{:S(2)}) async-start(f32[16,1,192]{2,1,0:T(1,128)} %all_to_all.25), calls=%async_computation.1 | async-start | bytes 32768 | tf_op jit(solution)/shard_map/all_to_all | solution.py:802
  517.4 449.2 %reduce-scatter.2.cloned.1.call-start = ((), (), s32[]{:S(2)}) async-start(), calls=%async_computation.5 | async-start | bytes 13369344 | tf_op jit(solution)/shard_map/reduce_scatter | solution.py:820
  530.2 57.4 %collective-permute-start.73 = (bf16[192,2048]{1,0:T(8,128)(2,1)S(1)}, bf16[192,2048]{1,0:T(8,128)(2,1)S(1)}, u32[]{:S(2)}, u32[]{:S(2)}) collective-permute-start(bf16[192,2048]{1,0:T(8,128)(2,1)S(1)} %pad_maximum_fusion.15), channel_id=1, source_target_pairs={{0,2},{1,3},{2,0},{3,1},{4,6},{5,7},{6,4},{7,5},{8,10},{9,11},{10,... | collective-permute-start | bytes 2359304 | tf_op jit(solution)/shard_map/ppermute | solution.py:312
  536.0 42.1 %collective-permute-start.67 = (bf16[192,2048]{1,0:T(8,128)(2,1)S(1)}, bf16[192,2048]{1,0:T(8,128)(2,1)S(1)}, u32[]{:S(2)}, u32[]{:S(2)}) collective-permute-start(bf16[192,2048]{1,0:T(8,128)(2,1)S(1)} %pad_maximum_fusion.12), channel_id=1, source_target_pairs={{0,1},{1,0},{2,3},{3,2},{4,5},{5,4},{6,7},{7,6},{8,9},{9,8},{10,11... | collective-permute-start | bytes 2359304 | tf_op jit(solution)/shard_map/ppermute | solution.py:308
  732.7 64.9 %collective-permute-start.94 = (bf16[256,2048]{1,0:T(8,128)(2,1)}, bf16[256,2048]{1,0:T(8,128)(2,1)S(1)}, u32[]{:S(2)}, u32[]{:S(2)}) collective-permute-start(bf16[256,2048]{1,0:T(8,128)(2,1)} %pad_maximum_fusion.8), channel_id=1, source_target_pairs={{0,1},{1,0},{2,3},{3,2},{4,5},{5,4},{6,7},{7,6},{8,9},{9,8},{10,11... | collective-permute-start | bytes 3145736 | tf_op jit(solution)/shard_map/ppermute | solution.py:308
  733.0 64.6 %collective-permute-start.96 = (bf16[256,2048]{1,0:T(8,128)(2,1)}, bf16[256,2048]{1,0:T(8,128)(2,1)}, u32[]{:S(2)}, u32[]{:S(2)}) collective-permute-start(bf16[256,2048]{1,0:T(8,128)(2,1)} %fusion.140), channel_id=1, source_target_pairs={{0,2},{1,3},{2,0},{3,1},{4,6},{5,7},{6,4},{7,5},{8,10},{9,11},{10,... | collective-permute-start | bytes 3145736 | tf_op jit(solution)/shard_map/ppermute | solution.py:312
  745.7 46.0 %collective-permute-start.103 = (bf16[128,2048]{1,0:T(8,128)(2,1)}, bf16[128,2048]{1,0:T(8,128)(2,1)}, u32[]{:S(2)}, u32[]{:S(2)}) collective-permute-start(bf16[128,2048]{1,0:T(8,128)(2,1)} %get-tuple-element.176), channel_id=1, source_target_pairs={{0,1},{1,0},{2,3},{3,2},{4,5},{5,4},{6,7},{7,6},{8,9},{9,8},{10,11... | collective-permute-start | bytes 1572872 | tf_op jit(solution)/shard_map/ppermute | solution.py:308
  753.7 38.0 %collective-permute-start.101 = (bf16[128,2048]{1,0:T(8,128)(2,1)}, bf16[128,2048]{1,0:T(8,128)(2,1)S(1)}, u32[]{:S(2)}, u32[]{:S(2)}) collective-permute-start(bf16[128,2048]{1,0:T(8,128)(2,1)} %get-tuple-element.173), channel_id=1, source_target_pairs={{0,2},{1,3},{2,0},{3,1},{4,6},{5,7},{6,4},{7,5},{8,10},{9,11},{10,... | collective-permute-start | bytes 1572872 | tf_op jit(solution)/shard_map/ppermute | solution.py:312
  791.7 43.1 %collective-permute-start.107 = (bf16[128,2048]{1,0:T(8,128)(2,1)}, bf16[128,2048]{1,0:T(8,128)(2,1)}, u32[]{:S(2)}, u32[]{:S(2)}) collective-permute-start(bf16[128,2048]{1,0:T(8,128)(2,1)} %get-tuple-element.181), channel_id=1, source_target_pairs={{0,1},{1,0},{2,3},{3,2},{4,5},{5,4},{6,7},{7,6},{8,9},{9,8},{10,11... | collective-permute-start | bytes 1572872 | tf_op jit(solution)/shard_map/ppermute | solution.py:308
  793.2 44.2 %collective-permute-start.106 = (bf16[128,2048]{1,0:T(8,128)(2,1)}, bf16[128,2048]{1,0:T(8,128)(2,1)}, u32[]{:S(2)}, u32[]{:S(2)}) collective-permute-start(bf16[128,2048]{1,0:T(8,128)(2,1)} %get-tuple-element.180), channel_id=1, source_target_pairs={{0,2},{1,3},{2,0},{3,1},{4,6},{5,7},{6,4},{7,5},{8,10},{9,11},{10,... | collective-permute-start | bytes 1572872 | tf_op jit(solution)/shard_map/ppermute | solution.py:312
  800.4 61.2 %collective-permute-start.97 = (bf16[256,2048]{1,0:T(8,128)(2,1)}, bf16[256,2048]{1,0:T(8,128)(2,1)}, u32[]{:S(2)}, u32[]{:S(2)}) collective-permute-start(bf16[256,2048]{1,0:T(8,128)(2,1)} %convert_add_fusion.3), channel_id=1, source_target_pairs={{0,4},{1,5},{2,6},{3,7},{4,8},{5,9},{6,10},{7,11},{8,12},{9,13},{1... | collective-permute-start | bytes 3145736 | tf_op jit(solution)/shard_map/ppermute | solution.py:316
  802.9 144.2 %collective-permute-start.112 = (bf16[512,2048]{1,0:T(8,128)(2,1)}, bf16[512,2048]{1,0:T(8,128)(2,1)}, u32[]{:S(2)}, u32[]{:S(2)}) collective-permute-start(bf16[512,2048]{1,0:T(8,128)(2,1)} %get-tuple-element.191), channel_id=1, source_target_pairs={{0,16},{16,0},{1,17},{17,1},{2,18},{18,2},{3,19},{19,3},{4,20},{20... | collective-permute-start | bytes 6291464 | tf_op jit(solution)/shard_map/ppermute | solution.py:320
  840.8 112.5 %collective-permute-start.109 = (bf16[256,2048]{1,0:T(8,128)(2,1)}, bf16[256,2048]{1,0:T(8,128)(2,1)}, u32[]{:S(2)}, u32[]{:S(2)}) collective-permute-start(bf16[256,2048]{1,0:T(8,128)(2,1)} %fusion.146), channel_id=1, source_target_pairs={{0,2},{1,3},{2,0},{3,1},{4,6},{5,7},{6,4},{7,5},{8,10},{9,11},{10,... | collective-permute-start | bytes 3145736 | tf_op jit(solution)/shard_map/ppermute | solution.py:312
  868.1 55.1 %collective-permute-start.104 = (bf16[256,2048]{1,0:T(8,128)(2,1)}, bf16[256,2048]{1,0:T(8,128)(2,1)}, u32[]{:S(2)}, u32[]{:S(2)}) collective-permute-start(bf16[256,2048]{1,0:T(8,128)(2,1)} %fusion.144), channel_id=1, source_target_pairs={{0,2},{1,3},{2,0},{3,1},{4,6},{5,7},{6,4},{7,5},{8,10},{9,11},{10,... | collective-permute-start | bytes 3145736 | tf_op jit(solution)/shard_map/ppermute | solution.py:312
  869.1 54.1 %collective-permute-start.100 = (bf16[256,2048]{1,0:T(8,128)(2,1)}, bf16[256,2048]{1,0:T(8,128)(2,1)}, u32[]{:S(2)}, u32[]{:S(2)}) collective-permute-start(bf16[256,2048]{1,0:T(8,128)(2,1)} %add_convert_fusion.5), channel_id=1, source_target_pairs={{0,4},{1,5},{2,6},{3,7},{4,8},{5,9},{6,10},{7,11},{8,12},{9,13},{1... | collective-permute-start | bytes 3145736 | tf_op jit(solution)/shard_map/ppermute | solution.py:316
  895.0 58.3 %collective-permute-start.108 = (bf16[256,2048]{1,0:T(8,128)(2,1)}, bf16[256,2048]{1,0:T(8,128)(2,1)}, u32[]{:S(2)}, u32[]{:S(2)}) collective-permute-start(bf16[256,2048]{1,0:T(8,128)(2,1)} %pad_maximum_fusion.11), channel_id=1, source_target_pairs={{0,1},{1,0},{2,3},{3,2},{4,5},{5,4},{6,7},{7,6},{8,9},{9,8},{10,11... | collective-permute-start | bytes 3145736 | tf_op jit(solution)/shard_map/ppermute | solution.py:308
  (251 other events, 3378.0 us)
Sparse Core Ops, SparseCore 0:
  174.9 220.8 all-gather.1
  659.0 259.2 reduce-scatter.1

commit v3 on v2

--- a/solution.py
+++ b/solution.py
@@ -289,8 +289,6 @@
 NZ, NY, NX = 4, 2, 2
 VMEM_LIMIT = 48 * 1024 * 1024
 EXPERT_VMEM = 60 * 1024 * 1024
-WINDOW = 5
-UPSTREAM_AT = 1
 
 
 def chip(z, y, x):
@@ -324,25 +322,12 @@
     return (rows // 2 + 15) // 16 * 16
 
 
-def after(values, *earlier):
-    return lax.optimization_barrier((values, *earlier))[0]
-
-
-class Line:
-    def __init__(self):
-        self.sent, self.held = [], []
-
-    def hold(self, *earlier):
-        self.held += earlier
-
-    def send(self, move, values):
-        if len(self.sent) >= WINDOW:
-            self.held.append(self.sent[-WINDOW])
-        if self.held:
-            values = after(values, *self.held)
-            self.held = []
-        self.sent.append(move(values))
-        return self.sent[-1]
+def tie(*values):
+    return lax.optimization_barrier(values)
+
+
+def without(kernel, start, count):
+    return lambda *refs: kernel(*refs[:start], *refs[start + count :])
 
 
 def gather_z(block):
@@ -369,32 +354,20 @@
 
 
 class Reduce:
-    def __init__(self, line):
-        self.line, self.planes, self.open, self.steps = line, {}, None, 0
-        self.total = None
-
-    def add(self, step, parts):
-        by_x = self.line.send(move_x, parts[3])
-        by_y = self.line.send(move_y, parts[4])
-        self.finish_plane()
-        self.open = (step, parts, by_x, by_y)
-        self.push()
-
-    def ways(self):
-        return self.open[2:]
-
-    def finish_plane(self):
-        if self.open is None:
-            return
-        step, (own, for_x, for_y, *_), by_x, by_y = self.open
+    def __init__(self):
+        self.planes, self.steps, self.total = {}, 0, None
+
+    def across(self, low, high):
+        return move_x(low), move_y(high)
+
+    def finish(self, steps, own, for_x, for_y, by_x, by_y):
         low = own.dtype
         cut = by_x.shape[0]
         for_y = jnp.concatenate([add_f32(for_y[:cut], by_x).astype(low), for_y[cut:]], axis=0)
         for_x = jnp.concatenate([for_x[:cut], add_f32(for_x[cut:], by_y).astype(low)], axis=0)
-        from_x = self.line.send(move_x, for_x)
-        from_y = self.line.send(move_y, for_y)
-        self.planes[step] = add_f32(own, from_x) + from_y.astype(jnp.float32)
-        self.open = None
+        total = add_f32(own, move_x(for_x)) + move_y(for_y).astype(jnp.float32)
+        for step, part in zip(steps, jnp.split(total, len(steps), axis=0), strict=True):
+            self.planes[step] = part
 
     def push(self):
         while self.steps + 1 < NZ and self.steps + 1 in self.planes:
@@ -402,10 +375,9 @@
             total = self.planes[self.steps]
             if self.total is not None:
                 total = add_f32(self.total, total)
-            self.total = self.line.send(move_z, total.astype(jnp.bfloat16))
+            self.total = move_z(total.astype(jnp.bfloat16))
 
     def result(self):
-        self.finish_plane()
         self.push()
         return add_f32(self.total, self.planes[0])
 
@@ -473,15 +445,19 @@
             )
 
 
-def apply_weight(position, values, pieces, rows, slot, back=False):
+def apply_weight(position, values, pieces, rows, slot, back=False, waits=()):
     tokens, width = values.shape
     return pl.pallas_call(
-        functools.partial(
-            apply_back_kernel if back else apply_kernel, rows=rows, slot=slot, tile=512
+        without(
+            functools.partial(
+                apply_back_kernel if back else apply_kernel, rows=rows, slot=slot, tile=512
+            ),
+            2 + len(pieces),
+            len(waits),
         ),
         out_shape=jax.ShapeDtypeStruct((tokens, width), jnp.float32),
         in_specs=[pl.BlockSpec(memory_space=pltpu.SMEM), pl.BlockSpec(memory_space=pltpu.VMEM)]
-        + [pl.BlockSpec(memory_space=pl.ANY)] * len(pieces),
+        + [pl.BlockSpec(memory_space=pl.ANY)] * (len(pieces) + len(waits)),
         out_specs=pl.BlockSpec(memory_space=pltpu.VMEM),
         scratch_shapes=[
             pltpu.VMEM((2, width // 2, width), jnp.bfloat16),
@@ -493,47 +469,65 @@
             bytes_accessed=2 * width * width + 6 * tokens * width,
             transcendentals=0,
         ),
-    )(position, values, *pieces)
-
-
-def weight_grad_kernel(position, own_left, other_left, *refs, rows, count, tile, step):
-    grads, outs, stage = refs[: 2 * count], refs[2 * count : -1], refs[-1]
+    )(position, values, *pieces, *waits)
+
+
+def weight_grad_kernel(position, *refs, rows, lefts, steps, tile):
+    count = len(lefts)
+    turned, grads = refs[: 2 * max(lefts) + 2], refs[2 * max(lefts) + 2 :]
+    grads, (own, for_x, for_y, *across, stage) = grads[: 2 * count], grads[2 * count :]
     span = NY * NX * rows
-    z_of = (position[1] + NZ - step) % NZ
-    lines = pl.ds(pl.multiple_of(z_of * span, span), span)
-    own, other = own_left[lines, :], other_left[lines, :]
-    for i in range(count):
-
-        @pl.loop(0, grads[0].shape[1] // tile)
-        def _(j):
-            part = pl.ds(pl.multiple_of(j * tile, tile), tile)
-            product = jnp.dot(
-                own, grads[2 * i][:, part], preferred_element_type=jnp.float32
-            ) + jnp.dot(other, grads[2 * i + 1][:, part], preferred_element_type=jnp.float32)
-            stage[...] = product.astype(stage.dtype)
-            for k in range(NY * NX):
-                place = pl.multiple_of(place_of(position, k) * rows, rows)
-                outs[k][pl.ds(i * rows, rows), part] = stage[pl.ds(place, rows), :]
-
-
-def weight_grad_parts(position, own_left, other_left, grads, rows, step):
-    count, width = len(grads) // 2, grads[0].shape[1]
-    tokens, tile = own_left.shape[1], 512
-    block = jax.ShapeDtypeStruct((count * rows, width), jnp.bfloat16)
+    for p, step in enumerate(steps):
+        z_of = (position[1] + NZ - step) % NZ
+        lines = pl.ds(pl.multiple_of(z_of * span, span), span)
+        for i, left in enumerate(lefts):
+            low = p * count * rows + i * rows
+            targets = [(own, low), (for_x, low), (for_y, low), (across[p], i * rows)]
+
+            @pl.loop(0, grads[0].shape[1] // tile)
+            def _(j):
+                part = pl.ds(pl.multiple_of(j * tile, tile), tile)
+                product = jnp.dot(
+                    turned[2 * left][lines, :],
+                    grads[2 * i][:, part],
+                    preferred_element_type=jnp.float32,
+                ) + jnp.dot(
+                    turned[2 * left + 1][lines, :],
+                    grads[2 * i + 1][:, part],
+                    preferred_element_type=jnp.float32,
+                )
+                stage[...] = product.astype(stage.dtype)
+                for k, (target, at) in enumerate(targets):
+                    place = pl.multiple_of(place_of(position, k) * rows, rows)
+                    target[pl.ds(at, rows), part] = stage[pl.ds(place, rows), :]
+
+
+def weight_grad_parts(position, turned, grads, lefts, rows, steps, waits=()):
+    count, width = len(lefts), grads[0].shape[1]
+    tokens, tile = turned[0].shape[1], 512
+    vmem_spec = pl.BlockSpec(memory_space=pltpu.VMEM)
+    both = jax.ShapeDtypeStruct((2 * count * rows, width), jnp.bfloat16)
+    one = jax.ShapeDtypeStruct((count * rows, width), jnp.bfloat16)
+    operands = [*turned, *grads]
     return pl.pallas_call(
-        functools.partial(weight_grad_kernel, rows=rows, count=count, tile=tile, step=step),
-        out_shape=[block] * (NY * NX),
+        without(
+            functools.partial(weight_grad_kernel, rows=rows, lefts=lefts, steps=steps, tile=tile),
+            1 + len(operands),
+            len(waits),
+        ),
+        out_shape=[both] * 3 + [one] * 2,
         in_specs=[pl.BlockSpec(memory_space=pltpu.SMEM)]
-        + [pl.BlockSpec(memory_space=pltpu.VMEM)] * (2 + len(grads)),
-        out_specs=[pl.BlockSpec(memory_space=pltpu.VMEM)] * (NY * NX),
+        + [vmem_spec] * len(operands)
+        + [pl.BlockSpec(memory_space=pl.ANY)] * len(waits),
+        out_specs=[vmem_spec] * 5,
         scratch_shapes=[pltpu.VMEM((NY * NX * rows, tile), jnp.bfloat16)],
         compiler_params=pltpu.CompilerParams(vmem_limit_bytes=VMEM_LIMIT),
         cost_estimate=pl.CostEstimate(
-            flops=4 * count * tokens * NY * NX * rows * width,
-            bytes_accessed=2 * count * NY * NX * rows * width + 4 * tokens * width * (count + 1),
+            flops=8 * count * tokens * NY * NX * rows * width,
+            bytes_accessed=4 * count * NY * NX * rows * width + 4 * tokens * width * (count + 1),
             transcendentals=0,
         ),
-    )(position, own_left, other_left, *grads)
+    )(position, *operands, *waits)
 
 
 def column_grad_kernel(position, *refs):
@@ -550,7 +544,7 @@
         out[...] = total.astype(out.dtype)
 
 
-def column_grads(position, acts, grads):
+def column_grads(position, acts, grads, waits=()):
     parts = len(acts)
     count, width = acts[0].shape
     units = grads[0].shape[1]
@@ -558,12 +552,13 @@
     whole = pl.BlockSpec((count, units), lambda i: (0, 0), pipeline_mode=pl.Buffered(1))
     out = pl.BlockSpec((tile, units // 2), lambda i: (i, 0))
     return pl.pallas_call(
-        column_grad_kernel,
+        without(column_grad_kernel, 1 + 2 * parts, len(waits)),
         grid=(width // tile,),
         out_shape=[jax.ShapeDtypeStruct((width, units // 2), t) for t in (jnp.float32, jnp.bfloat16)],
         in_specs=[pl.BlockSpec(memory_space=pltpu.SMEM)]
         + [pl.BlockSpec((count, tile), lambda i: (0, i))] * parts
-        + [whole] * parts,
+        + [whole] * parts
+        + [pl.BlockSpec(memory_space=pl.ANY)] * len(waits),
         out_specs=[out] * 2,
         compiler_params=pltpu.CompilerParams(vmem_limit_bytes=EXPERT_VMEM),
         cost_estimate=pl.CostEstimate(
@@ -571,7 +566,7 @@
             bytes_accessed=2 * parts * count * (width + units) + 3 * width * units,
             transcendentals=0,
         ),
-    )(position, *acts, *grads)
+    )(position, *acts, *grads, *waits)
 
 
 def down_grad_kernel(position, *refs):
@@ -606,7 +601,7 @@
             other[:, columns] = total.astype(other.dtype)
 
 
-def down_grads(position, hiddens, grads):
+def down_grads(position, hiddens, grads, waits=()):
     parts = len(hiddens)
     count, units = hiddens[0].shape
     width = grads[0].shape[1]
@@ -614,7 +609,7 @@
     half = units // 2 // tile
     whole = pl.BlockSpec((count, width), lambda i, at: (0, 0), pipeline_mode=pl.Buffered(1))
     return pl.pallas_call(
-        down_grad_kernel,
+        without(down_grad_kernel, 1 + 2 * parts, len(waits)),
         grid_spec=pltpu.PrefetchScalarGridSpec(
             num_scalar_prefetch=1,
             grid=(2 * half,),
@@ -622,7 +617,8 @@
                 pl.BlockSpec((count, tile), lambda i, at: (0, (i + at[0] * half) % (2 * half)))
             ]
             * parts
-            + [whole] * parts,
+            + [whole] * parts
+            + [pl.BlockSpec(memory_space=pl.ANY)] * len(waits),
             out_specs=[
                 pl.BlockSpec((tile, width), lambda i, at: (jnp.minimum(i, half - 1), 0)),
                 pl.BlockSpec((tile, width), lambda i, at: (jnp.maximum(i - half, 0), 0)),
@@ -639,7 +635,7 @@
             bytes_accessed=2 * parts * count * (width + units) + 3 * width * units,
             transcendentals=0,
         ),
-    )(position, *hiddens, *grads)
+    )(position, *hiddens, *grads, *waits)
 
 
 def gather_weights(blocks):
@@ -682,11 +678,11 @@
     places = [(y_at ^ (k >> 1)) * NX + (x_at ^ (k & 1)) for k in range(plane)]
     planes = [(z_at + NZ - s) % NZ for s in range(NZ)]
 
-    line = Line()
     pieces_qk = gather_weights([w_query, w_key])
     pieces_vo = gather_weights([w_value, w_output])
+    upstream, pieces_vo[0] = tie(cotangent, pieces_vo[0])
     upstream_all = lax.all_gather(
-        after(cotangent, pieces_vo[UPSTREAM_AT]), "expert", axis=0, tiled=True
+        upstream, "expert", axis=0, tiled=True
     ).reshape(NZ, plane * tokens_here, model_width)
 
     expert_ids = jnp.arange(experts_all, dtype=jnp.int32)
@@ -715,7 +711,9 @@
     ).T
     query_pre = apply_weight(position, act_attn, pieces_qk, rows, 0)
     key_pre = apply_weight(position, act_attn, pieces_qk, rows, 1)
-    value_low = apply_weight(after(position, small), act_attn, pieces_vo, rows, 0).astype(bf16)
+    value_low = apply_weight(
+        position, act_attn, pieces_vo, rows, 0, waits=(small,)
+    ).astype(bf16)
     query_normed, query_inverse = norm_forward(query_pre, query_gain)
     key_normed, key_inverse = norm_forward(key_pre, key_gain)
     cosine, sine_table = rotary_tables(tokens_here, head_dim)
@@ -748,15 +746,12 @@
 
     gate_w, up_w, down_w = w_gate[0], w_up[0], w_down[0]
     mine = (expert_ids == here).astype(f32)
-    forward, backward, ways = [], [], []
-    all_outs = jnp.zeros((NZ, plane * tokens_here, model_width), bf16)
+    forward, backward = [], []
     for s, pieces in enumerate(gather_chips(act_moe)):
         act_rows = jnp.zeros((plane, tokens_here, model_width), bf16)
         for k in range(plane):
             act_rows = lax.dynamic_update_slice(act_rows, pieces[k][None], (places[k], 0, 0))
         act_rows = act_rows.reshape(plane * tokens_here, model_width)
-        if s:
-            act_rows = after(act_rows, expert_out)
         used = lax.dynamic_index_in_dim(used_here, planes[s], axis=0, keepdims=False)
         probs_rows = jax.nn.softmax(
             jnp.dot(act_rows, full_router, preferred_element_type=f32), axis=-1
@@ -769,15 +764,14 @@
         hidden_low = (swish * up_pre).astype(bf16)
         expert_out = jnp.dot(hidden_low, down_w, preferred_element_type=f32).astype(bf16)
         out_low = (gate_rows * expert_out.astype(f32)).astype(bf16)
-        all_outs = lax.dynamic_update_slice(all_outs, out_low[None], (planes[s], 0, 0))
-        forward.append((act_rows, used, gate_rows, gate_pre, up_pre, hidden_low, expert_out))
-    rows_reduce = Reduce(line)
+        forward.append((act_rows, used, gate_rows, gate_pre, up_pre, hidden_low, expert_out, out_low))
+    rows_reduce = Reduce()
     choice_rows = jnp.zeros((NZ, plane * tokens_here, 1), f32)
     for s in range(NZ):
-        act_rows, used, gate_rows, gate_pre, up_pre, hidden_low, expert_out = forward[s]
+        act_rows, used, gate_rows, gate_pre, up_pre, hidden_low, expert_out, _ = forward[s]
         upstream_rows = lax.dynamic_index_in_dim(upstream_all, planes[s], axis=0, keepdims=False)
-        if s:
-            upstream_rows = after(upstream_rows, row_grad)
+        if s == NZ - 1:
+            upstream_rows, rows_reduce.planes[0] = tie(upstream_rows, rows_reduce.planes[0])
         upstream_f32 = upstream_rows.astype(f32)
         dots = jnp.sum(upstream_f32 * expert_out.astype(f32), axis=-1, keepdims=True) * used
         choice_rows = lax.dynamic_update_slice(choice_rows, dots[None], (planes[s], 0, 0))
@@ -790,6 +784,9 @@
         row_grad = (
             times_transposed(gate_pre_grad, gate_w) + times_transposed(up_pre_grad, up_w)
         ).astype(bf16)
+        if s == NZ - 1:
+            tied = tie(row_grad, *[chunk[7] for chunk in forward])
+            row_grad, out_lows = tied[0], tied[1:]
         blocks = row_grad.reshape(plane, tokens_here, model_width)
         own, for_x, for_y, across = [
             lax.dynamic_index_in_dim(blocks, places[k], axis=0, keepdims=False)
@@ -797,15 +794,24 @@
         ]
         cut = split_row(tokens_here)
         backward.append((out_grad, gate_pre_grad, up_pre_grad))
-        rows_reduce.add(s, [own, for_x, for_y, across[:cut], across[cut:]])
-        ways.append(rows_reduce.ways())
+        ways = rows_reduce.across(across[:cut], across[cut:])
+        if s:
+            rows_reduce.finish([s - 1], *opened)
+        opened = (own, for_x, for_y, *ways)
+    rows_reduce.finish([NZ - 1], *opened)
     choice_grad = lax.all_to_all(
         choice_rows.reshape(owners, tokens_here), "expert", split_axis=0, concat_axis=0, tiled=True
     ).T
-    own_down, other_down = down_grads(
-        after(position, *ways[3]), [chunk[5] for chunk in forward], [chunk[0] for chunk in backward]
-    )
-    moe_in_grad = after(rows_reduce.result(), own_down, other_down)
+    all_outs = jnp.zeros((NZ, plane * tokens_here, model_width), bf16)
+    for s in range(NZ):
+        all_outs = lax.dynamic_update_slice(all_outs, out_lows[s][None], (planes[s], 0, 0))
+    expert_acts = [chunk[0] for chunk in forward]
+    gate_grads = [chunk[1] for chunk in backward]
+    moe_in_grad = rows_reduce.result()
+    own_gate, other_gate = column_grads(
+        position, expert_acts, gate_grads, waits=(rows_reduce.planes[3],)
+    )
+    moe_in_grad, own_gate, all_outs = tie(moe_in_grad, own_gate, all_outs)
 
     logit_grad = router_probs * (
         choice_grad - jnp.sum(router_probs * choice_grad, axis=-1, keepdims=True)
@@ -818,7 +824,7 @@
     mid_grad = upstream + mid_norm_grad
     mid_low = mid_grad.astype(bf16)
     moe_term = lax.psum_scatter(
-        after(all_outs, moe_in_grad).reshape(-1, model_width), "expert", scatter_dimension=0, tiled=True
+        all_outs.reshape(-1, model_width), "expert", scatter_dimension=0, tiled=True
     ).astype(f32)
     own_attended = lax.dynamic_slice_in_dim(attended_low, core * half_width, half_width, axis=1).T
     other_attended = move_core(
@@ -851,34 +857,33 @@
     attn_grads = []
     for low in (query_low, key_low, value_grad):
         attn_grads += [low, move_core(low)]
-    output_grads = [mid_low, move_core(mid_low)]
-    weights_reduce = Reduce(line)
-    ways = []
-    for s in (1, 2, 3, 0):
-        at = after(position, *ways[-2]) if len(ways) > 1 else position
-        attn_parts = weight_grad_parts(at, own_act, other_act, attn_grads, rows, s)
-        output_parts = weight_grad_parts(at, own_attended, other_attended, output_grads, rows, s)
-        own_part, for_x, for_y, across = [
-            jnp.concatenate(pair, axis=0) for pair in zip(attn_parts, output_parts, strict=True)
-        ]
-        weights_reduce.add(s, [own_part, for_x, for_y, *jnp.split(across, 2, axis=0)])
-        ways.append(weights_reduce.ways())
+    weights_reduce = Reduce()
+    turned = [own_act, other_act, own_attended, other_attended]
+    attn_grads += [mid_low, move_core(mid_low)]
+    lefts = (0, 0, 0, 1)
+    first = weight_grad_parts(position, turned, attn_grads, lefts, rows, (1, 2))
+    first_ways = weights_reduce.across(*first[3:])
+    last = weight_grad_parts(position, turned, attn_grads, lefts, rows, (3, 0))
+    last_ways = weights_reduce.across(*last[3:])
+    weights_reduce.finish([1, 2], *first[:3], *first_ways)
+    act_grad = (
+        apply_weight(position, query_low, pieces_qk, rows, 0, back=True, waits=first_ways)
+        + apply_weight(position, key_low, pieces_qk, rows, 1, back=True, waits=first_ways)
+        + apply_weight(position, value_grad, pieces_vo, rows, 0, back=True, waits=first_ways)
+    )
+    up_grads = [chunk[2] for chunk in backward]
+    own_up, other_up = column_grads(position, expert_acts, up_grads, waits=(act_grad,))
+    weights_reduce.push()
+    weights_reduce.finish([3, 0], *last[:3], *last_ways)
+    own_down, other_down = down_grads(
+        position,
+        [chunk[5] for chunk in forward],
+        [chunk[0] for chunk in backward],
+        waits=(weights_reduce.planes[1], own_up),
+    )
+    weight_sums, moe_term = tie(weights_reduce.result(), moe_term)
     query_weight_grad, key_weight_grad, value_weight_grad, output_grad = jnp.split(
-        weights_reduce.result(), 4, axis=0
-    )
-    sums = weights_reduce.planes
-    later = after(position, *attn_parts, *output_parts, sums[1])
-    act_grad = (
-        apply_weight(later, query_low, pieces_qk, rows, 0, back=True)
-        + apply_weight(later, key_low, pieces_qk, rows, 1, back=True)
-        + apply_weight(later, value_grad, pieces_vo, rows, 0, back=True)
-    )
-    expert_acts = [chunk[0] for chunk in forward]
-    own_gate, other_gate = column_grads(
-        after(later, act_grad, sums[2]), expert_acts, [chunk[1] for chunk in backward]
-    )
-    own_up, other_up = column_grads(
-        after(later, own_gate, sums[3]), expert_acts, [chunk[2] for chunk in backward]
+        weight_sums, 4, axis=0
     )
     input_norm_grad, attn_gain_grad = norm_backward(inputs_f32, inverse_attn, attn_gain, act_grad)
     input_grad = (mid_grad + input_norm_grad).astype(bf16)
@@ -902,7 +907,7 @@
     )
 
     block_out = (middle + moe_term).astype(bf16)
-    down_grad = after(own_down, sums[2]) + move_core(after(other_down, sums[1])).astype(f32)
+    down_grad = own_down + move_core(other_down).astype(f32)
     gate_weight_grad = own_gate + move_core(other_gate).astype(f32)
     up_weight_grad = own_up + move_core(other_up).astype(f32)
     return (

time: 987 us -> 994 us (level)
  starting transfers between devices: 143 us -> 116 us
  local copies, waits for them, and re-layouts: 73.9 us -> 97 us
  waiting for transfers between devices: 328 us -> 350 us
  other arithmetic: 123 us -> 102 us
  matrix products: 141 us -> 159 us
    ppermute x15, waiting for transfers between devices: 17.8 us -> 40.5 us  [move_z(): return lax.ppermute(values, 'expert', Z_PAIRS)]
    dot_general x4, matrix products: 19.8 us -> 33.8 us  [body_dense(): jnp.dot(hidden_low, down_w, preferred_element_type=f32).astype(bf16)]
    ppermute x40 -> x36, waiting for transfers between devices: 110 us -> 97.1 us  [move_x(): return lax.ppermute(values, 'expert', X_PAIRS)]
    unnamed x334 -> x304, local copies, waits for them, and re-layouts: 24 us -> 35.9 us
    dynamic_update_slice x4 -> x0, other arithmetic: 11.1 us -> none  [body_dense(): lax.dynamic_update_slice(all_outs, out_low[None], (planes[s], 0, 0))]
    dynamic_update_slice x0 -> x4, local copies, waits for them, and re-layouts: none -> 10.3 us  [body_dense(): lax.dynamic_update_slice(all_outs, out_lows[s][None], (planes[s], 0, 0))]
    ppermute x40 -> x36, starting transfers between devices: 47.2 us -> 37.4 us  [move_y(): return lax.ppermute(values, 'expert', Y_PAIRS)]
    convert_element_type x17 -> x14, other arithmetic: 25.2 us -> 18.2 us  [the longest x4 8.68 us: push(): self.total = move_z(total.astype(jnp.bfloat16))]
  transfers between devices with their start and end apart: 118 -> 110, of which waited for: 53 -> 44; matrix products, arithmetic and copies ran while one was open for 27% -> 26% of each run, Pallas kernels for 16% -> 15%
where the time goes in v3:
time: 994 us; the launch traced here: 986 us
  waiting for transfers between devices  350 us (35%)
  matrix products  159 us (16%)
  Pallas kernels  146 us (15%)
  starting transfers between devices  116 us (12%)
  other arithmetic  102 us (10%)
  local copies, waits for them, and re-layouts  97 us (10%)
  between operations  17 us (2%)
    ppermute x36, waiting for transfers between devices, move_y(): return lax.ppermute(values, 'expert', Y_PAIRS)  199 us
    ppermute x36, waiting for transfers between devices, move_x(): return lax.ppermute(values, 'expert', X_PAIRS)  97.1 us
    dot_general x13, matrix products, times_transposed(): jnp.einsum('ta,ba->tb', left, right, preferred_element_type=jnp.float32)  63.1 us
    pallas_call x8, Pallas kernels, apply_weight(): pl.pallas_call(without(functools.partial(apply_back_kernel if back else a...  50.6 us
    ppermute x36, starting transfers between devices, move_x(): return lax.ppermute(values, 'expert', X_PAIRS)  42.5 us
    ppermute x15, waiting for transfers between devices, move_z(): return lax.ppermute(values, 'expert', Z_PAIRS)  40.5 us
    pallas_call x2, Pallas kernels, column_grads(): pl.pallas_call(without(column_grad_kernel, 1 + 2 * parts, len(waits)), gr...  38.4 us
    ppermute x36, starting transfers between devices, move_y(): return lax.ppermute(values, 'expert', Y_PAIRS)  37.4 us
  transfers between devices with their start and end apart: 110, of which 44 were waited for; matrix products, arithmetic and copies ran while one was open for 26% of the time, Pallas kernels for 15%

profile of v3, /device:TPU:0, one launch (start us, length us, event | category | flops | bytes accessed | tf_op | source)
XLA Modules:
  0.0 986.1 jit_solution(11613810824094805411)
XLA Ops:
  19.4 7.7 collective-permute-done.1
  29.2 8.3 collective-permute-done.27
  71.2 7.7 collective-permute-done.6
  98.0 11.7 %collective-permute-done.34 = bf16[128,2048]{1,0:T(8,128)(2,1)S(1)} collective-permute-done((bf16[128,2048]{1,0:T(8,128)(2,1)}, bf16[128,2048]{1,0:T(8,128)(2,1)S(1)}, u32[]{:S(2)}, u32[]{:S(2)}) %collective-permute-start.34) | collective-permute-done | bytes 524320 | tf_op jit(solution)/shard_map/ppermute | solution.py:310
  118.7 14.1 %collective-permute-done.35 = bf16[64,2048]{1,0:T(8,128)(2,1)S(1)} collective-permute-done((bf16[64,2048]{1,0:T(8,128)(2,1)S(1)}, bf16[64,2048]{1,0:T(8,128)(2,1)S(1)}, u32[]{:S(2)}, u32[]{:S(2)}) %collective-permute-start.35) | collective-permute-done | bytes 262176 | tf_op jit(solution)/shard_map/ppermute | solution.py:306
  142.0 18.5 %collective-permute-done.12 = bf16[64,2048]{1,0:T(8,128)(2,1)S(1)} collective-permute-done((bf16[64,2048]{1,0:T(8,128)(2,1)S(1)}, bf16[64,2048]{1,0:T(8,128)(2,1)S(1)}, u32[]{:S(2)}, u32[]{:S(2)}) %collective-permute-start.12) | collective-permute-done | bytes 262176 | tf_op jit(solution)/shard_map/ppermute | solution.py:306
  180.7 9.3 collective-permute-done.40
  196.1 7.9 collective-permute-done.17
  269.9 14.7 %collective-permute-done.75 = bf16[192,2048]{1,0:T(8,128)(2,1)} collective-permute-done((bf16[192,2048]{1,0:T(8,128)(2,1)}, bf16[192,2048]{1,0:T(8,128)(2,1)}, u32[]{:S(2)}, u32[]{:S(2)}) %collective-permute-start.75) | collective-permute-done | bytes 786464 | tf_op jit(solution)/shard_map/ppermute | solution.py:310
  334.9 6.7 collective-permute-done.61
  346.5 7.3 collective-permute-done.62
  384.0 8.6 fusion.62
  401.3 8.3 multiply_convert_fusion.3
  468.6 16.0 %fusion.15 = (f32[768]{0:T(1024)S(1)}, f32[768]{0:T(1024)S(1)}, f32[768]{0:T(1024)S(1)}, bf16[768,2048]{1,0:T(8,128)(2,1)}, bf16[768,2048]{1,0:T(8,128)(2,1)}, /...) fusion(bf16[4,768,2048]{2,1,0:T(8,128)(2,1)} %bitcast.527, ...), kind=kOutput, calls=%fused_computation.30 | convolution fusion | flops 3260544768 | bytes 40388620 | tf_op jit(solution)/shard_map/dot_general | solution.py:765
  501.4 8.8 collective-permute-done.81
  524.3 7.8 multiply_convert_fusion.1
  537.9 6.8 add_convert_fusion
  544.7 8.3 fusion.17
  586.6 13.2 %collective-permute-done.68 = bf16[192,2048]{1,0:T(8,128)(2,1)S(1)} collective-permute-done((bf16[192,2048]{1,0:T(8,128)(2,1)S(1)}, bf16[192,2048]{1,0:T(8,128)(2,1)S(1)}, u32[]{:S(2)}, u32[]{:S(2)}) %collective-permute-start.68) | collective-permute-done | bytes 786464 | tf_op jit(solution)/shard_map/ppermute | solution.py:314
  601.8 19.2 %shard_map.267 = (f32[2048,512]{1,0:T(8,128)}, bf16[2048,512]{1,0:T(8,128)(2,1)}) custom-call(s32[5]{0:T(128)} %copy-done.17, bf16[768,2048]{1,0:T(8,128)(2,1)} %bitcast.478, bf16[768,2048]{1,0:T(8,128)(2,1)} %bitcast.483, bf16[768,2048]{1,0:T(8,128)(2,1)} %bitcast.488, bf16[768,2048]{1,0:T(8,128)(2,1)} %bitcast.493, bf16[768,1024]{1,0:T(8,128)(2,1)} %copy-done.139, ...), custom_call_target="tpu_custom_call" | custom-call | flops 12884901888 | bytes 25165824 | tf_op jit(solution)/shard_map/pallas_call | solution.py:554
  635.5 7.4 all-to-all-done.1
  648.2 6.7 shard_map.268
  675.7 15.6 %shard_map.269 = (bf16[512,2048]{1,0:T(8,128)(2,1)}, bf16[512,2048]{1,0:T(8,128)(2,1)}, bf16[512,2048]{1,0:T(8,128)(2,1)}, bf16[256,2048]{1,0:T(8,128)(2,1)}, bf16[256,2048]{1,0:T(8,128)(2,1)}) custom-call(s32[5]{0:T(128)S(1)} %copy-done.18, bf16[1024,192]{1,0:T(8,128)(2,1)S(1)} %copy-done.11, bf16[1024,192]{1,0:T(8,128)(2,1)S(1)} %copy-done.13, ...), custom_call_target="tpu_custom_call" | custom-call | flops 3221225472 | bytes 16252928 | tf_op jit(solution)/shard_map/pallas_call | solution.py:512
  703.0 15.5 %shard_map.270 = (bf16[512,2048]{1,0:T(8,128)(2,1)}, bf16[512,2048]{1,0:T(8,128)(2,1)}, bf16[512,2048]{1,0:T(8,128)(2,1)}, bf16[256,2048]{1,0:T(8,128)(2,1)}, bf16[256,2048]{1,0:T(8,128)(2,1)}) custom-call(s32[5]{0:T(128)S(1)} %copy-done.18, bf16[1024,192]{1,0:T(8,128)(2,1)S(1)} %copy-done.12, bf16[1024,192]{1,0:T(8,128)(2,1)S(1)} %copy-done.14, ...), custom_call_target="tpu_custom_call" | custom-call | flops 3221225472 | bytes 16252928 | tf_op jit(solution)/shard_map/pallas_call | solution.py:512
  733.6 51.8 %collective-permute-done.91.refs_11_ = bf16[256,2048]{1,0:T(8,128)(2,1)S(1)} collective-permute-done((bf16[256,2048]{1,0:T(8,128)(2,1)}, bf16[256,2048]{1,0:T(8,128)(2,1)S(1)}, u32[]{:S(2)}, u32[]{:S(2)}) %collective-permute-start.91) | collective-permute-done | bytes 1048608 | tf_op jit(solution)/shard_map/ppermute | solution.py:310
  800.6 6.5 shard_map.272
  807.1 6.7 shard_map.271
  815.4 33.7 %collective-permute-done.94 = bf16[512,2048]{1,0:T(8,128)(2,1)S(1)} collective-permute-done((bf16[512,2048]{1,0:T(8,128)(2,1)}, bf16[512,2048]{1,0:T(8,128)(2,1)S(1)}, u32[]{:S(2)}, u32[]{:S(2)}) %collective-permute-start.94) | collective-permute-done | bytes 2097184 | tf_op jit(solution)/shard_map/ppermute | solution.py:310
  855.4 19.2 %shard_map.274 = (f32[2048,512]{1,0:T(8,128)}, bf16[2048,512]{1,0:T(8,128)(2,1)}) custom-call(s32[5]{0:T(128)} %copy-done.17, bf16[768,2048]{1,0:T(8,128)(2,1)} %bitcast.479, bf16[768,2048]{1,0:T(8,128)(2,1)} %bitcast.484, bf16[768,2048]{1,0:T(8,128)(2,1)} %bitcast.489, bf16[768,2048]{1,0:T(8,128)(2,1)} %bitcast.494, ...), custom_call_target="tpu_custom_call" | custom-call | flops 12884901888 | bytes 25165824 | tf_op jit(solution)/shard_map/pallas_call | solution.py:554
  879.5 21.4 %collective-permute-done.100 = bf16[512,2048]{1,0:T(8,128)(2,1)} collective-permute-done((bf16[512,2048]{1,0:T(8,128)(2,1)}, bf16[512,2048]{1,0:T(8,128)(2,1)}, u32[]{:S(2)}, u32[]{:S(2)}) %collective-permute-start.100) | collective-permute-done | bytes 2097184 | tf_op jit(solution)/shard_map/ppermute | solution.py:310
  911.7 25.8 %shard_map.275 = (f32[512,2048]{1,0:T(8,128)}, bf16[512,2048]{1,0:T(8,128)(2,1)}) custom-call(s32[5]{0:T(128)} %copy-done.17, bf16[768,1024]{1,0:T(8,128)(2,1)} %copy-done.146, bf16[768,1024]{1,0:T(8,128)(2,1)} %copy-done.145, bf16[768,1024]{1,0:T(8,128)(2,1)} %get-tuple-element.150.refs_3_, bf16[768,1024]{1,0:T(8,128)(2,1)} %copy-done.137, ...), custom_call_target="tpu_custom_call" | custom-call | flops 12884901888 | bytes 25165824 | tf_op jit(solution)/shard_map/pallas_call | solution.py:611
  950.6 17.4 %collective-permute-done.101 = bf16[256,2048]{1,0:T(8,128)(2,1)S(1)} collective-permute-done((bf16[256,2048]{1,0:T(8,128)(2,1)}, bf16[256,2048]{1,0:T(8,128)(2,1)S(1)}, u32[]{:S(2)}, u32[]{:S(2)}) %collective-permute-start.101) | collective-permute-done | bytes 1048608 | tf_op jit(solution)/shard_map/ppermute | solution.py:314
  (745 shorter events, 530.4 us)
Async XLA Ops:
  7.2 376.8 %all-gather.2.cloned.1.call-start = ((), (), s32[]{:S(2)}) async-start(), calls=%async_computation.4 | async-start | bytes 13369344 | tf_op jit(solution)/shard_map/all_gather | solution.py:684
  79.0 33.9 %collective-permute-start.11 = (bf16[128,2048]{1,0:T(8,128)(2,1)}, bf16[128,2048]{1,0:T(8,128)(2,1)S(1)}, u32[]{:S(2)}, u32[]{:S(2)}) collective-permute-start(bf16[128,2048]{1,0:T(8,128)(2,1)} %copy-done.89), channel_id=1, source_target_pairs={{0,2},{1,3},{2,0},{3,1},{4,6},{5,7},{6,4},{7,5},{8,10},{9,11},{10,... | collective-permute-start | bytes 1572872 | tf_op jit(solution)/shard_map/ppermute | solution.py:310
  79.5 35.0 %collective-permute-start.10 = (bf16[128,2048]{1,0:T(8,128)(2,1)}, bf16[128,2048]{1,0:T(8,128)(2,1)S(1)}, u32[]{:S(2)}, u32[]{:S(2)}) collective-permute-start(bf16[128,2048]{1,0:T(8,128)(2,1)} %copy-done.89), channel_id=1, source_target_pairs={{0,1},{1,0},{2,3},{3,2},{4,5},{5,4},{6,7},{7,6},{8,9},{9,8},{10,11... | collective-permute-start | bytes 1572872 | tf_op jit(solution)/shard_map/ppermute | solution.py:306
  81.0 35.0 %collective-permute-start.37 = (bf16[128,2048]{1,0:T(8,128)(2,1)}, bf16[128,2048]{1,0:T(8,128)(2,1)}, u32[]{:S(2)}, u32[]{:S(2)}) collective-permute-start(bf16[128,2048]{1,0:T(8,128)(2,1)} %collective-permute-done.32), channel_id=1, source_target_pairs={{0,4},{1,5},{2,6},{3,7},{4,8},{5,9},{6,10},{7,11},{8,12},{9,13},{1... | collective-permute-start | bytes 1572872 | tf_op jit(solution)/shard_map/ppermute | solution.py:314
  142.0 65.7 %collective-permute-start.42 = (bf16[4,128,2048]{2,1,0:T(8,128)(2,1)}, bf16[4,128,2048]{2,1,0:T(8,128)(2,1)}, u32[]{:S(2)}, u32[]{:S(2)}) collective-permute-start(bf16[4,128,2048]{2,1,0:T(8,128)(2,1)} %pad_maximum_fusion.4.refs_2_), channel_id=1, source_target_pairs={{0,16},{16,0},{1,17},{17,1},{2,18},{18,2},{3,19},{19,3},{4,20},{20... | collective-permute-start | bytes 6291464 | tf_op jit(solution)/shard_map/ppermute | solution.py:318
  160.5 47.7 %collective-permute-start.43 = (bf16[4,128,2048]{2,1,0:T(8,128)(2,1)}, bf16[4,128,2048]{2,1,0:T(8,128)(2,1)}, u32[]{:S(2)}, u32[]{:S(2)}) collective-permute-start(bf16[4,128,2048]{2,1,0:T(8,128)(2,1)} %pad_maximum_fusion.5.refs_3_), channel_id=1, source_target_pairs={{0,16},{16,0},{1,17},{17,1},{2,18},{18,2},{3,19},{19,3},{4,20},{20... | collective-permute-start | bytes 6291464 | tf_op jit(solution)/shard_map/ppermute | solution.py:318
  161.2 47.1 %collective-permute-start.44 = (bf16[4,128,2048]{2,1,0:T(8,128)(2,1)}, bf16[4,128,2048]{2,1,0:T(8,128)(2,1)}, u32[]{:S(2)}, u32[]{:S(2)}) collective-permute-start(bf16[4,128,2048]{2,1,0:T(8,128)(2,1)} %pad_maximum_fusion.6.refs_4_), channel_id=1, source_target_pairs={{0,16},{16,0},{1,17},{17,1},{2,18},{18,2},{3,19},{19,3},{4,20},{20... | collective-permute-start | bytes 6291464 | tf_op jit(solution)/shard_map/ppermute | solution.py:318
  204.0 30.4 %collective-permute-start.19 = (bf16[4,128,2048]{2,1,0:T(8,128)(2,1)S(1)}, bf16[4,128,2048]{2,1,0:T(8,128)(2,1)}, u32[]{:S(2)}, u32[]{:S(2)}) collective-permute-start(bf16[4,128,2048]{2,1,0:T(8,128)(2,1)S(1)} %pad_maximum_fusion.refs_2_), channel_id=1, source_target_pairs={{0,16},{16,0},{1,17},{17,1},{2,18},{18,2},{3,19},{19,3},{4,20},{20... | collective-permute-start | bytes 6291464 | tf_op jit(solution)/shard_map/ppermute | solution.py:318
  213.5 760.5 %reduce-scatter.2.cloned.1.call-start = ((), (), s32[]{:S(2)}) async-start(), calls=%async_computation.5 | async-start | bytes 13369344 | tf_op jit(solution)/shard_map/reduce_scatter | solution.py:826
  438.3 48.6 %collective-permute-start.78 = (bf16[96,2048]{1,0:T(8,128)(2,1)}, bf16[96,2048]{1,0:T(8,128)(2,1)}, u32[]{:S(2)}, u32[]{:S(2)}) collective-permute-start(bf16[96,2048]{1,0:T(8,128)(2,1)} %get-tuple-element.185), channel_id=1, source_target_pairs={{0,2},{1,3},{2,0},{3,1},{4,6},{5,7},{6,4},{7,5},{8,10},{9,11},{10,... | collective-permute-start | bytes 1179656 | tf_op jit(solution)/shard_map/ppermute | solution.py:310
  440.0 48.1 %collective-permute-start.80 = (bf16[96,2048]{1,0:T(8,128)(2,1)}, bf16[96,2048]{1,0:T(8,128)(2,1)}, u32[]{:S(2)}, u32[]{:S(2)}) collective-permute-start(bf16[96,2048]{1,0:T(8,128)(2,1)} %get-tuple-element.187), channel_id=1, source_target_pairs={{0,1},{1,0},{2,3},{3,2},{4,5},{5,4},{6,7},{7,6},{8,9},{9,8},{10,11... | collective-permute-start | bytes 1179656 | tf_op jit(solution)/shard_map/ppermute | solution.py:306
  455.4 35.6 %collective-permute-start.64 = (bf16[96,2048]{1,0:T(8,128)(2,1)}, bf16[96,2048]{1,0:T(8,128)(2,1)}, u32[]{:S(2)}, u32[]{:S(2)}) collective-permute-start(bf16[96,2048]{1,0:T(8,128)(2,1)} %get-tuple-element.179), channel_id=1, source_target_pairs={{0,2},{1,3},{2,0},{3,1},{4,6},{5,7},{6,4},{7,5},{8,10},{9,11},{10,... | collective-permute-start | bytes 1179656 | tf_op jit(solution)/shard_map/ppermute | solution.py:310
  457.1 34.5 %collective-permute-start.66 = (bf16[96,2048]{1,0:T(8,128)(2,1)}, bf16[96,2048]{1,0:T(8,128)(2,1)}, u32[]{:S(2)}, u32[]{:S(2)}) collective-permute-start(bf16[96,2048]{1,0:T(8,128)(2,1)} %get-tuple-element.181), channel_id=1, source_target_pairs={{0,1},{1,0},{2,3},{3,2},{4,5},{5,4},{6,7},{7,6},{8,9},{9,8},{10,11... | collective-permute-start | bytes 1179656 | tf_op jit(solution)/shard_map/ppermute | solution.py:306
  493.9 81.4 %collective-permute-start.67 = (bf16[192,2048]{1,0:T(8,128)(2,1)}, bf16[192,2048]{1,0:T(8,128)(2,1)}, u32[]{:S(2)}, u32[]{:S(2)}) collective-permute-start(bf16[192,2048]{1,0:T(8,128)(2,1)} %pad_maximum_fusion.15), channel_id=1, source_target_pairs={{0,2},{1,3},{2,0},{3,1},{4,6},{5,7},{6,4},{7,5},{8,10},{9,11},{10,... | collective-permute-start | bytes 2359304 | tf_op jit(solution)/shard_map/ppermute | solution.py:310
  496.0 79.3 %collective-permute-start.65 = (bf16[192,2048]{1,0:T(8,128)(2,1)}, bf16[192,2048]{1,0:T(8,128)(2,1)}, u32[]{:S(2)}, u32[]{:S(2)}) collective-permute-start(bf16[192,2048]{1,0:T(8,128)(2,1)} %pad_maximum_fusion.14), channel_id=1, source_target_pairs={{0,1},{1,0},{2,3},{3,2},{4,5},{5,4},{6,7},{7,6},{8,9},{9,8},{10,11... | collective-permute-start | bytes 2359304 | tf_op jit(solution)/shard_map/ppermute | solution.py:306
  500.4 54.6 %collective-permute-start.57 = (bf16[192,2048]{1,0:T(8,128)(2,1)S(1)}, bf16[192,2048]{1,0:T(8,128)(2,1)S(1)}, u32[]{:S(2)}, u32[]{:S(2)}) collective-permute-start(bf16[192,2048]{1,0:T(8,128)(2,1)S(1)} %pad_maximum_fusion.13), channel_id=1, source_target_pairs={{0,2},{1,3},{2,0},{3,1},{4,6},{5,7},{6,4},{7,5},{8,10},{9,11},{10,... | collective-permute-start | bytes 2359304 | tf_op jit(solution)/shard_map/ppermute | solution.py:310
  510.2 46.2 %collective-permute-start.55 = (bf16[192,2048]{1,0:T(8,128)(2,1)S(1)}, bf16[192,2048]{1,0:T(8,128)(2,1)S(1)}, u32[]{:S(2)}, u32[]{:S(2)}) collective-permute-start(bf16[192,2048]{1,0:T(8,128)(2,1)S(1)} %pad_maximum_fusion.12), channel_id=1, source_target_pairs={{0,1},{1,0},{2,3},{3,2},{4,5},{5,4},{6,7},{7,6},{8,9},{9,8},{10,11... | collective-permute-start | bytes 2359304 | tf_op jit(solution)/shard_map/ppermute | solution.py:306
  625.0 42.9 %collective-permute-start.46 = (bf16[192,1024]{1,0:T(8,128)(2,1)}, bf16[192,1024]{1,0:T(8,128)(2,1)}, u32[]{:S(2)}, u32[]{:S(2)}) collective-permute-start(bf16[192,1024]{1,0:T(8,128)(2,1)} %get-tuple-element.204), channel_id=1, source_target_pairs={{0,16},{16,0},{1,17},{17,1},{2,18},{18,2},{3,19},{19,3},{4,20},{20... | collective-permute-start | bytes 1179656 | tf_op jit(solution)/shard_map/ppermute | solution.py:318
  626.5 41.6 %collective-permute-start.47 = (bf16[192,1024]{0,1:T(8,128)(2,1)}, bf16[192,1024]{0,1:T(8,128)(2,1)}, u32[]{:S(2)}, u32[]{:S(2)}) collective-permute-start(bf16[192,1024]{0,1:T(8,128)(2,1)} %get-tuple-element.202), channel_id=1, source_target_pairs={{0,16},{16,0},{1,17},{17,1},{2,18},{18,2},{3,19},{19,3},{4,20},{20... | collective-permute-start | bytes 1179656 | tf_op jit(solution)/shard_map/ppermute | solution.py:318
  642.9 82.4 %collective-permute-start.102 = (bf16[2048,512]{1,0:T(8,128)(2,1)}, bf16[2048,512]{1,0:T(8,128)(2,1)}, u32[]{:S(2)}, u32[]{:S(2)}) collective-permute-start(bf16[2048,512]{1,0:T(8,128)(2,1)} %get-tuple-element.69), channel_id=1, source_target_pairs={{0,16},{16,0},{1,17},{17,1},{2,18},{18,2},{3,19},{19,3},{4,20},{20... | collective-permute-start | bytes 6291464 | tf_op jit(solution)/shard_map/ppermute | solution.py:318
  691.3 38.7 %collective-permute-start.93 = (bf16[256,2048]{1,0:T(8,128)(2,1)}, bf16[256,2048]{1,0:T(8,128)(2,1)S(1)}, u32[]{:S(2)}, u32[]{:S(2)}) collective-permute-start(bf16[256,2048]{1,0:T(8,128)(2,1)} %get-tuple-element.59), channel_id=1, source_target_pairs={{0,1},{1,0},{2,3},{3,2},{4,5},{5,4},{6,7},{7,6},{8,9},{9,8},{10,11... | collective-permute-start | bytes 3145736 | tf_op jit(solution)/shard_map/ppermute | solution.py:306
  721.6 69.3 %collective-permute-start.97 = (bf16[256,2048]{1,0:T(8,128)(2,1)}, bf16[256,2048]{1,0:T(8,128)(2,1)S(1)}, u32[]{:S(2)}, u32[]{:S(2)}) collective-permute-start(bf16[256,2048]{1,0:T(8,128)(2,1)} %get-tuple-element.62), channel_id=1, source_target_pairs={{0,2},{1,3},{2,0},{3,1},{4,6},{5,7},{6,4},{7,5},{8,10},{9,11},{10,... | collective-permute-start | bytes 3145736 | tf_op jit(solution)/shard_map/ppermute | solution.py:310
  722.1 66.3 %collective-permute-start.99 = (bf16[256,2048]{1,0:T(8,128)(2,1)}, bf16[256,2048]{1,0:T(8,128)(2,1)S(1)}, u32[]{:S(2)}, u32[]{:S(2)}) collective-permute-start(bf16[256,2048]{1,0:T(8,128)(2,1)} %get-tuple-element.64), channel_id=1, source_target_pairs={{0,1},{1,0},{2,3},{3,2},{4,5},{5,4},{6,7},{7,6},{8,9},{9,8},{10,11... | collective-permute-start | bytes 3145736 | tf_op jit(solution)/shard_map/ppermute | solution.py:306
  723.7 61.8 %collective-permute-start.91 = (bf16[256,2048]{1,0:T(8,128)(2,1)}, bf16[256,2048]{1,0:T(8,128)(2,1)S(1)}, u32[]{:S(2)}, u32[]{:S(2)}) collective-permute-start(bf16[256,2048]{1,0:T(8,128)(2,1)} %get-tuple-element.57), channel_id=1, source_target_pairs={{0,2},{1,3},{2,0},{3,1},{4,6},{5,7},{6,4},{7,5},{8,10},{9,11},{10,... | collective-permute-start | bytes 3145736 | tf_op jit(solution)/shard_map/ppermute | solution.py:310
  732.0 117.1 %collective-permute-start.94 = (bf16[512,2048]{1,0:T(8,128)(2,1)}, bf16[512,2048]{1,0:T(8,128)(2,1)S(1)}, u32[]{:S(2)}, u32[]{:S(2)}) collective-permute-start(bf16[512,2048]{1,0:T(8,128)(2,1)} %pad_maximum_fusion.9), channel_id=1, source_target_pairs={{0,2},{1,3},{2,0},{3,1},{4,6},{5,7},{6,4},{7,5},{8,10},{9,11},{10,... | collective-permute-start | bytes 6291464 | tf_op jit(solution)/shard_map/ppermute | solution.py:310
  787.4 61.8 %collective-permute-start.92 = (bf16[512,2048]{1,0:T(8,128)(2,1)}, bf16[512,2048]{1,0:T(8,128)(2,1)}, u32[]{:S(2)}, u32[]{:S(2)}) collective-permute-start(bf16[512,2048]{1,0:T(8,128)(2,1)} %pad_maximum_fusion.8), channel_id=1, source_target_pairs={{0,1},{1,0},{2,3},{3,2},{4,5},{5,4},{6,7},{7,6},{8,9},{9,8},{10,11... | collective-permute-start | bytes 6291464 | tf_op jit(solution)/shard_map/ppermute | solution.py:306
  790.4 110.5 %collective-permute-start.100 = (bf16[512,2048]{1,0:T(8,128)(2,1)}, bf16[512,2048]{1,0:T(8,128)(2,1)}, u32[]{:S(2)}, u32[]{:S(2)}) collective-permute-start(bf16[512,2048]{1,0:T(8,128)(2,1)} %pad_maximum_fusion.11), channel_id=1, source_target_pairs={{0,2},{1,3},{2,0},{3,1},{4,6},{5,7},{6,4},{7,5},{8,10},{9,11},{10,... | collective-permute-start | bytes 6291464 | tf_op jit(solution)/shard_map/ppermute | solution.py:310
  793.2 107.7 %collective-permute-start.98 = (bf16[512,2048]{1,0:T(8,128)(2,1)}, bf16[512,2048]{1,0:T(8,128)(2,1)}, u32[]{:S(2)}, u32[]{:S(2)}) collective-permute-start(bf16[512,2048]{1,0:T(8,128)(2,1)} %pad_maximum_fusion.10), channel_id=1, source_target_pairs={{0,1},{1,0},{2,3},{3,2},{4,5},{5,4},{6,7},{7,6},{8,9},{9,8},{10,11... | collective-permute-start | bytes 6291464 | tf_op jit(solution)/shard_map/ppermute | solution.py:306
  854.0 53.1 %collective-permute-start.95 = (bf16[256,2048]{1,0:T(8,128)(2,1)S(1)}, bf16[256,2048]{1,0:T(8,128)(2,1)}, u32[]{:S(2)}, u32[]{:S(2)}) collective-permute-start(bf16[256,2048]{1,0:T(8,128)(2,1)S(1)} %split.69), channel_id=1, source_target_pairs={{0,4},{1,5},{2,6},{3,7},{4,8},{5,9},{6,10},{7,11},{8,12},{9,13},{1... | collective-permute-start | bytes 3145736 | tf_op jit(solution)/shard_map/ppermute | solution.py:314
  875.6 67.8 %all-to-all-start.2 = ((f32[32,1,1280]{2,1,0:T(1,128)}), f32[32,1,1280]{2,1,0:T(1,128)S(1)}, u32[]{:S(2)}, u32[]{:S(2)}) async-start(f32[32,1,1280]{2,1,0:T(1,128)} %copy.134), calls=%async_computation.3 | async-start | bytes 327680 | tf_op jit(solution)/shard_map/all_to_all | solution.py:900
  879.2 65.7 %collective-permute-start.103 = (bf16[2048,512]{1,0:T(8,128)(2,1)}, bf16[2048,512]{1,0:T(8,128)(2,1)}, u32[]{:S(2)}, u32[]{:S(2)}) collective-permute-start(bf16[2048,512]{1,0:T(8,128)(2,1)} %get-tuple-element.71), channel_id=1, source_target_pairs={{0,16},{16,0},{1,17},{17,1},{2,18},{18,2},{3,19},{19,3},{4,20},{20... | collective-permute-start | bytes 6291464 | tf_op jit(solution)/shard_map/ppermute | solution.py:318
  937.5 32.2 %collective-permute-start.104 = (bf16[512,2048]{1,0:T(8,128)(2,1)}, bf16[512,2048]{1,0:T(8,128)(2,1)}, u32[]{:S(2)}, u32[]{:S(2)}) collective-permute-start(bf16[512,2048]{1,0:T(8,128)(2,1)} %get-tuple-element.73), channel_id=1, source_target_pairs={{0,16},{16,0},{1,17},{17,1},{2,18},{18,2},{3,19},{19,3},{4,20},{20... | collective-permute-start | bytes 6291464 | tf_op jit(solution)/shard_map/ppermute | solution.py:318
  (228 other events, 3149.3 us)
Sparse Core Ops, SparseCore 0:
  70.9 190.4 all-gather.1
  624.1 256.7 reduce-scatter.1

commit v4 on v3

--- a/solution.py
+++ b/solution.py
@@ -784,9 +784,6 @@
         row_grad = (
             times_transposed(gate_pre_grad, gate_w) + times_transposed(up_pre_grad, up_w)
         ).astype(bf16)
-        if s == NZ - 1:
-            tied = tie(row_grad, *[chunk[7] for chunk in forward])
-            row_grad, out_lows = tied[0], tied[1:]
         blocks = row_grad.reshape(plane, tokens_here, model_width)
         own, for_x, for_y, across = [
             lax.dynamic_index_in_dim(blocks, places[k], axis=0, keepdims=False)
@@ -804,7 +801,7 @@
     ).T
     all_outs = jnp.zeros((NZ, plane * tokens_here, model_width), bf16)
     for s in range(NZ):
-        all_outs = lax.dynamic_update_slice(all_outs, out_lows[s][None], (planes[s], 0, 0))
+        all_outs = lax.dynamic_update_slice(all_outs, forward[s][7][None], (planes[s], 0, 0))
     expert_acts = [chunk[0] for chunk in forward]
     gate_grads = [chunk[1] for chunk in backward]
     moe_in_grad = rows_reduce.result()

time: 994 us -> 970 us (0.976)
  local copies, waits for them, and re-layouts: 97 us -> 79.6 us
    ppermute x36, waiting for transfers between devices: 199 us -> 127 us  [move_y(): return lax.ppermute(values, 'expert', Y_PAIRS)]
    ppermute x36, waiting for transfers between devices: 97.1 us -> 157 us  [move_x(): return lax.ppermute(values, 'expert', X_PAIRS)]
    reduce_sum x0 -> x2, other arithmetic: none -> 11.7 us  [body_dense(): jnp.sum(upstream_f32 * expert_out.astype(f32), axis=-1, keepdims=True)]
    dynamic_update_slice x4 -> x0, local copies, waits for them, and re-layouts: 10.3 us -> none  [body_dense(): lax.dynamic_update_slice(all_outs, out_lows[s][None], (planes[s], 0, 0))]
    unnamed x304 -> x286, local copies, waits for them, and re-layouts: 35.9 us -> 28.6 us
  transfers between devices with their start and end apart: 110 -> 110, of which waited for: 44 -> 48; matrix products, arithmetic and copies ran while one was open for 26% -> 27% of each run, Pallas kernels for 15% -> 15%
where the time goes in v4:
time: 970 us; the launch traced here: 962 us
  waiting for transfers between devices  347 us (36%)
  matrix products  153 us (16%)
  Pallas kernels  146 us (15%)
  starting transfers between devices  114 us (12%)
  other arithmetic  104 us (11%)
  local copies, waits for them, and re-layouts  79.6 us (8%)
  between operations  17.2 us (2%)
    ppermute x36, waiting for transfers between devices, move_x(): return lax.ppermute(values, 'expert', X_PAIRS)  157 us
    ppermute x36, waiting for transfers between devices, move_y(): return lax.ppermute(values, 'expert', Y_PAIRS)  127 us
    dot_general x13, matrix products, times_transposed(): jnp.einsum('ta,ba->tb', left, right, preferred_element_type=jnp.float32)  62 us
    pallas_call x8, Pallas kernels, apply_weight(): pl.pallas_call(without(functools.partial(apply_back_kernel if back else a...  50.6 us
    ppermute x15, waiting for transfers between devices, move_z(): return lax.ppermute(values, 'expert', Z_PAIRS)  49.5 us
    ppermute x36, starting transfers between devices, move_y(): return lax.ppermute(values, 'expert', Y_PAIRS)  39.7 us
    pallas_call x2, Pallas kernels, column_grads(): pl.pallas_call(without(column_grad_kernel, 1 + 2 * parts, len(waits)), gr...  38.9 us
    ppermute x36, starting transfers between devices, move_x(): return lax.ppermute(values, 'expert', X_PAIRS)  38.6 us
  transfers between devices with their start and end apart: 110, of which 48 were waited for; matrix products, arithmetic and copies ran while one was open for 27% of the time, Pallas kernels for 15%

profile of v4, /device:TPU:0, one launch (start us, length us, event | category | flops | bytes accessed | tf_op | source)
XLA Modules:
  0.0 961.5 jit_solution(16668027818805373739)
XLA Ops:
  19.4 7.7 collective-permute-done.1
  29.2 8.3 collective-permute-done.27
  71.2 7.7 collective-permute-done.6
  98.0 11.7 %collective-permute-done.34 = bf16[128,2048]{1,0:T(8,128)(2,1)S(1)} collective-permute-done((bf16[128,2048]{1,0:T(8,128)(2,1)}, bf16[128,2048]{1,0:T(8,128)(2,1)S(1)}, u32[]{:S(2)}, u32[]{:S(2)}) %collective-permute-start.34) | collective-permute-done | bytes 524320 | tf_op jit(solution)/shard_map/ppermute | solution.py:310
  118.7 14.1 %collective-permute-done.35 = bf16[64,2048]{1,0:T(8,128)(2,1)S(1)} collective-permute-done((bf16[64,2048]{1,0:T(8,128)(2,1)S(1)}, bf16[64,2048]{1,0:T(8,128)(2,1)S(1)}, u32[]{:S(2)}, u32[]{:S(2)}) %collective-permute-start.35) | collective-permute-done | bytes 262176 | tf_op jit(solution)/shard_map/ppermute | solution.py:306
  141.9 18.5 %collective-permute-done.12 = bf16[64,2048]{1,0:T(8,128)(2,1)S(1)} collective-permute-done((bf16[64,2048]{1,0:T(8,128)(2,1)S(1)}, bf16[64,2048]{1,0:T(8,128)(2,1)S(1)}, u32[]{:S(2)}, u32[]{:S(2)}) %collective-permute-start.12) | collective-permute-done | bytes 262176 | tf_op jit(solution)/shard_map/ppermute | solution.py:306
  180.7 9.4 collective-permute-done.40
  196.2 7.8 collective-permute-done.17
  269.8 14.7 %collective-permute-done.75 = bf16[192,2048]{1,0:T(8,128)(2,1)} collective-permute-done((bf16[192,2048]{1,0:T(8,128)(2,1)}, bf16[192,2048]{1,0:T(8,128)(2,1)}, u32[]{:S(2)}, u32[]{:S(2)}) %collective-permute-start.75) | collective-permute-done | bytes 786464 | tf_op jit(solution)/shard_map/ppermute | solution.py:310
  383.9 8.6 fusion.60
  401.2 8.0 multiply_convert_fusion.4
  421.4 7.9 multiply_convert_fusion.3
  441.9 7.5 multiply_convert_fusion.2
  465.7 8.9 fusion.85
  501.5 15.3 %collective-permute-done.79 = bf16[192,2048]{1,0:T(8,128)(2,1)S(1)} collective-permute-done((bf16[192,2048]{1,0:T(8,128)(2,1)S(1)}, bf16[192,2048]{1,0:T(8,128)(2,1)S(1)}, u32[]{:S(2)}, u32[]{:S(2)}) %collective-permute-start.79) | collective-permute-done | bytes 786464 | tf_op jit(solution)/shard_map/ppermute | solution.py:306
  522.7 8.6 multiply_convert_fusion.1
  537.1 8.0 add_convert_fusion
  548.9 7.9 collective-permute-done.82
  561.4 7.5 collective-permute-done.58
  575.0 16.5 %collective-permute-done.68 = bf16[192,2048]{1,0:T(8,128)(2,1)S(1)} collective-permute-done((bf16[192,2048]{1,0:T(8,128)(2,1)S(1)}, bf16[192,2048]{1,0:T(8,128)(2,1)S(1)}, u32[]{:S(2)}, u32[]{:S(2)}) %collective-permute-start.68) | collective-permute-done | bytes 786464 | tf_op jit(solution)/shard_map/ppermute | solution.py:314
  593.4 19.2 %shard_map.267 = (f32[2048,512]{1,0:T(8,128)}, bf16[2048,512]{1,0:T(8,128)(2,1)}) custom-call(s32[5]{0:T(128)} %copy-done.17, bf16[768,2048]{1,0:T(8,128)(2,1)} %bitcast.489, bf16[768,2048]{1,0:T(8,128)(2,1)} %bitcast.494, bf16[768,2048]{1,0:T(8,128)(2,1)} %bitcast.499, bf16[768,2048]{1,0:T(8,128)(2,1)} %bitcast.504, bf16[768,1024]{1,0:T(8,128)(2,1)} %copy-done.136, ...), custom_call_target="tpu_custom_call" | custom-call | flops 12884901888 | bytes 25165824 | tf_op jit(solution)/shard_map/pallas_call | solution.py:554
  619.7 10.8 %fusion.15 = (f32[768]{0:T(1024)S(1)}, f32[768]{0:T(1024)S(1)}, f32[768]{0:T(1024)S(1)}, bf16[768,2048]{1,0:T(8,128)(2,1)}, bf16[768,2048]{1,0:T(8,128)(2,1)}, /*index=5*/bf16[768,2048]{1,0:T(8,128)(2,1)}) fusion(bf16[768,2048]{1,0:T(8,128)(2,1)} %get-tuple-element.224, bf16[4,768,2048]{2,1,0:T(8,128)(2,1)} %bitcast.509, s32[]{:T(128)S(6)} %select_n.137, ...), kind=kLoop, calls=%fused_computation.30 | loop fusion | flops 28309248 | bytes 28329996 | tf_op jit(solution)/shard_map/reduce_sum | solution.py:776
  639.0 7.6 all-to-all-done.1
  679.2 15.7 %shard_map.269 = (bf16[512,2048]{1,0:T(8,128)(2,1)}, bf16[512,2048]{1,0:T(8,128)(2,1)}, bf16[512,2048]{1,0:T(8,128)(2,1)}, bf16[256,2048]{1,0:T(8,128)(2,1)}, bf16[256,2048]{1,0:T(8,128)(2,1)}) custom-call(s32[5]{0:T(128)S(1)} %copy-done.18, bf16[1024,192]{1,0:T(8,128)(2,1)S(1)} %copy-done.11, bf16[1024,192]{1,0:T(8,128)(2,1)S(1)} %copy-done.13, ...), custom_call_target="tpu_custom_call" | custom-call | flops 3221225472 | bytes 16252928 | tf_op jit(solution)/shard_map/pallas_call | solution.py:512
  705.8 15.4 %shard_map.270 = (bf16[512,2048]{1,0:T(8,128)(2,1)}, bf16[512,2048]{1,0:T(8,128)(2,1)}, bf16[512,2048]{1,0:T(8,128)(2,1)}, bf16[256,2048]{1,0:T(8,128)(2,1)}, bf16[256,2048]{1,0:T(8,128)(2,1)}) custom-call(s32[5]{0:T(128)S(1)} %copy-done.18, bf16[1024,192]{1,0:T(8,128)(2,1)S(1)} %copy-done.12, bf16[1024,192]{1,0:T(8,128)(2,1)S(1)} %copy-done.14, ...), custom_call_target="tpu_custom_call" | custom-call | flops 3221225472 | bytes 16252928 | tf_op jit(solution)/shard_map/pallas_call | solution.py:512
  741.3 20.3 %collective-permute-done.97 = bf16[256,2048]{1,0:T(8,128)(2,1)S(1)} collective-permute-done((bf16[256,2048]{1,0:T(8,128)(2,1)}, bf16[256,2048]{1,0:T(8,128)(2,1)S(1)}, u32[]{:S(2)}, u32[]{:S(2)}) %collective-permute-start.97) | collective-permute-done | bytes 1048608 | tf_op jit(solution)/shard_map/ppermute | solution.py:310
  790.4 31.5 %collective-permute-done.92 = bf16[512,2048]{1,0:T(8,128)(2,1)S(1)} collective-permute-done((bf16[512,2048]{1,0:T(8,128)(2,1)}, bf16[512,2048]{1,0:T(8,128)(2,1)S(1)}, u32[]{:S(2)}, u32[]{:S(2)}) %collective-permute-start.92) | collective-permute-done | bytes 2097184 | tf_op jit(solution)/shard_map/ppermute | solution.py:306
  834.9 19.7 %shard_map.274 = (f32[2048,512]{1,0:T(8,128)}, bf16[2048,512]{1,0:T(8,128)(2,1)}) custom-call(s32[5]{0:T(128)} %copy-done.17, bf16[768,2048]{1,0:T(8,128)(2,1)} %bitcast.490, bf16[768,2048]{1,0:T(8,128)(2,1)} %bitcast.495, bf16[768,2048]{1,0:T(8,128)(2,1)} %bitcast.500, bf16[768,2048]{1,0:T(8,128)(2,1)} %bitcast.505, ...), custom_call_target="tpu_custom_call" | custom-call | flops 12884901888 | bytes 25165824 | tf_op jit(solution)/shard_map/pallas_call | solution.py:554
  859.5 12.5 %collective-permute-done.98 = bf16[512,2048]{1,0:T(8,128)(2,1)} collective-permute-done((bf16[512,2048]{1,0:T(8,128)(2,1)}, bf16[512,2048]{1,0:T(8,128)(2,1)}, u32[]{:S(2)}, u32[]{:S(2)}) %collective-permute-start.98) | collective-permute-done | bytes 2097184 | tf_op jit(solution)/shard_map/ppermute | solution.py:306
  872.1 8.9 collective-permute-done.100
  889.9 25.8 %shard_map.275 = (f32[512,2048]{1,0:T(8,128)}, bf16[512,2048]{1,0:T(8,128)(2,1)}) custom-call(s32[5]{0:T(128)} %copy-done.17, bf16[768,1024]{1,0:T(8,128)(2,1)} %get-tuple-element.146.refs_1_, bf16[768,1024]{1,0:T(8,128)(2,1)} %get-tuple-element.143.refs_2_, bf16[768,1024]{1,0:T(8,128)(2,1)} %get-tuple-element.140.refs_3_, ...), custom_call_target="tpu_custom_call" | custom-call | flops 12884901888 | bytes 25165824 | tf_op jit(solution)/shard_map/pallas_call | solution.py:611
  927.9 17.2 %collective-permute-done.101 = bf16[256,2048]{1,0:T(8,128)(2,1)S(1)} collective-permute-done((bf16[256,2048]{1,0:T(8,128)(2,1)S(1)}, bf16[256,2048]{1,0:T(8,128)(2,1)S(1)}, u32[]{:S(2)}, u32[]{:S(2)}) %collective-permute-start.101) | collective-permute-done | bytes 1048608 | tf_op jit(solution)/shard_map/ppermute | solution.py:314
  (725 shorter events, 535.0 us)
Async XLA Ops:
  7.2 376.8 %all-gather.2.cloned.1.call-start = ((), (), s32[]{:S(2)}) async-start(), calls=%async_computation.4 | async-start | bytes 13369344 | tf_op jit(solution)/shard_map/all_gather | solution.py:684
  79.0 33.9 %collective-permute-start.11 = (bf16[128,2048]{1,0:T(8,128)(2,1)}, bf16[128,2048]{1,0:T(8,128)(2,1)S(1)}, u32[]{:S(2)}, u32[]{:S(2)}) collective-permute-start(bf16[128,2048]{1,0:T(8,128)(2,1)} %copy-done.88), channel_id=1, source_target_pairs={{0,2},{1,3},{2,0},{3,1},{4,6},{5,7},{6,4},{7,5},{8,10},{9,11},{10,... | collective-permute-start | bytes 1572872 | tf_op jit(solution)/shard_map/ppermute | solution.py:310
  79.5 35.0 %collective-permute-start.10 = (bf16[128,2048]{1,0:T(8,128)(2,1)}, bf16[128,2048]{1,0:T(8,128)(2,1)S(1)}, u32[]{:S(2)}, u32[]{:S(2)}) collective-permute-start(bf16[128,2048]{1,0:T(8,128)(2,1)} %copy-done.88), channel_id=1, source_target_pairs={{0,1},{1,0},{2,3},{3,2},{4,5},{5,4},{6,7},{7,6},{8,9},{9,8},{10,11... | collective-permute-start | bytes 1572872 | tf_op jit(solution)/shard_map/ppermute | solution.py:306
  81.0 35.0 %collective-permute-start.37 = (bf16[128,2048]{1,0:T(8,128)(2,1)}, bf16[128,2048]{1,0:T(8,128)(2,1)}, u32[]{:S(2)}, u32[]{:S(2)}) collective-permute-start(bf16[128,2048]{1,0:T(8,128)(2,1)} %collective-permute-done.32), channel_id=1, source_target_pairs={{0,4},{1,5},{2,6},{3,7},{4,8},{5,9},{6,10},{7,11},{8,12},{9,13},{1... | collective-permute-start | bytes 1572872 | tf_op jit(solution)/shard_map/ppermute | solution.py:314
  141.9 65.7 %collective-permute-start.42 = (bf16[4,128,2048]{2,1,0:T(8,128)(2,1)}, bf16[4,128,2048]{2,1,0:T(8,128)(2,1)}, u32[]{:S(2)}, u32[]{:S(2)}) collective-permute-start(bf16[4,128,2048]{2,1,0:T(8,128)(2,1)} %pad_maximum_fusion.4.refs_2_), channel_id=1, source_target_pairs={{0,16},{16,0},{1,17},{17,1},{2,18},{18,2},{3,19},{19,3},{4,20},{20... | collective-permute-start | bytes 6291464 | tf_op jit(solution)/shard_map/ppermute | solution.py:318
  160.5 47.7 %collective-permute-start.43 = (bf16[4,128,2048]{2,1,0:T(8,128)(2,1)}, bf16[4,128,2048]{2,1,0:T(8,128)(2,1)}, u32[]{:S(2)}, u32[]{:S(2)}) collective-permute-start(bf16[4,128,2048]{2,1,0:T(8,128)(2,1)} %pad_maximum_fusion.5.refs_3_), channel_id=1, source_target_pairs={{0,16},{16,0},{1,17},{17,1},{2,18},{18,2},{3,19},{19,3},{4,20},{20... | collective-permute-start | bytes 6291464 | tf_op jit(solution)/shard_map/ppermute | solution.py:318
  161.2 47.1 %collective-permute-start.44 = (bf16[4,128,2048]{2,1,0:T(8,128)(2,1)}, bf16[4,128,2048]{2,1,0:T(8,128)(2,1)}, u32[]{:S(2)}, u32[]{:S(2)}) collective-permute-start(bf16[4,128,2048]{2,1,0:T(8,128)(2,1)} %pad_maximum_fusion.6.refs_4_), channel_id=1, source_target_pairs={{0,16},{16,0},{1,17},{17,1},{2,18},{18,2},{3,19},{19,3},{4,20},{20... | collective-permute-start | bytes 6291464 | tf_op jit(solution)/shard_map/ppermute | solution.py:318
  204.0 30.4 %collective-permute-start.19 = (bf16[4,128,2048]{2,1,0:T(8,128)(2,1)S(1)}, bf16[4,128,2048]{2,1,0:T(8,128)(2,1)}, u32[]{:S(2)}, u32[]{:S(2)}) collective-permute-start(bf16[4,128,2048]{2,1,0:T(8,128)(2,1)S(1)} %pad_maximum_fusion.refs_2_), channel_id=1, source_target_pairs={{0,16},{16,0},{1,17},{17,1},{2,18},{18,2},{3,19},{19,3},{4,20},{20... | collective-permute-start | bytes 6291464 | tf_op jit(solution)/shard_map/ppermute | solution.py:318
  213.5 736.2 %reduce-scatter.2.cloned.1.call-start = ((), (), s32[]{:S(2)}) async-start(), calls=%async_computation.5 | async-start | bytes 13369344 | tf_op jit(solution)/shard_map/reduce_scatter | solution.py:823
  419.0 68.8 %collective-permute-start.78 = (bf16[96,2048]{1,0:T(8,128)(2,1)}, bf16[96,2048]{1,0:T(8,128)(2,1)}, u32[]{:S(2)}, u32[]{:S(2)}) collective-permute-start(bf16[96,2048]{1,0:T(8,128)(2,1)} %get-tuple-element.170), channel_id=1, source_target_pairs={{0,2},{1,3},{2,0},{3,1},{4,6},{5,7},{6,4},{7,5},{8,10},{9,11},{10,... | collective-permute-start | bytes 1179656 | tf_op jit(solution)/shard_map/ppermute | solution.py:310
  420.8 67.2 %collective-permute-start.80 = (bf16[96,2048]{1,0:T(8,128)(2,1)}, bf16[96,2048]{1,0:T(8,128)(2,1)}, u32[]{:S(2)}, u32[]{:S(2)}) collective-permute-start(bf16[96,2048]{1,0:T(8,128)(2,1)} %get-tuple-element.172), channel_id=1, source_target_pairs={{0,1},{1,0},{2,3},{3,2},{4,5},{5,4},{6,7},{7,6},{8,9},{9,8},{10,11... | collective-permute-start | bytes 1179656 | tf_op jit(solution)/shard_map/ppermute | solution.py:306
  439.6 52.0 %collective-permute-start.54 = (bf16[96,2048]{1,0:T(8,128)(2,1)}, bf16[96,2048]{1,0:T(8,128)(2,1)}, u32[]{:S(2)}, u32[]{:S(2)}) collective-permute-start(bf16[96,2048]{1,0:T(8,128)(2,1)} %get-tuple-element.158), channel_id=1, source_target_pairs={{0,2},{1,3},{2,0},{3,1},{4,6},{5,7},{6,4},{7,5},{8,10},{9,11},{10,... | collective-permute-start | bytes 1179656 | tf_op jit(solution)/shard_map/ppermute | solution.py:310
  441.3 51.3 %collective-permute-start.56 = (bf16[96,2048]{1,0:T(8,128)(2,1)}, bf16[96,2048]{1,0:T(8,128)(2,1)}, u32[]{:S(2)}, u32[]{:S(2)}) collective-permute-start(bf16[96,2048]{1,0:T(8,128)(2,1)} %get-tuple-element.160), channel_id=1, source_target_pairs={{0,1},{1,0},{2,3},{3,2},{4,5},{5,4},{6,7},{7,6},{8,9},{9,8},{10,11... | collective-permute-start | bytes 1179656 | tf_op jit(solution)/shard_map/ppermute | solution.py:306
  457.7 37.2 %collective-permute-start.64 = (bf16[96,2048]{1,0:T(8,128)(2,1)}, bf16[96,2048]{1,0:T(8,128)(2,1)}, u32[]{:S(2)}, u32[]{:S(2)}) collective-permute-start(bf16[96,2048]{1,0:T(8,128)(2,1)} %get-tuple-element.164), channel_id=1, source_target_pairs={{0,2},{1,3},{2,0},{3,1},{4,6},{5,7},{6,4},{7,5},{8,10},{9,11},{10,... | collective-permute-start | bytes 1179656 | tf_op jit(solution)/shard_map/ppermute | solution.py:310
  494.1 53.1 %collective-permute-start.55 = (bf16[192,2048]{1,0:T(8,128)(2,1)S(1)}, bf16[192,2048]{1,0:T(8,128)(2,1)S(1)}, u32[]{:S(2)}, u32[]{:S(2)}) collective-permute-start(bf16[192,2048]{1,0:T(8,128)(2,1)S(1)} %pad_maximum_fusion.12), channel_id=1, source_target_pairs={{0,1},{1,0},{2,3},{3,2},{4,5},{5,4},{6,7},{7,6},{8,9},{9,8},{10,11... | collective-permute-start | bytes 2359304 | tf_op jit(solution)/shard_map/ppermute | solution.py:306
  495.0 52.2 %collective-permute-start.57 = (bf16[192,2048]{1,0:T(8,128)(2,1)S(1)}, bf16[192,2048]{1,0:T(8,128)(2,1)S(1)}, u32[]{:S(2)}, u32[]{:S(2)}) collective-permute-start(bf16[192,2048]{1,0:T(8,128)(2,1)S(1)} %pad_maximum_fusion.13), channel_id=1, source_target_pairs={{0,2},{1,3},{2,0},{3,1},{4,6},{5,7},{6,4},{7,5},{8,10},{9,11},{10,... | collective-permute-start | bytes 2359304 | tf_op jit(solution)/shard_map/ppermute | solution.py:310
  501.3 60.1 %collective-permute-start.65 = (bf16[192,2048]{1,0:T(8,128)(2,1)S(1)}, bf16[192,2048]{1,0:T(8,128)(2,1)S(1)}, u32[]{:S(2)}, u32[]{:S(2)}) collective-permute-start(bf16[192,2048]{1,0:T(8,128)(2,1)S(1)} %pad_maximum_fusion.14), channel_id=1, source_target_pairs={{0,1},{1,0},{2,3},{3,2},{4,5},{5,4},{6,7},{7,6},{8,9},{9,8},{10,11... | collective-permute-start | bytes 2359304 | tf_op jit(solution)/shard_map/ppermute | solution.py:306
  516.8 44.6 %collective-permute-start.67 = (bf16[192,2048]{1,0:T(8,128)(2,1)S(1)}, bf16[192,2048]{1,0:T(8,128)(2,1)S(1)}, u32[]{:S(2)}, u32[]{:S(2)}) collective-permute-start(bf16[192,2048]{1,0:T(8,128)(2,1)S(1)} %pad_maximum_fusion.15), channel_id=1, source_target_pairs={{0,2},{1,3},{2,0},{3,1},{4,6},{5,7},{6,4},{7,5},{8,10},{9,11},{10,... | collective-permute-start | bytes 2359304 | tf_op jit(solution)/shard_map/ppermute | solution.py:310
  616.6 54.7 %collective-permute-start.46 = (bf16[192,1024]{1,0:T(8,128)(2,1)}, bf16[192,1024]{1,0:T(8,128)(2,1)}, u32[]{:S(2)}, u32[]{:S(2)}) collective-permute-start(bf16[192,1024]{1,0:T(8,128)(2,1)} %get-tuple-element.189), channel_id=1, source_target_pairs={{0,16},{16,0},{1,17},{17,1},{2,18},{18,2},{3,19},{19,3},{4,20},{20... | collective-permute-start | bytes 1179656 | tf_op jit(solution)/shard_map/ppermute | solution.py:318
  618.2 53.3 %collective-permute-start.47 = (bf16[192,1024]{0,1:T(8,128)(2,1)}, bf16[192,1024]{0,1:T(8,128)(2,1)}, u32[]{:S(2)}, u32[]{:S(2)}) collective-permute-start(bf16[192,1024]{0,1:T(8,128)(2,1)} %get-tuple-element.187), channel_id=1, source_target_pairs={{0,16},{16,0},{1,17},{17,1},{2,18},{18,2},{3,19},{19,3},{4,20},{20... | collective-permute-start | bytes 1179656 | tf_op jit(solution)/shard_map/ppermute | solution.py:318
  646.7 80.2 %collective-permute-start.102 = (bf16[2048,512]{1,0:T(8,128)(2,1)}, bf16[2048,512]{1,0:T(8,128)(2,1)}, u32[]{:S(2)}, u32[]{:S(2)}) collective-permute-start(bf16[2048,512]{1,0:T(8,128)(2,1)} %get-tuple-element.59), channel_id=1, source_target_pairs={{0,16},{16,0},{1,17},{17,1},{2,18},{18,2},{3,19},{19,3},{4,20},{20... | collective-permute-start | bytes 6291464 | tf_op jit(solution)/shard_map/ppermute | solution.py:318
  694.9 36.9 %collective-permute-start.91 = (bf16[256,2048]{1,0:T(8,128)(2,1)}, bf16[256,2048]{1,0:T(8,128)(2,1)S(1)}, u32[]{:S(2)}, u32[]{:S(2)}) collective-permute-start(bf16[256,2048]{1,0:T(8,128)(2,1)} %get-tuple-element.47), channel_id=1, source_target_pairs={{0,2},{1,3},{2,0},{3,1},{4,6},{5,7},{6,4},{7,5},{8,10},{9,11},{10,... | collective-permute-start | bytes 3145736 | tf_op jit(solution)/shard_map/ppermute | solution.py:310
  700.1 37.5 %collective-permute-start.93 = (bf16[256,2048]{1,0:T(8,128)(2,1)}, bf16[256,2048]{1,0:T(8,128)(2,1)S(1)}, u32[]{:S(2)}, u32[]{:S(2)}) collective-permute-start(bf16[256,2048]{1,0:T(8,128)(2,1)} %get-tuple-element.49), channel_id=1, source_target_pairs={{0,1},{1,0},{2,3},{3,2},{4,5},{5,4},{6,7},{7,6},{8,9},{9,8},{10,11... | collective-permute-start | bytes 3145736 | tf_op jit(solution)/shard_map/ppermute | solution.py:306
  721.2 40.4 %collective-permute-start.97 = (bf16[256,2048]{1,0:T(8,128)(2,1)}, bf16[256,2048]{1,0:T(8,128)(2,1)S(1)}, u32[]{:S(2)}, u32[]{:S(2)}) collective-permute-start(bf16[256,2048]{1,0:T(8,128)(2,1)} %get-tuple-element.52), channel_id=1, source_target_pairs={{0,2},{1,3},{2,0},{3,1},{4,6},{5,7},{6,4},{7,5},{8,10},{9,11},{10,... | collective-permute-start | bytes 3145736 | tf_op jit(solution)/shard_map/ppermute | solution.py:310
  724.0 41.6 %collective-permute-start.99 = (bf16[256,2048]{1,0:T(8,128)(2,1)}, bf16[256,2048]{1,0:T(8,128)(2,1)S(1)}, u32[]{:S(2)}, u32[]{:S(2)}) collective-permute-start(bf16[256,2048]{1,0:T(8,128)(2,1)} %get-tuple-element.54), channel_id=1, source_target_pairs={{0,1},{1,0},{2,3},{3,2},{4,5},{5,4},{6,7},{7,6},{8,9},{9,8},{10,11... | collective-permute-start | bytes 3145736 | tf_op jit(solution)/shard_map/ppermute | solution.py:306
  734.3 87.6 %collective-permute-start.92 = (bf16[512,2048]{1,0:T(8,128)(2,1)}, bf16[512,2048]{1,0:T(8,128)(2,1)S(1)}, u32[]{:S(2)}, u32[]{:S(2)}) collective-permute-start(bf16[512,2048]{1,0:T(8,128)(2,1)} %pad_maximum_fusion.8), channel_id=1, source_target_pairs={{0,1},{1,0},{2,3},{3,2},{4,5},{5,4},{6,7},{7,6},{8,9},{9,8},{10,11... | collective-permute-start | bytes 6291464 | tf_op jit(solution)/shard_map/ppermute | solution.py:306
  739.8 89.3 %collective-permute-start.94 = (bf16[512,2048]{1,0:T(8,128)(2,1)}, bf16[512,2048]{1,0:T(8,128)(2,1)}, u32[]{:S(2)}, u32[]{:S(2)}) collective-permute-start(bf16[512,2048]{1,0:T(8,128)(2,1)} %pad_maximum_fusion.9), channel_id=1, source_target_pairs={{0,2},{1,3},{2,0},{3,1},{4,6},{5,7},{6,4},{7,5},{8,10},{9,11},{10,... | collective-permute-start | bytes 6291464 | tf_op jit(solution)/shard_map/ppermute | solution.py:310
  763.6 108.4 %collective-permute-start.98 = (bf16[512,2048]{1,0:T(8,128)(2,1)}, bf16[512,2048]{1,0:T(8,128)(2,1)}, u32[]{:S(2)}, u32[]{:S(2)}) collective-permute-start(bf16[512,2048]{1,0:T(8,128)(2,1)} %pad_maximum_fusion.10), channel_id=1, source_target_pairs={{0,1},{1,0},{2,3},{3,2},{4,5},{5,4},{6,7},{7,6},{8,9},{9,8},{10,11... | collective-permute-start | bytes 6291464 | tf_op jit(solution)/shard_map/ppermute | solution.py:306
  767.7 113.3 %collective-permute-start.100 = (bf16[512,2048]{1,0:T(8,128)(2,1)}, bf16[512,2048]{1,0:T(8,128)(2,1)}, u32[]{:S(2)}, u32[]{:S(2)}) collective-permute-start(bf16[512,2048]{1,0:T(8,128)(2,1)} %pad_maximum_fusion.11), channel_id=1, source_target_pairs={{0,2},{1,3},{2,0},{3,1},{4,6},{5,7},{6,4},{7,5},{8,10},{9,11},{10,... | collective-permute-start | bytes 6291464 | tf_op jit(solution)/shard_map/ppermute | solution.py:310
  834.1 53.2 %collective-permute-start.95 = (bf16[256,2048]{1,0:T(8,128)(2,1)S(1)}, bf16[256,2048]{1,0:T(8,128)(2,1)S(1)}, u32[]{:S(2)}, u32[]{:S(2)}) collective-permute-start(bf16[256,2048]{1,0:T(8,128)(2,1)S(1)} %split.69), channel_id=1, source_target_pairs={{0,4},{1,5},{2,6},{3,7},{4,8},{5,9},{6,10},{7,11},{8,12},{9,13},{1... | collective-permute-start | bytes 3145736 | tf_op jit(solution)/shard_map/ppermute | solution.py:314
  854.5 67.7 %collective-permute-start.103 = (bf16[2048,512]{1,0:T(8,128)(2,1)}, bf16[2048,512]{1,0:T(8,128)(2,1)}, u32[]{:S(2)}, u32[]{:S(2)}) collective-permute-start(bf16[2048,512]{1,0:T(8,128)(2,1)} %get-tuple-element.61), channel_id=1, source_target_pairs={{0,16},{16,0},{1,17},{17,1},{2,18},{18,2},{3,19},{19,3},{4,20},{20... | collective-permute-start | bytes 6291464 | tf_op jit(solution)/shard_map/ppermute | solution.py:318
  855.5 65.2 %all-to-all-start.2 = ((f32[32,1,1280]{2,1,0:T(1,128)}), f32[32,1,1280]{2,1,0:T(1,128)S(1)}, u32[]{:S(2)}, u32[]{:S(2)}) async-start(f32[32,1,1280]{2,1,0:T(1,128)} %copy.134), calls=%async_computation.3 | async-start | bytes 327680 | tf_op jit(solution)/shard_map/all_to_all | solution.py:897
  (219 other events, 3108.4 us)
Sparse Core Ops, SparseCore 0:
  70.9 190.4 all-gather.1
  615.8 266.2 reduce-scatter.1

commit v5 on v4

--- a/solution.py
+++ b/solution.py
@@ -360,12 +360,15 @@
     def across(self, low, high):
         return move_x(low), move_y(high)
 
-    def finish(self, steps, own, for_x, for_y, by_x, by_y):
+    def finish(self, steps, own, for_x, for_y, by_x, by_y, chained=False):
         low = own.dtype
         cut = by_x.shape[0]
         for_y = jnp.concatenate([add_f32(for_y[:cut], by_x).astype(low), for_y[cut:]], axis=0)
         for_x = jnp.concatenate([for_x[:cut], add_f32(for_x[cut:], by_y).astype(low)], axis=0)
-        total = add_f32(own, move_x(for_x)) + move_y(for_y).astype(jnp.float32)
+        from_x, from_y = move_x(for_x), move_y(for_y)
+        if chained:
+            from_x, from_y, self.total = tie(from_x, from_y, self.total)
+        total = add_f32(own, from_x) + from_y.astype(jnp.float32)
         for step, part in zip(steps, jnp.split(total, len(steps), axis=0), strict=True):
             self.planes[step] = part
 
@@ -871,7 +874,7 @@
     up_grads = [chunk[2] for chunk in backward]
     own_up, other_up = column_grads(position, expert_acts, up_grads, waits=(act_grad,))
     weights_reduce.push()
-    weights_reduce.finish([3, 0], *last[:3], *last_ways)
+    weights_reduce.finish([3, 0], *last[:3], *last_ways, chained=True)
     own_down, other_down = down_grads(
         position,
         [chunk[5] for chunk in forward],

time: 970 us -> 969 us (level)
    ppermute x36, waiting for transfers between devices: 127 us -> 97.9 us  [move_y(): return lax.ppermute(values, 'expert', Y_PAIRS)]
    ppermute x15, waiting for transfers between devices: 49.5 us -> 68.3 us  [move_z(): return lax.ppermute(values, 'expert', Z_PAIRS)]
    unnamed x286 -> x284, local copies, waits for them, and re-layouts: 28.6 us -> 28.1 us
  transfers between devices with their start and end apart: 110 -> 110, of which waited for: 48 -> 45; matrix products, arithmetic and copies ran while one was open for 27% -> 28% of each run, Pallas kernels for 15% -> 15%
where the time goes in v5:
time: 969 us; the launch traced here: 961 us
  waiting for transfers between devices  345 us (36%)
  matrix products  153 us (16%)
  Pallas kernels  146 us (15%)
  starting transfers between devices  113 us (12%)
  other arithmetic  105 us (11%)
  local copies, waits for them, and re-layouts  80.6 us (8%)
  between operations  17.2 us (2%)
    ppermute x36, waiting for transfers between devices, move_x(): return lax.ppermute(values, 'expert', X_PAIRS)  166 us
    ppermute x36, waiting for transfers between devices, move_y(): return lax.ppermute(values, 'expert', Y_PAIRS)  97.9 us
    ppermute x15, waiting for transfers between devices, move_z(): return lax.ppermute(values, 'expert', Z_PAIRS)  68.3 us
    dot_general x13, matrix products, times_transposed(): jnp.einsum('ta,ba->tb', left, right, preferred_element_type=jnp.float32)  62.1 us
    pallas_call x8, Pallas kernels, apply_weight(): pl.pallas_call(without(functools.partial(apply_back_kernel if back else a...  50.6 us
    ppermute x36, starting transfers between devices, move_y(): return lax.ppermute(values, 'expert', Y_PAIRS)  39.7 us
    pallas_call x2, Pallas kernels, column_grads(): pl.pallas_call(without(column_grad_kernel, 1 + 2 * parts, len(waits)), gr...  38.9 us
    ppermute x36, starting transfers between devices, move_x(): return lax.ppermute(values, 'expert', X_PAIRS)  37.6 us
  transfers between devices with their start and end apart: 110, of which 45 were waited for; matrix products, arithmetic and copies ran while one was open for 28% of the time, Pallas kernels for 15%

profile of v5, /device:TPU:0, one launch (start us, length us, event | category | flops | bytes accessed | tf_op | source)
XLA Modules:
  0.0 961.0 jit_solution(14407606497911224271)
XLA Ops:
  19.4 7.7 collective-permute-done.1
  29.2 8.3 collective-permute-done.27
  71.2 7.7 collective-permute-done.6
  98.0 11.7 %collective-permute-done.34 = bf16[128,2048]{1,0:T(8,128)(2,1)S(1)} collective-permute-done((bf16[128,2048]{1,0:T(8,128)(2,1)}, bf16[128,2048]{1,0:T(8,128)(2,1)S(1)}, u32[]{:S(2)}, u32[]{:S(2)}) %collective-permute-start.34) | collective-permute-done | bytes 524320 | tf_op jit(solution)/shard_map/ppermute | solution.py:310
  118.7 14.1 %collective-permute-done.35 = bf16[64,2048]{1,0:T(8,128)(2,1)S(1)} collective-permute-done((bf16[64,2048]{1,0:T(8,128)(2,1)S(1)}, bf16[64,2048]{1,0:T(8,128)(2,1)S(1)}, u32[]{:S(2)}, u32[]{:S(2)}) %collective-permute-start.35) | collective-permute-done | bytes 262176 | tf_op jit(solution)/shard_map/ppermute | solution.py:306
  142.0 18.5 %collective-permute-done.12 = bf16[64,2048]{1,0:T(8,128)(2,1)S(1)} collective-permute-done((bf16[64,2048]{1,0:T(8,128)(2,1)S(1)}, bf16[64,2048]{1,0:T(8,128)(2,1)S(1)}, u32[]{:S(2)}, u32[]{:S(2)}) %collective-permute-start.12) | collective-permute-done | bytes 262176 | tf_op jit(solution)/shard_map/ppermute | solution.py:306
  180.7 9.4 collective-permute-done.40
  196.2 7.8 collective-permute-done.17
  269.8 14.7 %collective-permute-done.75 = bf16[192,2048]{1,0:T(8,128)(2,1)} collective-permute-done((bf16[192,2048]{1,0:T(8,128)(2,1)}, bf16[192,2048]{1,0:T(8,128)(2,1)}, u32[]{:S(2)}, u32[]{:S(2)}) %collective-permute-start.75) | collective-permute-done | bytes 786464 | tf_op jit(solution)/shard_map/ppermute | solution.py:310
  346.3 7.3 collective-permute-done.62
  383.8 8.6 fusion.60
  401.2 8.0 multiply_convert_fusion.4
  421.5 7.9 multiply_convert_fusion.3
  442.0 7.4 multiply_convert_fusion.2
  465.4 8.9 fusion.85
  501.3 15.3 %collective-permute-done.79 = bf16[192,2048]{1,0:T(8,128)(2,1)S(1)} collective-permute-done((bf16[192,2048]{1,0:T(8,128)(2,1)S(1)}, bf16[192,2048]{1,0:T(8,128)(2,1)S(1)}, u32[]{:S(2)}, u32[]{:S(2)}) %collective-permute-start.79) | collective-permute-done | bytes 786464 | tf_op jit(solution)/shard_map/ppermute | solution.py:306
  522.4 8.5 multiply_convert_fusion.1
  536.8 8.0 add_convert_fusion
  548.4 8.1 collective-permute-done.82
  561.1 7.4 collective-permute-done.58
  574.5 16.5 %collective-permute-done.68 = bf16[192,2048]{1,0:T(8,128)(2,1)S(1)} collective-permute-done((bf16[192,2048]{1,0:T(8,128)(2,1)S(1)}, bf16[192,2048]{1,0:T(8,128)(2,1)S(1)}, u32[]{:S(2)}, u32[]{:S(2)}) %collective-permute-start.68) | collective-permute-done | bytes 786464 | tf_op jit(solution)/shard_map/ppermute | solution.py:314
  592.9 19.2 %shard_map.267 = (f32[2048,512]{1,0:T(8,128)}, bf16[2048,512]{1,0:T(8,128)(2,1)}) custom-call(s32[5]{0:T(128)} %copy-done.17, bf16[768,2048]{1,0:T(8,128)(2,1)} %bitcast.489, bf16[768,2048]{1,0:T(8,128)(2,1)} %bitcast.494, bf16[768,2048]{1,0:T(8,128)(2,1)} %bitcast.499, bf16[768,2048]{1,0:T(8,128)(2,1)} %bitcast.504, bf16[768,1024]{1,0:T(8,128)(2,1)} %copy-done.135, ...), custom_call_target="tpu_custom_call" | custom-call | flops 12884901888 | bytes 25165824 | tf_op jit(solution)/shard_map/pallas_call | solution.py:557
  619.2 10.7 %fusion.15 = (f32[768]{0:T(1024)S(1)}, f32[768]{0:T(1024)S(1)}, f32[768]{0:T(1024)S(1)}, bf16[768,2048]{1,0:T(8,128)(2,1)}, bf16[768,2048]{1,0:T(8,128)(2,1)}, /*index=5*/bf16[768,2048]{1,0:T(8,128)(2,1)}) fusion(bf16[768,2048]{1,0:T(8,128)(2,1)} %get-tuple-element.230, bf16[4,768,2048]{2,1,0:T(8,128)(2,1)} %bitcast.509, s32[]{:T(128)S(6)} %select_n.137, ...), kind=kLoop, calls=%fused_computation.30 | loop fusion | flops 28309248 | bytes 28329996 | tf_op jit(solution)/shard_map/reduce_sum | solution.py:779
  638.6 7.6 all-to-all-done.1
  678.7 15.7 %shard_map.270 = (bf16[512,2048]{1,0:T(8,128)(2,1)}, bf16[512,2048]{1,0:T(8,128)(2,1)}, bf16[512,2048]{1,0:T(8,128)(2,1)}, bf16[256,2048]{1,0:T(8,128)(2,1)}, bf16[256,2048]{1,0:T(8,128)(2,1)}) custom-call(s32[5]{0:T(128)S(1)} %copy-done.18, bf16[1024,192]{1,0:T(8,128)(2,1)S(1)} %copy-done.11, bf16[1024,192]{1,0:T(8,128)(2,1)S(1)} %copy-done.13, ...), custom_call_target="tpu_custom_call" | custom-call | flops 3221225472 | bytes 16252928 | tf_op jit(solution)/shard_map/pallas_call | solution.py:515
  705.4 15.5 %shard_map.269 = (bf16[512,2048]{1,0:T(8,128)(2,1)}, bf16[512,2048]{1,0:T(8,128)(2,1)}, bf16[512,2048]{1,0:T(8,128)(2,1)}, bf16[256,2048]{1,0:T(8,128)(2,1)}, bf16[256,2048]{1,0:T(8,128)(2,1)}) custom-call(s32[5]{0:T(128)S(1)} %copy-done.18, bf16[1024,192]{1,0:T(8,128)(2,1)S(1)} %copy-done.12, bf16[1024,192]{1,0:T(8,128)(2,1)S(1)} %copy-done.14, ...), custom_call_target="tpu_custom_call" | custom-call | flops 3221225472 | bytes 16252928 | tf_op jit(solution)/shard_map/pallas_call | solution.py:515
  740.6 24.7 %collective-permute-done.93 = bf16[256,2048]{1,0:T(8,128)(2,1)S(1)} collective-permute-done((bf16[256,2048]{1,0:T(8,128)(2,1)}, bf16[256,2048]{1,0:T(8,128)(2,1)S(1)}, u32[]{:S(2)}, u32[]{:S(2)}) %collective-permute-start.93) | collective-permute-done | bytes 1048608 | tf_op jit(solution)/shard_map/ppermute | solution.py:306
  792.8 28.7 %collective-permute-done.96 = bf16[512,2048]{1,0:T(8,128)(2,1)S(1)} collective-permute-done((bf16[512,2048]{1,0:T(8,128)(2,1)}, bf16[512,2048]{1,0:T(8,128)(2,1)S(1)}, u32[]{:S(2)}, u32[]{:S(2)}) %collective-permute-start.96) | collective-permute-done | bytes 2097184 | tf_op jit(solution)/shard_map/ppermute | solution.py:306
  836.0 19.7 %shard_map.274 = (f32[2048,512]{1,0:T(8,128)}, bf16[2048,512]{1,0:T(8,128)(2,1)}) custom-call(s32[5]{0:T(128)} %copy-done.17, bf16[768,2048]{1,0:T(8,128)(2,1)} %bitcast.490, bf16[768,2048]{1,0:T(8,128)(2,1)} %bitcast.495, bf16[768,2048]{1,0:T(8,128)(2,1)} %bitcast.500, bf16[768,2048]{1,0:T(8,128)(2,1)} %bitcast.505, ...), custom_call_target="tpu_custom_call" | custom-call | flops 12884901888 | bytes 25165824 | tf_op jit(solution)/shard_map/pallas_call | solution.py:557
  861.4 18.5 %collective-permute-done.99 = bf16[256,2048]{1,0:T(8,128)(2,1)S(1)} collective-permute-done((bf16[256,2048]{1,0:T(8,128)(2,1)S(1)}, bf16[256,2048]{1,0:T(8,128)(2,1)S(1)}, u32[]{:S(2)}, u32[]{:S(2)}) %collective-permute-start.99) | collective-permute-done | bytes 1048608 | tf_op jit(solution)/shard_map/ppermute | solution.py:314
  884.3 25.8 %shard_map.275 = (f32[512,2048]{1,0:T(8,128)}, bf16[512,2048]{1,0:T(8,128)(2,1)}) custom-call(s32[5]{0:T(128)} %copy-done.17, bf16[768,1024]{1,0:T(8,128)(2,1)} %get-tuple-element.152.refs_1_, bf16[768,1024]{1,0:T(8,128)(2,1)} %get-tuple-element.149.refs_2_, bf16[768,1024]{1,0:T(8,128)(2,1)} %get-tuple-element.146.refs_3_, ...), custom_call_target="tpu_custom_call" | custom-call | flops 12884901888 | bytes 25165824 | tf_op jit(solution)/shard_map/pallas_call | solution.py:614
  927.0 17.6 %collective-permute-done.101 = bf16[256,2048]{1,0:T(8,128)(2,1)S(1)} collective-permute-done((bf16[256,2048]{1,0:T(8,128)(2,1)}, bf16[256,2048]{1,0:T(8,128)(2,1)S(1)}, u32[]{:S(2)}, u32[]{:S(2)}) %collective-permute-start.101) | collective-permute-done | bytes 1048608 | tf_op jit(solution)/shard_map/ppermute | solution.py:314
  (723 shorter events, 528.4 us)
Async XLA Ops:
  7.2 376.7 %all-gather.2.cloned.1.call-start = ((), (), s32[]{:S(2)}) async-start(), calls=%async_computation.4 | async-start | bytes 13369344 | tf_op jit(solution)/shard_map/all_gather | solution.py:687
  79.0 33.9 %collective-permute-start.11 = (bf16[128,2048]{1,0:T(8,128)(2,1)}, bf16[128,2048]{1,0:T(8,128)(2,1)S(1)}, u32[]{:S(2)}, u32[]{:S(2)}) collective-permute-start(bf16[128,2048]{1,0:T(8,128)(2,1)} %copy-done.87), channel_id=1, source_target_pairs={{0,2},{1,3},{2,0},{3,1},{4,6},{5,7},{6,4},{7,5},{8,10},{9,11},{10,... | collective-permute-start | bytes 1572872 | tf_op jit(solution)/shard_map/ppermute | solution.py:310
  79.5 35.0 %collective-permute-start.10 = (bf16[128,2048]{1,0:T(8,128)(2,1)}, bf16[128,2048]{1,0:T(8,128)(2,1)S(1)}, u32[]{:S(2)}, u32[]{:S(2)}) collective-permute-start(bf16[128,2048]{1,0:T(8,128)(2,1)} %copy-done.87), channel_id=1, source_target_pairs={{0,1},{1,0},{2,3},{3,2},{4,5},{5,4},{6,7},{7,6},{8,9},{9,8},{10,11... | collective-permute-start | bytes 1572872 | tf_op jit(solution)/shard_map/ppermute | solution.py:306
  81.0 35.0 %collective-permute-start.37 = (bf16[128,2048]{1,0:T(8,128)(2,1)}, bf16[128,2048]{1,0:T(8,128)(2,1)}, u32[]{:S(2)}, u32[]{:S(2)}) collective-permute-start(bf16[128,2048]{1,0:T(8,128)(2,1)} %collective-permute-done.32), channel_id=1, source_target_pairs={{0,4},{1,5},{2,6},{3,7},{4,8},{5,9},{6,10},{7,11},{8,12},{9,13},{1... | collective-permute-start | bytes 1572872 | tf_op jit(solution)/shard_map/ppermute | solution.py:314
  142.0 65.7 %collective-permute-start.42 = (bf16[4,128,2048]{2,1,0:T(8,128)(2,1)}, bf16[4,128,2048]{2,1,0:T(8,128)(2,1)}, u32[]{:S(2)}, u32[]{:S(2)}) collective-permute-start(bf16[4,128,2048]{2,1,0:T(8,128)(2,1)} %pad_maximum_fusion.4.refs_2_), channel_id=1, source_target_pairs={{0,16},{16,0},{1,17},{17,1},{2,18},{18,2},{3,19},{19,3},{4,20},{20... | collective-permute-start | bytes 6291464 | tf_op jit(solution)/shard_map/ppermute | solution.py:318
  160.5 47.7 %collective-permute-start.43 = (bf16[4,128,2048]{2,1,0:T(8,128)(2,1)}, bf16[4,128,2048]{2,1,0:T(8,128)(2,1)}, u32[]{:S(2)}, u32[]{:S(2)}) collective-permute-start(bf16[4,128,2048]{2,1,0:T(8,128)(2,1)} %pad_maximum_fusion.5.refs_3_), channel_id=1, source_target_pairs={{0,16},{16,0},{1,17},{17,1},{2,18},{18,2},{3,19},{19,3},{4,20},{20... | collective-permute-start | bytes 6291464 | tf_op jit(solution)/shard_map/ppermute | solution.py:318
  161.2 47.1 %collective-permute-start.44 = (bf16[4,128,2048]{2,1,0:T(8,128)(2,1)}, bf16[4,128,2048]{2,1,0:T(8,128)(2,1)}, u32[]{:S(2)}, u32[]{:S(2)}) collective-permute-start(bf16[4,128,2048]{2,1,0:T(8,128)(2,1)} %pad_maximum_fusion.6.refs_4_), channel_id=1, source_target_pairs={{0,16},{16,0},{1,17},{17,1},{2,18},{18,2},{3,19},{19,3},{4,20},{20... | collective-permute-start | bytes 6291464 | tf_op jit(solution)/shard_map/ppermute | solution.py:318
  213.5 735.7 %reduce-scatter.2.cloned.1.call-start = ((), (), s32[]{:S(2)}) async-start(), calls=%async_computation.5 | async-start | bytes 13369344 | tf_op jit(solution)/shard_map/reduce_scatter | solution.py:826
  419.1 68.5 %collective-permute-start.78 = (bf16[96,2048]{1,0:T(8,128)(2,1)}, bf16[96,2048]{1,0:T(8,128)(2,1)}, u32[]{:S(2)}, u32[]{:S(2)}) collective-permute-start(bf16[96,2048]{1,0:T(8,128)(2,1)} %get-tuple-element.176), channel_id=1, source_target_pairs={{0,2},{1,3},{2,0},{3,1},{4,6},{5,7},{6,4},{7,5},{8,10},{9,11},{10,... | collective-permute-start | bytes 1179656 | tf_op jit(solution)/shard_map/ppermute | solution.py:310
  420.8 66.9 %collective-permute-start.80 = (bf16[96,2048]{1,0:T(8,128)(2,1)}, bf16[96,2048]{1,0:T(8,128)(2,1)}, u32[]{:S(2)}, u32[]{:S(2)}) collective-permute-start(bf16[96,2048]{1,0:T(8,128)(2,1)} %get-tuple-element.178), channel_id=1, source_target_pairs={{0,1},{1,0},{2,3},{3,2},{4,5},{5,4},{6,7},{7,6},{8,9},{9,8},{10,11... | collective-permute-start | bytes 1179656 | tf_op jit(solution)/shard_map/ppermute | solution.py:306
  439.6 51.7 %collective-permute-start.54 = (bf16[96,2048]{1,0:T(8,128)(2,1)}, bf16[96,2048]{1,0:T(8,128)(2,1)}, u32[]{:S(2)}, u32[]{:S(2)}) collective-permute-start(bf16[96,2048]{1,0:T(8,128)(2,1)} %get-tuple-element.164), channel_id=1, source_target_pairs={{0,2},{1,3},{2,0},{3,1},{4,6},{5,7},{6,4},{7,5},{8,10},{9,11},{10,... | collective-permute-start | bytes 1179656 | tf_op jit(solution)/shard_map/ppermute | solution.py:310
  441.3 50.9 %collective-permute-start.56 = (bf16[96,2048]{1,0:T(8,128)(2,1)}, bf16[96,2048]{1,0:T(8,128)(2,1)}, u32[]{:S(2)}, u32[]{:S(2)}) collective-permute-start(bf16[96,2048]{1,0:T(8,128)(2,1)} %get-tuple-element.166), channel_id=1, source_target_pairs={{0,1},{1,0},{2,3},{3,2},{4,5},{5,4},{6,7},{7,6},{8,9},{9,8},{10,11... | collective-permute-start | bytes 1179656 | tf_op jit(solution)/shard_map/ppermute | solution.py:306
  457.6 37.1 %collective-permute-start.64 = (bf16[96,2048]{1,0:T(8,128)(2,1)}, bf16[96,2048]{1,0:T(8,128)(2,1)}, u32[]{:S(2)}, u32[]{:S(2)}) collective-permute-start(bf16[96,2048]{1,0:T(8,128)(2,1)} %get-tuple-element.170), channel_id=1, source_target_pairs={{0,2},{1,3},{2,0},{3,1},{4,6},{5,7},{6,4},{7,5},{8,10},{9,11},{10,... | collective-permute-start | bytes 1179656 | tf_op jit(solution)/shard_map/ppermute | solution.py:310
  493.8 53.0 %collective-permute-start.55 = (bf16[192,2048]{1,0:T(8,128)(2,1)S(1)}, bf16[192,2048]{1,0:T(8,128)(2,1)S(1)}, u32[]{:S(2)}, u32[]{:S(2)}) collective-permute-start(bf16[192,2048]{1,0:T(8,128)(2,1)S(1)} %pad_maximum_fusion.12), channel_id=1, source_target_pairs={{0,1},{1,0},{2,3},{3,2},{4,5},{5,4},{6,7},{7,6},{8,9},{9,8},{10,11... | collective-permute-start | bytes 2359304 | tf_op jit(solution)/shard_map/ppermute | solution.py:306
  494.7 52.2 %collective-permute-start.57 = (bf16[192,2048]{1,0:T(8,128)(2,1)S(1)}, bf16[192,2048]{1,0:T(8,128)(2,1)S(1)}, u32[]{:S(2)}, u32[]{:S(2)}) collective-permute-start(bf16[192,2048]{1,0:T(8,128)(2,1)S(1)} %pad_maximum_fusion.13), channel_id=1, source_target_pairs={{0,2},{1,3},{2,0},{3,1},{4,6},{5,7},{6,4},{7,5},{8,10},{9,11},{10,... | collective-permute-start | bytes 2359304 | tf_op jit(solution)/shard_map/ppermute | solution.py:310
  501.0 60.0 %collective-permute-start.65 = (bf16[192,2048]{1,0:T(8,128)(2,1)S(1)}, bf16[192,2048]{1,0:T(8,128)(2,1)S(1)}, u32[]{:S(2)}, u32[]{:S(2)}) collective-permute-start(bf16[192,2048]{1,0:T(8,128)(2,1)S(1)} %pad_maximum_fusion.14), channel_id=1, source_target_pairs={{0,1},{1,0},{2,3},{3,2},{4,5},{5,4},{6,7},{7,6},{8,9},{9,8},{10,11... | collective-permute-start | bytes 2359304 | tf_op jit(solution)/shard_map/ppermute | solution.py:306
  516.5 44.5 %collective-permute-start.67 = (bf16[192,2048]{1,0:T(8,128)(2,1)S(1)}, bf16[192,2048]{1,0:T(8,128)(2,1)S(1)}, u32[]{:S(2)}, u32[]{:S(2)}) collective-permute-start(bf16[192,2048]{1,0:T(8,128)(2,1)S(1)} %pad_maximum_fusion.15), channel_id=1, source_target_pairs={{0,2},{1,3},{2,0},{3,1},{4,6},{5,7},{6,4},{7,5},{8,10},{9,11},{10,... | collective-permute-start | bytes 2359304 | tf_op jit(solution)/shard_map/ppermute | solution.py:310
  616.1 54.9 %collective-permute-start.46 = (bf16[192,1024]{1,0:T(8,128)(2,1)}, bf16[192,1024]{1,0:T(8,128)(2,1)}, u32[]{:S(2)}, u32[]{:S(2)}) collective-permute-start(bf16[192,1024]{1,0:T(8,128)(2,1)} %get-tuple-element.195), channel_id=1, source_target_pairs={{0,16},{16,0},{1,17},{17,1},{2,18},{18,2},{3,19},{19,3},{4,20},{20... | collective-permute-start | bytes 1179656 | tf_op jit(solution)/shard_map/ppermute | solution.py:318
  617.7 53.4 %collective-permute-start.47 = (bf16[192,1024]{0,1:T(8,128)(2,1)}, bf16[192,1024]{0,1:T(8,128)(2,1)}, u32[]{:S(2)}, u32[]{:S(2)}) collective-permute-start(bf16[192,1024]{0,1:T(8,128)(2,1)} %get-tuple-element.193), channel_id=1, source_target_pairs={{0,16},{16,0},{1,17},{17,1},{2,18},{18,2},{3,19},{19,3},{4,20},{20... | collective-permute-start | bytes 1179656 | tf_op jit(solution)/shard_map/ppermute | solution.py:318
  646.3 80.3 %collective-permute-start.102 = (bf16[2048,512]{1,0:T(8,128)(2,1)}, bf16[2048,512]{1,0:T(8,128)(2,1)}, u32[]{:S(2)}, u32[]{:S(2)}) collective-permute-start(bf16[2048,512]{1,0:T(8,128)(2,1)} %get-tuple-element.65), channel_id=1, source_target_pairs={{0,16},{16,0},{1,17},{17,1},{2,18},{18,2},{3,19},{19,3},{4,20},{20... | collective-permute-start | bytes 6291464 | tf_op jit(solution)/shard_map/ppermute | solution.py:318
  694.4 36.8 %collective-permute-start.95 = (bf16[256,2048]{1,0:T(8,128)(2,1)}, bf16[256,2048]{1,0:T(8,128)(2,1)S(1)}, u32[]{:S(2)}, u32[]{:S(2)}) collective-permute-start(bf16[256,2048]{1,0:T(8,128)(2,1)} %get-tuple-element.54), channel_id=1, source_target_pairs={{0,2},{1,3},{2,0},{3,1},{4,6},{5,7},{6,4},{7,5},{8,10},{9,11},{10,... | collective-permute-start | bytes 3145736 | tf_op jit(solution)/shard_map/ppermute | solution.py:310
  699.7 37.5 %collective-permute-start.97 = (bf16[256,2048]{1,0:T(8,128)(2,1)}, bf16[256,2048]{1,0:T(8,128)(2,1)S(1)}, u32[]{:S(2)}, u32[]{:S(2)}) collective-permute-start(bf16[256,2048]{1,0:T(8,128)(2,1)} %get-tuple-element.56), channel_id=1, source_target_pairs={{0,1},{1,0},{2,3},{3,2},{4,5},{5,4},{6,7},{7,6},{8,9},{9,8},{10,11... | collective-permute-start | bytes 3145736 | tf_op jit(solution)/shard_map/ppermute | solution.py:306
  720.9 44.4 %collective-permute-start.93 = (bf16[256,2048]{1,0:T(8,128)(2,1)}, bf16[256,2048]{1,0:T(8,128)(2,1)S(1)}, u32[]{:S(2)}, u32[]{:S(2)}) collective-permute-start(bf16[256,2048]{1,0:T(8,128)(2,1)} %get-tuple-element.51), channel_id=1, source_target_pairs={{0,1},{1,0},{2,3},{3,2},{4,5},{5,4},{6,7},{7,6},{8,9},{9,8},{10,11... | collective-permute-start | bytes 3145736 | tf_op jit(solution)/shard_map/ppermute | solution.py:306
  723.6 45.2 %collective-permute-start.91 = (bf16[256,2048]{1,0:T(8,128)(2,1)}, bf16[256,2048]{1,0:T(8,128)(2,1)S(1)}, u32[]{:S(2)}, u32[]{:S(2)}) collective-permute-start(bf16[256,2048]{1,0:T(8,128)(2,1)} %get-tuple-element.49), channel_id=1, source_target_pairs={{0,2},{1,3},{2,0},{3,1},{4,6},{5,7},{6,4},{7,5},{8,10},{9,11},{10,... | collective-permute-start | bytes 3145736 | tf_op jit(solution)/shard_map/ppermute | solution.py:310
  734.0 87.5 %collective-permute-start.96 = (bf16[512,2048]{1,0:T(8,128)(2,1)}, bf16[512,2048]{1,0:T(8,128)(2,1)S(1)}, u32[]{:S(2)}, u32[]{:S(2)}) collective-permute-start(bf16[512,2048]{1,0:T(8,128)(2,1)} %pad_maximum_fusion.10), channel_id=1, source_target_pairs={{0,1},{1,0},{2,3},{3,2},{4,5},{5,4},{6,7},{7,6},{8,9},{9,8},{10,11... | collective-permute-start | bytes 6291464 | tf_op jit(solution)/shard_map/ppermute | solution.py:306
  739.2 89.5 %collective-permute-start.98 = (bf16[512,2048]{1,0:T(8,128)(2,1)}, bf16[512,2048]{1,0:T(8,128)(2,1)}, u32[]{:S(2)}, u32[]{:S(2)}) collective-permute-start(bf16[512,2048]{1,0:T(8,128)(2,1)} %pad_maximum_fusion.11), channel_id=1, source_target_pairs={{0,2},{1,3},{2,0},{3,1},{4,6},{5,7},{6,4},{7,5},{8,10},{9,11},{10,... | collective-permute-start | bytes 6291464 | tf_op jit(solution)/shard_map/ppermute | solution.py:310
  767.3 142.7 %collective-permute-start.94 = (bf16[512,2048]{1,0:T(8,128)(2,1)}, bf16[512,2048]{1,0:T(8,128)(2,1)}, u32[]{:S(2)}, u32[]{:S(2)}) collective-permute-start(bf16[512,2048]{1,0:T(8,128)(2,1)} %pad_maximum_fusion.9), channel_id=1, source_target_pairs={{0,2},{1,3},{2,0},{3,1},{4,6},{5,7},{6,4},{7,5},{8,10},{9,11},{10,... | collective-permute-start | bytes 6291464 | tf_op jit(solution)/shard_map/ppermute | solution.py:310
  770.9 139.2 %collective-permute-start.92 = (bf16[512,2048]{1,0:T(8,128)(2,1)}, bf16[512,2048]{1,0:T(8,128)(2,1)}, u32[]{:S(2)}, u32[]{:S(2)}) collective-permute-start(bf16[512,2048]{1,0:T(8,128)(2,1)} %pad_maximum_fusion.8), channel_id=1, source_target_pairs={{0,1},{1,0},{2,3},{3,2},{4,5},{5,4},{6,7},{7,6},{8,9},{9,8},{10,11... | collective-permute-start | bytes 6291464 | tf_op jit(solution)/shard_map/ppermute | solution.py:306
  835.2 44.6 %collective-permute-start.99 = (bf16[256,2048]{1,0:T(8,128)(2,1)S(1)}, bf16[256,2048]{1,0:T(8,128)(2,1)S(1)}, u32[]{:S(2)}, u32[]{:S(2)}) collective-permute-start(bf16[256,2048]{1,0:T(8,128)(2,1)S(1)} %split.69), channel_id=1, source_target_pairs={{0,4},{1,5},{2,6},{3,7},{4,8},{5,9},{6,10},{7,11},{8,12},{9,13},{1... | collective-permute-start | bytes 3145736 | tf_op jit(solution)/shard_map/ppermute | solution.py:314
  855.8 65.5 %collective-permute-start.103 = (bf16[2048,512]{1,0:T(8,128)(2,1)}, bf16[2048,512]{1,0:T(8,128)(2,1)}, u32[]{:S(2)}, u32[]{:S(2)}) collective-permute-start(bf16[2048,512]{1,0:T(8,128)(2,1)} %get-tuple-element.67), channel_id=1, source_target_pairs={{0,16},{16,0},{1,17},{17,1},{2,18},{18,2},{3,19},{19,3},{4,20},{20... | collective-permute-start | bytes 6291464 | tf_op jit(solution)/shard_map/ppermute | solution.py:318
  856.8 63.1 %all-to-all-start.2 = ((f32[32,1,1280]{2,1,0:T(1,128)}), f32[32,1,1280]{2,1,0:T(1,128)S(1)}, u32[]{:S(2)}, u32[]{:S(2)}) async-start(f32[32,1,1280]{2,1,0:T(1,128)} %copy.134), calls=%async_computation.3 | async-start | bytes 327680 | tf_op jit(solution)/shard_map/all_to_all | solution.py:900
  910.1 34.8 %collective-permute-start.104 = (bf16[512,2048]{1,0:T(8,128)(2,1)}, bf16[512,2048]{1,0:T(8,128)(2,1)}, u32[]{:S(2)}, u32[]{:S(2)}) collective-permute-start(bf16[512,2048]{1,0:T(8,128)(2,1)} %get-tuple-element.69), channel_id=1, source_target_pairs={{0,16},{16,0},{1,17},{17,1},{2,18},{18,2},{3,19},{19,3},{4,20},{20... | collective-permute-start | bytes 6291464 | tf_op jit(solution)/shard_map/ppermute | solution.py:318
  (218 other events, 3104.7 us)
Sparse Core Ops, SparseCore 0:
  70.9 190.4 all-gather.1
  615.2 268.0 reduce-scatter.1

commit v6 on v5

--- a/solution.py
+++ b/solution.py
@@ -372,13 +372,17 @@
         for step, part in zip(steps, jnp.split(total, len(steps), axis=0), strict=True):
             self.planes[step] = part
 
-    def push(self):
+    def push(self, before=None):
         while self.steps + 1 < NZ and self.steps + 1 in self.planes:
             self.steps += 1
             total = self.planes[self.steps]
             if self.total is not None:
                 total = add_f32(self.total, total)
-            self.total = move_z(total.astype(jnp.bfloat16))
+            total = total.astype(jnp.bfloat16)
+            if before is not None and self.steps == NZ - 1:
+                total, before = tie(total, before)
+            self.total = move_z(total)
+        return before
 
     def result(self):
         self.push()
@@ -807,6 +811,7 @@
         all_outs = lax.dynamic_update_slice(all_outs, forward[s][7][None], (planes[s], 0, 0))
     expert_acts = [chunk[0] for chunk in forward]
     gate_grads = [chunk[1] for chunk in backward]
+    choice_grad = rows_reduce.push(choice_grad)
     moe_in_grad = rows_reduce.result()
     own_gate, other_gate = column_grads(
         position, expert_acts, gate_grads, waits=(rows_reduce.planes[3],)

time: 969 us -> 957 us (0.988)
  waiting for transfers between devices: 345 us -> 327 us
    ppermute x15, waiting for transfers between devices: 68.3 us -> 48.1 us  [move_z(): return lax.ppermute(values, 'expert', Z_PAIRS)]
    reduce_sum x2 -> x0, other arithmetic: 11.6 us -> none  [body_dense(): jnp.sum(upstream_f32 * expert_out.astype(f32), axis=-1, keepdims=True)]
    ppermute x36, waiting for transfers between devices: 166 us -> 176 us  [move_x(): return lax.ppermute(values, 'expert', X_PAIRS)]
    unnamed x284 -> x283, local copies, waits for them, and re-layouts: 28.1 us -> 30.9 us
where the time goes in v6:
time: 957 us; the launch traced here: 949 us
  waiting for transfers between devices  327 us (34%)
  matrix products  157 us (16%)
  Pallas kernels  146 us (15%)
  starting transfers between devices  115 us (12%)
  other arithmetic  103 us (11%)
  local copies, waits for them, and re-layouts  84.1 us (9%)
  between operations  17.1 us (2%)
    ppermute x36, waiting for transfers between devices, move_x(): return lax.ppermute(values, 'expert', X_PAIRS)  176 us
    ppermute x36, waiting for transfers between devices, move_y(): return lax.ppermute(values, 'expert', Y_PAIRS)  90.7 us
    dot_general x13, matrix products, times_transposed(): jnp.einsum('ta,ba->tb', left, right, preferred_element_type=jnp.float32)  59.8 us
    pallas_call x8, Pallas kernels, apply_weight(): pl.pallas_call(without(functools.partial(apply_back_kernel if back else a...  50.4 us
    ppermute x15, waiting for transfers between devices, move_z(): return lax.ppermute(values, 'expert', Z_PAIRS)  48.1 us
    ppermute x36, starting transfers between devices, move_x(): return lax.ppermute(values, 'expert', X_PAIRS)  41.7 us
    pallas_call x2, Pallas kernels, column_grads(): pl.pallas_call(without(column_grad_kernel, 1 + 2 * parts, len(waits)), gr...  38.7 us
    ppermute x36, starting transfers between devices, move_y(): return lax.ppermute(values, 'expert', Y_PAIRS)  37.7 us
  transfers between devices with their start and end apart: 110, of which 45 were waited for; matrix products, arithmetic and copies ran while one was open for 28% of the time, Pallas kernels for 15%

profile of v6, /device:TPU:0, one launch (start us, length us, event | category | flops | bytes accessed | tf_op | source)
XLA Modules:
  0.0 948.7 jit_solution(11167754383914882110)
XLA Ops:
  19.4 7.7 collective-permute-done.1
  29.2 8.3 collective-permute-done.27
  71.2 7.7 collective-permute-done.6
  97.9 11.8 %collective-permute-done.34 = bf16[128,2048]{1,0:T(8,128)(2,1)S(1)} collective-permute-done((bf16[128,2048]{1,0:T(8,128)(2,1)}, bf16[128,2048]{1,0:T(8,128)(2,1)S(1)}, u32[]{:S(2)}, u32[]{:S(2)}) %collective-permute-start.34) | collective-permute-done | bytes 524320 | tf_op jit(solution)/shard_map/ppermute | solution.py:310
  118.7 14.1 %collective-permute-done.35 = bf16[64,2048]{1,0:T(8,128)(2,1)S(1)} collective-permute-done((bf16[64,2048]{1,0:T(8,128)(2,1)S(1)}, bf16[64,2048]{1,0:T(8,128)(2,1)S(1)}, u32[]{:S(2)}, u32[]{:S(2)}) %collective-permute-start.35) | collective-permute-done | bytes 262176 | tf_op jit(solution)/shard_map/ppermute | solution.py:306
  142.0 18.5 %collective-permute-done.12 = bf16[64,2048]{1,0:T(8,128)(2,1)S(1)} collective-permute-done((bf16[64,2048]{1,0:T(8,128)(2,1)S(1)}, bf16[64,2048]{1,0:T(8,128)(2,1)S(1)}, u32[]{:S(2)}, u32[]{:S(2)}) %collective-permute-start.12) | collective-permute-done | bytes 262176 | tf_op jit(solution)/shard_map/ppermute | solution.py:306
  180.7 9.3 collective-permute-done.40
  196.1 7.9 collective-permute-done.17
  269.4 14.6 %collective-permute-done.75 = bf16[192,2048]{1,0:T(8,128)(2,1)} collective-permute-done((bf16[192,2048]{1,0:T(8,128)(2,1)}, bf16[192,2048]{1,0:T(8,128)(2,1)}, u32[]{:S(2)}, u32[]{:S(2)}) %collective-permute-start.75) | collective-permute-done | bytes 786464 | tf_op jit(solution)/shard_map/ppermute | solution.py:310
  334.1 6.8 collective-permute-done.61
  345.8 7.3 collective-permute-done.62
  383.1 8.6 fusion.60
  400.4 8.0 multiply_convert_fusion.4
  420.6 7.8 multiply_convert_fusion.3
  441.0 7.4 multiply_convert_fusion.2
  464.7 8.9 fusion.85
  479.2 11.7 %fusion.14 = (f32[768]{0:T(1024)S(1)}, f32[768]{0:T(1024)S(1)}, f32[768]{0:T(1024)S(1)}, bf16[768,2048]{1,0:T(8,128)(2,1)}, bf16[768,2048]{1,0:T(8,128)(2,1)}, /...) fusion(bf16[4,768,2048]{2,1,0:T(8,128)(2,1)} %bitcast.534, s32[]{:T(128)S(6)} %select_n.137, ...), kind=kOutput, calls=%fused_computation.29 | convolution fusion | flops 3251107584 | bytes 34097164 | tf_op jit(solution)/shard_map/dot_general | solution.py:772
  509.4 14.9 %collective-permute-done.79 = bf16[192,2048]{1,0:T(8,128)(2,1)S(1)} collective-permute-done((bf16[192,2048]{1,0:T(8,128)(2,1)S(1)}, bf16[192,2048]{1,0:T(8,128)(2,1)S(1)}, u32[]{:S(2)}, u32[]{:S(2)}) %collective-permute-start.79) | collective-permute-done | bytes 786464 | tf_op jit(solution)/shard_map/ppermute | solution.py:306
  533.2 9.0 multiply_convert_fusion.1
  547.7 8.0 add_convert_fusion
  559.7 7.5 collective-permute-done.82
  573.6 7.3 collective-permute-done.58
  607.8 19.2 %shard_map.267 = (f32[2048,512]{1,0:T(8,128)}, bf16[2048,512]{1,0:T(8,128)(2,1)}) custom-call(s32[5]{0:T(128)} %copy-done.17, bf16[768,2048]{1,0:T(8,128)(2,1)} %bitcast.485, bf16[768,2048]{1,0:T(8,128)(2,1)} %bitcast.490, bf16[768,2048]{1,0:T(8,128)(2,1)} %bitcast.495, bf16[768,2048]{1,0:T(8,128)(2,1)} %bitcast.500, bf16[768,1024]{1,0:T(8,128)(2,1)} %copy-done.134, ...), custom_call_target="tpu_custom_call" | custom-call | flops 12884901888 | bytes 25165824 | tf_op jit(solution)/shard_map/pallas_call | solution.py:561
  638.8 6.9 shard_map.268
  668.0 15.3 %shard_map.270 = (bf16[512,2048]{1,0:T(8,128)(2,1)}, bf16[512,2048]{1,0:T(8,128)(2,1)}, bf16[512,2048]{1,0:T(8,128)(2,1)}, bf16[256,2048]{1,0:T(8,128)(2,1)}, bf16[256,2048]{1,0:T(8,128)(2,1)}) custom-call(s32[5]{0:T(128)S(1)} %copy-done.18, bf16[1024,192]{1,0:T(8,128)(2,1)S(1)} %copy-done.11, bf16[1024,192]{1,0:T(8,128)(2,1)S(1)} %copy-done.13, ...), custom_call_target="tpu_custom_call" | custom-call | flops 3221225472 | bytes 16252928 | tf_op jit(solution)/shard_map/pallas_call | solution.py:519
  694.2 15.4 %shard_map.269 = (bf16[512,2048]{1,0:T(8,128)(2,1)}, bf16[512,2048]{1,0:T(8,128)(2,1)}, bf16[512,2048]{1,0:T(8,128)(2,1)}, bf16[256,2048]{1,0:T(8,128)(2,1)}, bf16[256,2048]{1,0:T(8,128)(2,1)}) custom-call(s32[5]{0:T(128)S(1)} %copy-done.18, bf16[1024,192]{1,0:T(8,128)(2,1)S(1)} %copy-done.12, bf16[1024,192]{1,0:T(8,128)(2,1)S(1)} %copy-done.14, ...), custom_call_target="tpu_custom_call" | custom-call | flops 3221225472 | bytes 16252928 | tf_op jit(solution)/shard_map/pallas_call | solution.py:519
  727.7 30.3 %collective-permute-done.93 = bf16[256,2048]{1,0:T(8,128)(2,1)S(1)} collective-permute-done((bf16[256,2048]{1,0:T(8,128)(2,1)}, bf16[256,2048]{1,0:T(8,128)(2,1)S(1)}, u32[]{:S(2)}, u32[]{:S(2)}) %collective-permute-start.93) | collective-permute-done | bytes 1048608 | tf_op jit(solution)/shard_map/ppermute | solution.py:306
  784.8 35.0 %collective-permute-done.96 = bf16[512,2048]{1,0:T(8,128)(2,1)S(1)} collective-permute-done((bf16[512,2048]{1,0:T(8,128)(2,1)}, bf16[512,2048]{1,0:T(8,128)(2,1)S(1)}, u32[]{:S(2)}, u32[]{:S(2)}) %collective-permute-start.96) | collective-permute-done | bytes 2097184 | tf_op jit(solution)/shard_map/ppermute | solution.py:306
  827.5 19.6 %shard_map.274 = (f32[2048,512]{1,0:T(8,128)}, bf16[2048,512]{1,0:T(8,128)(2,1)}) custom-call(s32[5]{0:T(128)} %copy-done.17, bf16[768,2048]{1,0:T(8,128)(2,1)} %bitcast.486, bf16[768,2048]{1,0:T(8,128)(2,1)} %bitcast.491, bf16[768,2048]{1,0:T(8,128)(2,1)} %bitcast.496, bf16[768,2048]{1,0:T(8,128)(2,1)} %bitcast.501, ...), custom_call_target="tpu_custom_call" | custom-call | flops 12884901888 | bytes 25165824 | tf_op jit(solution)/shard_map/pallas_call | solution.py:561
  858.2 25.8 %shard_map.275 = (f32[512,2048]{1,0:T(8,128)}, bf16[512,2048]{1,0:T(8,128)(2,1)}) custom-call(s32[5]{0:T(128)} %copy-done.17, bf16[768,1024]{1,0:T(8,128)(2,1)} %get-tuple-element.150.refs_1_, bf16[768,1024]{1,0:T(8,128)(2,1)} %get-tuple-element.153.refs_2_, bf16[768,1024]{1,0:T(8,128)(2,1)} %get-tuple-element.156.refs_3_, ...), custom_call_target="tpu_custom_call" | custom-call | flops 12884901888 | bytes 25165824 | tf_op jit(solution)/shard_map/pallas_call | solution.py:618
  884.0 14.9 %collective-permute-done.100 = bf16[256,2048]{1,0:T(8,128)(2,1)S(1)} collective-permute-done((bf16[256,2048]{1,0:T(8,128)(2,1)}, bf16[256,2048]{1,0:T(8,128)(2,1)S(1)}, u32[]{:S(2)}, u32[]{:S(2)}) %collective-permute-start.100) | collective-permute-done | bytes 1048608 | tf_op jit(solution)/shard_map/ppermute | solution.py:314
  915.4 16.8 %collective-permute-done.101 = bf16[256,2048]{1,0:T(8,128)(2,1)S(1)} collective-permute-done((bf16[256,2048]{1,0:T(8,128)(2,1)}, bf16[256,2048]{1,0:T(8,128)(2,1)S(1)}, u32[]{:S(2)}, u32[]{:S(2)}) %collective-permute-start.101) | collective-permute-done | bytes 1048608 | tf_op jit(solution)/shard_map/ppermute | solution.py:314
  (723 shorter events, 519.4 us)
Async XLA Ops:
  7.2 375.9 %all-gather.2.cloned.1.call-start = ((), (), s32[]{:S(2)}) async-start(), calls=%async_computation.4 | async-start | bytes 13369344 | tf_op jit(solution)/shard_map/all_gather | solution.py:691
  79.0 33.9 %collective-permute-start.11 = (bf16[128,2048]{1,0:T(8,128)(2,1)}, bf16[128,2048]{1,0:T(8,128)(2,1)S(1)}, u32[]{:S(2)}, u32[]{:S(2)}) collective-permute-start(bf16[128,2048]{1,0:T(8,128)(2,1)} %copy-done.85), channel_id=1, source_target_pairs={{0,2},{1,3},{2,0},{3,1},{4,6},{5,7},{6,4},{7,5},{8,10},{9,11},{10,... | collective-permute-start | bytes 1572872 | tf_op jit(solution)/shard_map/ppermute | solution.py:310
  79.5 35.0 %collective-permute-start.10 = (bf16[128,2048]{1,0:T(8,128)(2,1)}, bf16[128,2048]{1,0:T(8,128)(2,1)S(1)}, u32[]{:S(2)}, u32[]{:S(2)}) collective-permute-start(bf16[128,2048]{1,0:T(8,128)(2,1)} %copy-done.85), channel_id=1, source_target_pairs={{0,1},{1,0},{2,3},{3,2},{4,5},{5,4},{6,7},{7,6},{8,9},{9,8},{10,11... | collective-permute-start | bytes 1572872 | tf_op jit(solution)/shard_map/ppermute | solution.py:306
  81.0 35.0 %collective-permute-start.37 = (bf16[128,2048]{1,0:T(8,128)(2,1)}, bf16[128,2048]{1,0:T(8,128)(2,1)}, u32[]{:S(2)}, u32[]{:S(2)}) collective-permute-start(bf16[128,2048]{1,0:T(8,128)(2,1)} %collective-permute-done.32), channel_id=1, source_target_pairs={{0,4},{1,5},{2,6},{3,7},{4,8},{5,9},{6,10},{7,11},{8,12},{9,13},{1... | collective-permute-start | bytes 1572872 | tf_op jit(solution)/shard_map/ppermute | solution.py:314
  142.0 65.7 %collective-permute-start.42 = (bf16[4,128,2048]{2,1,0:T(8,128)(2,1)}, bf16[4,128,2048]{2,1,0:T(8,128)(2,1)}, u32[]{:S(2)}, u32[]{:S(2)}) collective-permute-start(bf16[4,128,2048]{2,1,0:T(8,128)(2,1)} %pad_maximum_fusion.4.refs_2_), channel_id=1, source_target_pairs={{0,16},{16,0},{1,17},{17,1},{2,18},{18,2},{3,19},{19,3},{4,20},{20... | collective-permute-start | bytes 6291464 | tf_op jit(solution)/shard_map/ppermute | solution.py:318
  160.5 47.7 %collective-permute-start.43 = (bf16[4,128,2048]{2,1,0:T(8,128)(2,1)}, bf16[4,128,2048]{2,1,0:T(8,128)(2,1)}, u32[]{:S(2)}, u32[]{:S(2)}) collective-permute-start(bf16[4,128,2048]{2,1,0:T(8,128)(2,1)} %pad_maximum_fusion.5.refs_3_), channel_id=1, source_target_pairs={{0,16},{16,0},{1,17},{17,1},{2,18},{18,2},{3,19},{19,3},{4,20},{20... | collective-permute-start | bytes 6291464 | tf_op jit(solution)/shard_map/ppermute | solution.py:318
  161.2 47.1 %collective-permute-start.44 = (bf16[4,128,2048]{2,1,0:T(8,128)(2,1)}, bf16[4,128,2048]{2,1,0:T(8,128)(2,1)}, u32[]{:S(2)}, u32[]{:S(2)}) collective-permute-start(bf16[4,128,2048]{2,1,0:T(8,128)(2,1)} %pad_maximum_fusion.6.refs_4_), channel_id=1, source_target_pairs={{0,16},{16,0},{1,17},{17,1},{2,18},{18,2},{3,19},{19,3},{4,20},{20... | collective-permute-start | bytes 6291464 | tf_op jit(solution)/shard_map/ppermute | solution.py:318
  418.2 77.2 %collective-permute-start.78 = (bf16[96,2048]{1,0:T(8,128)(2,1)}, bf16[96,2048]{1,0:T(8,128)(2,1)}, u32[]{:S(2)}, u32[]{:S(2)}) collective-permute-start(bf16[96,2048]{1,0:T(8,128)(2,1)} %get-tuple-element.180), channel_id=1, source_target_pairs={{0,2},{1,3},{2,0},{3,1},{4,6},{5,7},{6,4},{7,5},{8,10},{9,11},{10,... | collective-permute-start | bytes 1179656 | tf_op jit(solution)/shard_map/ppermute | solution.py:310
  419.9 76.0 %collective-permute-start.80 = (bf16[96,2048]{1,0:T(8,128)(2,1)}, bf16[96,2048]{1,0:T(8,128)(2,1)}, u32[]{:S(2)}, u32[]{:S(2)}) collective-permute-start(bf16[96,2048]{1,0:T(8,128)(2,1)} %get-tuple-element.182), channel_id=1, source_target_pairs={{0,1},{1,0},{2,3},{3,2},{4,5},{5,4},{6,7},{7,6},{8,9},{9,8},{10,11... | collective-permute-start | bytes 1179656 | tf_op jit(solution)/shard_map/ppermute | solution.py:306
  438.6 60.5 %collective-permute-start.54 = (bf16[96,2048]{1,0:T(8,128)(2,1)}, bf16[96,2048]{1,0:T(8,128)(2,1)}, u32[]{:S(2)}, u32[]{:S(2)}) collective-permute-start(bf16[96,2048]{1,0:T(8,128)(2,1)} %get-tuple-element.168), channel_id=1, source_target_pairs={{0,2},{1,3},{2,0},{3,1},{4,6},{5,7},{6,4},{7,5},{8,10},{9,11},{10,... | collective-permute-start | bytes 1179656 | tf_op jit(solution)/shard_map/ppermute | solution.py:310
  440.4 59.1 %collective-permute-start.56 = (bf16[96,2048]{1,0:T(8,128)(2,1)}, bf16[96,2048]{1,0:T(8,128)(2,1)}, u32[]{:S(2)}, u32[]{:S(2)}) collective-permute-start(bf16[96,2048]{1,0:T(8,128)(2,1)} %get-tuple-element.170), channel_id=1, source_target_pairs={{0,1},{1,0},{2,3},{3,2},{4,5},{5,4},{6,7},{7,6},{8,9},{9,8},{10,11... | collective-permute-start | bytes 1179656 | tf_op jit(solution)/shard_map/ppermute | solution.py:306
  456.7 45.7 %collective-permute-start.64 = (bf16[96,2048]{1,0:T(8,128)(2,1)}, bf16[96,2048]{1,0:T(8,128)(2,1)}, u32[]{:S(2)}, u32[]{:S(2)}) collective-permute-start(bf16[96,2048]{1,0:T(8,128)(2,1)} %get-tuple-element.174), channel_id=1, source_target_pairs={{0,2},{1,3},{2,0},{3,1},{4,6},{5,7},{6,4},{7,5},{8,10},{9,11},{10,... | collective-permute-start | bytes 1179656 | tf_op jit(solution)/shard_map/ppermute | solution.py:310
  501.0 56.7 %collective-permute-start.55 = (bf16[192,2048]{1,0:T(8,128)(2,1)S(1)}, bf16[192,2048]{1,0:T(8,128)(2,1)S(1)}, u32[]{:S(2)}, u32[]{:S(2)}) collective-permute-start(bf16[192,2048]{1,0:T(8,128)(2,1)S(1)} %pad_maximum_fusion.12), channel_id=1, source_target_pairs={{0,1},{1,0},{2,3},{3,2},{4,5},{5,4},{6,7},{7,6},{8,9},{9,8},{10,11... | collective-permute-start | bytes 2359304 | tf_op jit(solution)/shard_map/ppermute | solution.py:306
  502.5 55.6 %collective-permute-start.57 = (bf16[192,2048]{1,0:T(8,128)(2,1)S(1)}, bf16[192,2048]{1,0:T(8,128)(2,1)S(1)}, u32[]{:S(2)}, u32[]{:S(2)}) collective-permute-start(bf16[192,2048]{1,0:T(8,128)(2,1)S(1)} %pad_maximum_fusion.13), channel_id=1, source_target_pairs={{0,2},{1,3},{2,0},{3,1},{4,6},{5,7},{6,4},{7,5},{8,10},{9,11},{10,... | collective-permute-start | bytes 2359304 | tf_op jit(solution)/shard_map/ppermute | solution.py:310
  508.9 64.7 %collective-permute-start.65 = (bf16[192,2048]{1,0:T(8,128)(2,1)S(1)}, bf16[192,2048]{1,0:T(8,128)(2,1)S(1)}, u32[]{:S(2)}, u32[]{:S(2)}) collective-permute-start(bf16[192,2048]{1,0:T(8,128)(2,1)S(1)} %pad_maximum_fusion.14), channel_id=1, source_target_pairs={{0,1},{1,0},{2,3},{3,2},{4,5},{5,4},{6,7},{7,6},{8,9},{9,8},{10,11... | collective-permute-start | bytes 2359304 | tf_op jit(solution)/shard_map/ppermute | solution.py:306
  524.4 49.2 %collective-permute-start.67 = (bf16[192,2048]{1,0:T(8,128)(2,1)S(1)}, bf16[192,2048]{1,0:T(8,128)(2,1)S(1)}, u32[]{:S(2)}, u32[]{:S(2)}) collective-permute-start(bf16[192,2048]{1,0:T(8,128)(2,1)S(1)} %pad_maximum_fusion.15), channel_id=1, source_target_pairs={{0,2},{1,3},{2,0},{3,1},{4,6},{5,7},{6,4},{7,5},{8,10},{9,11},{10,... | collective-permute-start | bytes 2359304 | tf_op jit(solution)/shard_map/ppermute | solution.py:310
  571.0 32.6 %collective-permute-start.83 = (bf16[192,2048]{1,0:T(8,128)(2,1)}, bf16[192,2048]{1,0:T(8,128)(2,1)}, u32[]{:S(2)}, u32[]{:S(2)}) collective-permute-start(bf16[192,2048]{1,0:T(8,128)(2,1)} %pad_maximum_fusion.18), channel_id=1, source_target_pairs={{0,1},{1,0},{2,3},{3,2},{4,5},{5,4},{6,7},{7,6},{8,9},{9,8},{10,11... | collective-permute-start | bytes 2359304 | tf_op jit(solution)/shard_map/ppermute | solution.py:306
  572.3 31.2 %collective-permute-start.85 = (bf16[192,2048]{1,0:T(8,128)(2,1)}, bf16[192,2048]{1,0:T(8,128)(2,1)}, u32[]{:S(2)}, u32[]{:S(2)}) collective-permute-start(bf16[192,2048]{1,0:T(8,128)(2,1)} %pad_maximum_fusion.19), channel_id=1, source_target_pairs={{0,2},{1,3},{2,0},{3,1},{4,6},{5,7},{6,4},{7,5},{8,10},{9,11},{10,... | collective-permute-start | bytes 2359304 | tf_op jit(solution)/shard_map/ppermute | solution.py:310
  593.9 343.0 %reduce-scatter.2.cloned.1.call-start = ((), (), s32[]{:S(2)}) async-start(), calls=%async_computation.5 | async-start | bytes 13369344 | tf_op jit(solution)/shard_map/reduce_scatter | solution.py:831
  635.2 79.3 %collective-permute-start.102 = (bf16[2048,512]{1,0:T(8,128)(2,1)}, bf16[2048,512]{1,0:T(8,128)(2,1)}, u32[]{:S(2)}, u32[]{:S(2)}) collective-permute-start(bf16[2048,512]{1,0:T(8,128)(2,1)} %get-tuple-element.69), channel_id=1, source_target_pairs={{0,16},{16,0},{1,17},{17,1},{2,18},{18,2},{3,19},{19,3},{4,20},{20... | collective-permute-start | bytes 6291464 | tf_op jit(solution)/shard_map/ppermute | solution.py:318
  683.3 36.8 %collective-permute-start.95 = (bf16[256,2048]{1,0:T(8,128)(2,1)}, bf16[256,2048]{1,0:T(8,128)(2,1)S(1)}, u32[]{:S(2)}, u32[]{:S(2)}) collective-permute-start(bf16[256,2048]{1,0:T(8,128)(2,1)} %get-tuple-element.58), channel_id=1, source_target_pairs={{0,2},{1,3},{2,0},{3,1},{4,6},{5,7},{6,4},{7,5},{8,10},{9,11},{10,... | collective-permute-start | bytes 3145736 | tf_op jit(solution)/shard_map/ppermute | solution.py:310
  688.6 35.7 %collective-permute-start.97 = (bf16[256,2048]{1,0:T(8,128)(2,1)}, bf16[256,2048]{1,0:T(8,128)(2,1)S(1)}, u32[]{:S(2)}, u32[]{:S(2)}) collective-permute-start(bf16[256,2048]{1,0:T(8,128)(2,1)} %get-tuple-element.60), channel_id=1, source_target_pairs={{0,1},{1,0},{2,3},{3,2},{4,5},{5,4},{6,7},{7,6},{8,9},{9,8},{10,11... | collective-permute-start | bytes 3145736 | tf_op jit(solution)/shard_map/ppermute | solution.py:306
  709.6 48.4 %collective-permute-start.93 = (bf16[256,2048]{1,0:T(8,128)(2,1)}, bf16[256,2048]{1,0:T(8,128)(2,1)S(1)}, u32[]{:S(2)}, u32[]{:S(2)}) collective-permute-start(bf16[256,2048]{1,0:T(8,128)(2,1)} %get-tuple-element.55), channel_id=1, source_target_pairs={{0,1},{1,0},{2,3},{3,2},{4,5},{5,4},{6,7},{7,6},{8,9},{9,8},{10,11... | collective-permute-start | bytes 3145736 | tf_op jit(solution)/shard_map/ppermute | solution.py:306
  711.5 49.9 %collective-permute-start.91 = (bf16[256,2048]{1,0:T(8,128)(2,1)}, bf16[256,2048]{1,0:T(8,128)(2,1)S(1)}, u32[]{:S(2)}, u32[]{:S(2)}) collective-permute-start(bf16[256,2048]{1,0:T(8,128)(2,1)} %get-tuple-element.53), channel_id=1, source_target_pairs={{0,2},{1,3},{2,0},{3,1},{4,6},{5,7},{6,4},{7,5},{8,10},{9,11},{10,... | collective-permute-start | bytes 3145736 | tf_op jit(solution)/shard_map/ppermute | solution.py:310
  722.0 97.8 %collective-permute-start.96 = (bf16[512,2048]{1,0:T(8,128)(2,1)}, bf16[512,2048]{1,0:T(8,128)(2,1)S(1)}, u32[]{:S(2)}, u32[]{:S(2)}) collective-permute-start(bf16[512,2048]{1,0:T(8,128)(2,1)} %pad_maximum_fusion.10), channel_id=1, source_target_pairs={{0,1},{1,0},{2,3},{3,2},{4,5},{5,4},{6,7},{7,6},{8,9},{9,8},{10,11... | collective-permute-start | bytes 6291464 | tf_op jit(solution)/shard_map/ppermute | solution.py:306
  726.3 93.5 %collective-permute-start.98 = (bf16[512,2048]{1,0:T(8,128)(2,1)}, bf16[512,2048]{1,0:T(8,128)(2,1)}, u32[]{:S(2)}, u32[]{:S(2)}) collective-permute-start(bf16[512,2048]{1,0:T(8,128)(2,1)} %pad_maximum_fusion.11), channel_id=1, source_target_pairs={{0,2},{1,3},{2,0},{3,1},{4,6},{5,7},{6,4},{7,5},{8,10},{9,11},{10,... | collective-permute-start | bytes 6291464 | tf_op jit(solution)/shard_map/ppermute | solution.py:310
  760.0 124.0 %collective-permute-start.94 = (bf16[512,2048]{1,0:T(8,128)(2,1)}, bf16[512,2048]{1,0:T(8,128)(2,1)}, u32[]{:S(2)}, u32[]{:S(2)}) collective-permute-start(bf16[512,2048]{1,0:T(8,128)(2,1)} %pad_maximum_fusion.9), channel_id=1, source_target_pairs={{0,2},{1,3},{2,0},{3,1},{4,6},{5,7},{6,4},{7,5},{8,10},{9,11},{10,... | collective-permute-start | bytes 6291464 | tf_op jit(solution)/shard_map/ppermute | solution.py:310
  763.4 120.6 %collective-permute-start.92 = (bf16[512,2048]{1,0:T(8,128)(2,1)}, bf16[512,2048]{1,0:T(8,128)(2,1)}, u32[]{:S(2)}, u32[]{:S(2)}) collective-permute-start(bf16[512,2048]{1,0:T(8,128)(2,1)} %pad_maximum_fusion.8), channel_id=1, source_target_pairs={{0,1},{1,0},{2,3},{3,2},{4,5},{5,4},{6,7},{7,6},{8,9},{9,8},{10,11... | collective-permute-start | bytes 6291464 | tf_op jit(solution)/shard_map/ppermute | solution.py:306
  847.0 62.7 %collective-permute-start.103 = (bf16[2048,512]{1,0:T(8,128)(2,1)}, bf16[2048,512]{1,0:T(8,128)(2,1)}, u32[]{:S(2)}, u32[]{:S(2)}) collective-permute-start(bf16[2048,512]{1,0:T(8,128)(2,1)} %get-tuple-element.71), channel_id=1, source_target_pairs={{0,16},{16,0},{1,17},{17,1},{2,18},{18,2},{3,19},{19,3},{4,20},{20... | collective-permute-start | bytes 6291464 | tf_op jit(solution)/shard_map/ppermute | solution.py:318
  848.0 60.2 %all-to-all-start.2 = ((f32[32,1,1280]{2,1,0:T(1,128)}), f32[32,1,1280]{2,1,0:T(1,128)S(1)}, u32[]{:S(2)}, u32[]{:S(2)}) async-start(f32[32,1,1280]{2,1,0:T(1,128)} %copy.134), calls=%async_computation.3 | async-start | bytes 327680 | tf_op jit(solution)/shard_map/all_to_all | solution.py:905
  857.2 41.7 %collective-permute-start.100 = (bf16[256,2048]{1,0:T(8,128)(2,1)}, bf16[256,2048]{1,0:T(8,128)(2,1)S(1)}, u32[]{:S(2)}, u32[]{:S(2)}) collective-permute-start(bf16[256,2048]{1,0:T(8,128)(2,1)} %get-tuple-element.160), channel_id=1, source_target_pairs={{0,4},{1,5},{2,6},{3,7},{4,8},{5,9},{6,10},{7,11},{8,12},{9,13},{1... | collective-permute-start | bytes 3145736 | tf_op jit(solution)/shard_map/ppermute | solution.py:314
  884.0 48.6 %collective-permute-start.104 = (bf16[512,2048]{1,0:T(8,128)(2,1)}, bf16[512,2048]{1,0:T(8,128)(2,1)}, u32[]{:S(2)}, u32[]{:S(2)}) collective-permute-start(bf16[512,2048]{1,0:T(8,128)(2,1)} %get-tuple-element.73), channel_id=1, source_target_pairs={{0,16},{16,0},{1,17},{17,1},{2,18},{18,2},{3,19},{19,3},{4,20},{20... | collective-permute-start | bytes 6291464 | tf_op jit(solution)/shard_map/ppermute | solution.py:318
  (217 other events, 3066.7 us)
Sparse Core Ops, SparseCore 0:
  70.9 190.5 all-gather.1
  630.1 261.5 reduce-scatter.1
